TPU v7x, 256 devices: a whole 4x4x8 slice. The times are simulated.
256 devices in a mesh: tm: 16 (over z, core), chan: 8 (over x_hi, y), hank: 2 (over x_lo).
Axes of the slice: x: 4 (x_hi: 2, x_lo: 2; x = x_hi * 2 + x_lo), y: 4, z: 8, core: 2. Of those that a mesh axis runs over, the one named last changes fastest.
Arguments:
- records: bfloat16 [8192, 8192], P('tm', 'chan'), may hold values from -6 to 6
- ref_blocks: int32 [16], replicated, may hold values from 0 to 63, as said below
- probe_seed: int32 [1], replicated, may hold values from 0 to 1048575
Outputs:
- range_sketch: float32 [8, 1024, 16, 512], P('chan', 'tm', 'hank')
Inputs may be any that keep to these rules, and one draw needn't show every extreme that they name: `ref_blocks`: distinct channel block numbers; the first and the last block of the channels are always among them.
All inputs are finite; a program needn't handle non-finite values.
Results may differ from a plain program's by a relative error of at most 0.0029.
Values may be sent and summed in bfloat16 or wider, within the bound.
No kernel may reach another device: no remote copies, remote signals or barrier semaphores. Data moves between devices by JAX's collectives and lax.ppermute only.
A program may use at most 128 MiB of HBM per device.

v0:
```python
import math

import jax
import jax.numpy as jnp
from jax import lax
from jax.sharding import PartitionSpec as P

REF = 2048
BLK = 128
Q = 16
P_SIZE = 512


def from_behind(value, axis, steps):
    count = lax.axis_size(axis)
    leading, last = (max(0, -steps), min(count, count - steps))
    return lax.ppermute(value, axis, [(source, source + steps) for source in range(leading, last)])


def probe_signs(probe_seed, lag_index, ref_ids):
    r_ids = ref_ids[:, None]
    p_ids = jnp.arange(P_SIZE, dtype=jnp.int32)[None, :]
    flat_index = (lag_index * REF + r_ids) * P_SIZE + p_ids
    mixed = flat_index + probe_seed[0] * 7919
    mixed = mixed ^ mixed >> 15
    mixed = mixed * 668265263
    mixed = mixed ^ mixed >> 13
    low_bit = mixed >> 9 & 1
    return (1 - 2 * low_bit).astype(jnp.float32).astype(jnp.bfloat16)


def per_device(records, ref_blocks, probe_seed):
    time_rows, chan_width = records.shape
    tail_rows = records[time_rows - Q :]
    behind = from_behind(tail_rows, "tm", 1)
    extended = jnp.concatenate([behind, records], axis=0)
    chan_index = lax.axis_index("chan")
    block_count = chan_width // BLK
    local_ids = ref_blocks - chan_index * block_count
    owned_mask = (local_ids >= 0) & (local_ids < block_count)
    picked = jnp.take(
        extended.reshape(Q + time_rows, block_count, BLK),
        jnp.clip(local_ids, 0, block_count - 1),
        axis=1,
    )
    picked = jnp.where(owned_mask[None, :, None], picked, jnp.zeros_like(picked))
    picked = picked.reshape(Q + time_rows, REF).astype(jnp.float32)
    source = lax.psum_scatter(picked.astype(jnp.bfloat16), "chan", scatter_dimension=1, tiled=True)
    ref_share = source.shape[1]
    ref_ids = chan_index * ref_share + jnp.arange(ref_share, dtype=jnp.int32)
    hank_index = lax.axis_index("hank")
    hank_count = lax.axis_size("hank")
    j_first = jnp.int32(0)
    running = jnp.zeros((time_rows, P_SIZE), jnp.float32)
    for lag_step in range(Q):
        lag_index = j_first + lag_step
        segment = lax.dynamic_slice_in_dim(source, Q - lag_index, time_rows, 0)
        running = running + jnp.dot(
            segment, probe_signs(probe_seed, lag_index, ref_ids), preferred_element_type=jnp.float32
        )
    images = lax.psum(running, "chan")
    images = images.astype(jnp.bfloat16)
    per_hank = Q // hank_count
    first_row = hank_index * per_hank
    factor = 1.0 / math.sqrt(time_rows * lax.axis_size("tm") * Q * REF)
    front_rows = from_behind(records[:Q], "tm", -1)
    reach_rows = jnp.concatenate([records, front_rows], axis=0)
    stacked = jnp.stack(
        [
            lax.dynamic_slice_in_dim(reach_rows, first_row + row_step + 1, time_rows, 0)
            for row_step in range(per_hank)
        ]
    )
    summed = lax.psum_scatter(
        jnp.einsum("isc,sp->cip", stacked, images, preferred_element_type=jnp.float32),
        "tm",
        scatter_dimension=0,
        tiled=True,
    )
    return (summed * factor)[None]


def solution(mesh):
    in_specs = (P("tm", "chan"), P(), P())
    out_specs = P("chan", "tm", "hank", None)
    return jax.shard_map(
        per_device, mesh=mesh, in_specs=in_specs, out_specs=out_specs, check_vma=False
    )
```

profile of v0, /device:TPU:1, one launch (start us, length us, event | category | flops | bytes accessed | tf_op | source)
XLA Modules:
  0.0 326.2 jit_solution(693408314928771848)
XLA Ops:
  6.5 0.0 reduce-scatter.3.cloned.1.call-start
  6.5 0.8 fusion.373
  7.3 4.9 %collective-permute-start = (bf16[16,1024]{1,0:T(8,128)(2,1)S(1)}, bf16[16,1024]{1,0:T(8,128)(2,1)S(1)}, u32[]{:S(2)}, u32[]{:S(2)}) collective-permute-start(bf16[16,1024]{1,0:T(8,128)(2,1)S(1)} %get-tuple-element.7), channel_id=1, source_target_pairs={{0,16},{16,32},{32,48},{48,64},{64,80},{80,96},{96,112},{112,128},... | collective-permute-start | bytes 98312 | tf_op jit(solution)/shard_map/ppermute | solution.py:17
  12.3 0.7 compare_and_fusion
  12.9 0.1 broadcast_bitcast_fusion
  13.0 0.2 collective-permute-done
  13.3 1.4 copy_bitcast_fusion
  14.7 1.0 gather_fusion
  15.6 1.9 fusion
  17.5 0.0 copy-start
  17.5 0.0 reduce-scatter.3.cloned.1.call-update
  17.6 0.0 reduce-scatter.5.cloned.1.call-start
  17.6 2.1 collective-permute-start.1
  19.8 0.0 copy-done
  19.8 0.1 constant_dynamic-update-slice_fusion.1
  20.5 3.0 collective-permute-done.1
  23.6 1.3 bitcast_dynamic-update-slice_fusion.7
  24.8 1.3 bitcast_dynamic-update-slice_fusion.6
  26.1 1.2 bitcast_dynamic-update-slice_fusion.5
  27.3 1.3 bitcast_dynamic-update-slice_fusion.4
  28.6 1.2 bitcast_dynamic-update-slice_fusion.3
  29.9 1.3 bitcast_dynamic-update-slice_fusion.2
  31.1 1.3 bitcast_dynamic-update-slice_fusion.1
  32.4 1.1 bitcast_dynamic-update-slice_fusion
  33.4 66.5 %reduce-scatter.3.cloned.1.call-done = bf16[528,256]{1,0:T(8,128)(2,1)} async-done(((bf16[528,2048]{1,0:T(8,128)(2,1)}), bf16[528,256]{1,0:T(8,128)(2,1)}) %reduce-scatter.3.cloned.1.call-update) | async-done | bytes 270352 | tf_op jit(solution)/shard_map/reduce_scatter | solution.py:48
  100.0 1.6 fusion.130
  101.6 1.5 convolution_add_fusion.14
  103.1 0.0 copy-done.1
  103.1 0.6 convolution_add_fusion.13
  103.7 0.6 convolution_add_fusion.12
  104.3 0.6 convolution_add_fusion.11
  104.8 0.6 convolution_add_fusion.10
  105.4 0.6 convolution_add_fusion.9
  106.0 0.6 convolution_add_fusion.8
  106.6 0.6 convolution_add_fusion.7
  107.2 0.6 convolution_add_fusion.6
  107.8 0.6 convolution_add_fusion.5
  108.3 0.6 convolution_add_fusion.4
  108.9 0.6 convolution_add_fusion.3
  109.5 0.6 convolution_add_fusion.2
  110.1 0.6 convolution_add_fusion.1
  110.7 0.6 convolution_add_fusion
  111.2 65.1 %all-reduce.1 = bf16[512,512]{1,0:T(8,128)(2,1)S(1)} all-reduce(f32[512,512]{1,0:T(8,128)S(1)} %convolution_add_fusion), channel_id=1, replica_groups=mesh['tm'=16,'chan'=8,'hank'=2] {'chan'}, use_global_device_ids=true, to_apply=%region_1.2 | all-reduce | flops 262144 | bytes 1572864 | tf_op jit(solution)/shard_map/psum | solution.py:61
  176.3 11.5 %convolution_bitcast_fusion = f32[1024,8,512]{0,2,1:T(8,128)} fusion(bf16[8,512,1024]{2,1,0:T(8,128)(2,1)} %bitcast_dynamic-update-slice_fusion, bf16[512,512]{1,0:T(8,128)(2,1)S(1)} %all-reduce.1), kind=kOutput, calls=%fused_computation.1 | convolution fusion | flops 4294967296 | bytes 25690112 | tf_op jit(solution)/shard_map/isc,sp->cip/dot_general | solution.py:75
  187.8 17.6 %copy.13 = f32[1024,8,512]{2,1,0:T(8,128)} copy(f32[1024,8,512]{0,2,1:T(8,128)} %convolution_bitcast_fusion) | data formatting | bytes 33554432 | tf_op jit(solution)/shard_map/isc,sp->cip/transpose | solution.py:75
  205.4 0.0 reduce-scatter.5.cloned.1.call-update
  205.4 111.7 %reduce-scatter.5.cloned.1.call-done = f32[64,8,512]{2,1,0:T(8,128)} async-done(((f32[1024,8,512]{2,1,0:T(8,128)}), f32[64,8,512]{2,1,0:T(8,128)}) %reduce-scatter.5.cloned.1.call-update) | async-done | bytes 1048592 | tf_op jit(solution)/shard_map/reduce_scatter | solution.py:74
  317.1 2.3 multiply_bitcast_fusion
  (11 shorter events, 0.1 us)
Async XLA Ops:
  6.5 93.4 %reduce-scatter.3.cloned.1.call-start = ((), (), s32[]{:S(2)}) async-start(), calls=%async_computation.2 | async-start | bytes 2433024 | tf_op jit(solution)/shard_map/reduce_scatter | solution.py:48
  7.3 5.9 %collective-permute-start = (bf16[16,1024]{1,0:T(8,128)(2,1)S(1)}, bf16[16,1024]{1,0:T(8,128)(2,1)S(1)}, u32[]{:S(2)}, u32[]{:S(2)}) collective-permute-start(bf16[16,1024]{1,0:T(8,128)(2,1)S(1)} %get-tuple-element.7), channel_id=1, source_target_pairs={{0,16},{16,32},{32,48},{48,64},{64,80},{80,96},{96,112},{112,128},... | collective-permute-start | bytes 98312 | tf_op jit(solution)/shard_map/ppermute | solution.py:17
  17.5 2.2 copy-start
  17.6 299.5 %reduce-scatter.5.cloned.1.call-start = ((), (), s32[]{:S(2)}) async-start(), calls=%async_computation.3 | async-start | bytes 17825792 | tf_op jit(solution)/shard_map/reduce_scatter | solution.py:74
  17.6 5.9 %collective-permute-start.1 = (bf16[16,1024]{1,0:T(8,128)(2,1)S(1)}, bf16[16,1024]{1,0:T(8,128)(2,1)S(1)}, u32[]{:S(2)}, u32[]{:S(2)}) collective-permute-start(bf16[16,1024]{1,0:T(8,128)(2,1)S(1)} %get-tuple-element.8), channel_id=1, source_target_pairs={{16,0},{32,16},{48,32},{64,48},{80,64},{96,80},{112,96},{128,112},... | collective-permute-start | bytes 98312 | tf_op jit(solution)/shard_map/ppermute | solution.py:17
  100.0 3.1 copy-start.1
Sparse Core Ops, SparseCore 0:
  17.7 82.2 reduce-scatter.2
  205.6 111.4 reduce-scatter.4
where the time goes:
time: 327 us; the launch traced here: 326 us
  waiting for transfers between devices  181 us (55%)
  blocking collectives  65.1 us (20%)
  local copies, waits for them, and re-layouts  29.4 us (9%)
  matrix products  22.6 us (7%)
  between operations  14.3 us (4%)
  starting transfers between devices  7.02 us (2%)
  other arithmetic  6.32 us (2%)
    reduce_scatter x1, waiting for transfers between devices, per_device(): lax.psum_scatter(jnp.einsum('isc,sp->cip', stacked, images, preferred_ele...  112 us
    reduce_scatter x1, waiting for transfers between devices, per_device(): lax.psum_scatter(picked.astype(jnp.bfloat16), 'chan', scatter_dimension=1...  66.5 us
    psum x1, blocking collectives, per_device(): images = lax.psum(running, 'chan')  65.1 us
    transpose x1, local copies, waits for them, and re-layouts, per_device(): jnp.einsum('isc,sp->cip', stacked, images, preferred_element_type=jnp.flo...  17.6 us
    dot_general x1, matrix products, per_device(): jnp.einsum('isc,sp->cip', stacked, images, preferred_element_type=jnp.flo...  11.5 us
    dot_general x16, matrix products, per_device(): jnp.dot(segment, probe_signs(probe_seed, lag_index, ref_ids), preferred_e...  11.1 us
    unnamed x12, local copies, waits for them, and re-layouts  8.88 us
    ppermute x2, starting transfers between devices, from_behind(): lax.ppermute(value, axis, [(source, source + steps) for source in range(l...  6.98 us
  transfers between devices with their start and end apart: 4, of which 4 were waited for; matrix products, arithmetic and copies ran while one was open for 3% of the time, Pallas kernels for 0%

commit v1 on v0

v1 whole, which is shorter than its diff:
```python
import functools
import math

import jax
import jax.numpy as jnp
from jax import lax
from jax.experimental import pallas as pl
from jax.experimental.pallas import tpu as pltpu
from jax.sharding import PartitionSpec as P

REF = 2048
BLK = 128
Q = 16
P_SIZE = 512
HALF_P = P_SIZE // 2
LAGS = Q // 2
ROWS = 512
NZ = 8
NCHAN = 8
CDEV = 64
F32 = jnp.float32
BF16 = jnp.bfloat16
VMEM = pltpu.VMEM
SMEM = pltpu.SMEM


def tm_shift(value, steps):
    first, last = max(0, -steps), min(16, 16 - steps)
    return lax.ppermute(value, "tm", [(i, i + steps) for i in range(first, last)])


def z_shift(value, steps):
    return lax.ppermute(value, "tm", [(i, (i + 2 * steps) % 16) for i in range(16)])


def core_swap(value):
    return lax.ppermute(value, "tm", [(i, i ^ 1) for i in range(16)])


def hank_swap(value):
    return lax.ppermute(value, "hank", [(0, 1), (1, 0)])


def chan_xor(value, bit):
    return lax.ppermute(value, "chan", [(i, i ^ bit) for i in range(NCHAN)])


def images_kernel(place, blocks, seed, records, behind, out, staged, shifted, signs):
    first_block = place[0] * (1024 // BLK)
    start = seed[0] * 7919 + place[1] * HALF_P
    out[...] = jnp.zeros_like(out)

    def step(q, carry):
        local = blocks[q] - first_block

        @pl.when((local >= 0) & (local < 1024 // BLK))
        def _():
            cols = pl.ds(pl.multiple_of(local * BLK, BLK), BLK)
            staged[pl.ds(0, Q), :] = behind[:, cols].astype(F32)
            staged[pl.ds(Q, ROWS), :] = records[:, cols].astype(F32)
            index = lax.broadcasted_iota(jnp.int32, (BLK, HALF_P), 0) * P_SIZE
            index = index + lax.broadcasted_iota(jnp.int32, (BLK, HALF_P), 1)
            for j in range(Q):
                shifted[:, j * BLK : (j + 1) * BLK] = staged[pl.ds(Q - j, ROWS), :].astype(BF16)
                mixed = index + (start + (j * REF + q * BLK) * P_SIZE)
                mixed = mixed ^ (mixed >> 15)
                mixed = mixed * 668265263
                mixed = mixed ^ (mixed >> 13)
                sign = jnp.where((mixed & 512) != 0, F32(-1), F32(1))
                signs[j * BLK : (j + 1) * BLK, :] = sign.astype(BF16)
            out[...] += jnp.dot(shifted[...], signs[...], preferred_element_type=F32)

        return carry

    lax.fori_loop(0, REF // BLK, step, 0)


def partial_images(place, ref_blocks, probe_seed, records, behind):
    return pl.pallas_call(
        images_kernel,
        out_shape=jax.ShapeDtypeStruct((ROWS, HALF_P), F32),
        in_specs=[pl.BlockSpec(memory_space=SMEM)] * 3 + [pl.BlockSpec(memory_space=VMEM)] * 2,
        out_specs=pl.BlockSpec(memory_space=VMEM),
        scratch_shapes=[
            pltpu.VMEM((ROWS + Q, BLK), F32),
            pltpu.VMEM((ROWS, Q * BLK), BF16),
            pltpu.VMEM((Q * BLK, HALF_P), BF16),
        ],
        compiler_params=pltpu.CompilerParams(vmem_limit_bytes=24 << 20),
        cost_estimate=pl.CostEstimate(flops=3 << 30, bytes_accessed=2 << 20, transcendentals=0),
        name="partial_images",
    )(place, ref_blocks, probe_seed, records, behind)


def lagged_kernel(place, rows, ahead, out, wide):
    wide[pl.ds(0, ROWS), :] = rows[0].astype(F32)
    wide[pl.ds(ROWS, Q), :] = ahead[0].astype(F32)
    wide[pl.ds(ROWS + Q, BLK - Q), :] = jnp.zeros((BLK - Q, BLK), F32)
    turned = pltpu.roll(wide[...], place[2] * CDEV, 1).T
    span = ROWS + BLK
    for side in range(2):
        half = place[1] if side == 0 else 1 - place[1]
        first = pltpu.roll(turned, (span - half * LAGS) % span, 1)
        for i in range(LAGS):
            moved = pltpu.roll(first, span - (i + 1), 1)[:, :ROWS].astype(BF16)
            for other in range(2):
                at = ((other * 2 + side) * LAGS + i) * CDEV
                out[0, pl.ds(at, CDEV), :] = moved[other * CDEV : (other + 1) * CDEV]


def lagged_records(place, rows, ahead):
    return pl.pallas_call(
        lagged_kernel,
        grid=(NZ,),
        out_shape=jax.ShapeDtypeStruct((NZ, 2 * Q * CDEV, ROWS), BF16),
        in_specs=[
            pl.BlockSpec(memory_space=SMEM),
            pl.BlockSpec((1, ROWS, BLK), lambda k: (k, 0, 0)),
            pl.BlockSpec((1, Q, BLK), lambda k: (k, 0, 0)),
        ],
        out_specs=pl.BlockSpec((1, 2 * Q * CDEV, ROWS), lambda k: (k, 0, 0)),
        scratch_shapes=[pltpu.VMEM((ROWS + BLK, BLK), F32)],
        compiler_params=pltpu.CompilerParams(vmem_limit_bytes=24 << 20),
        cost_estimate=pl.CostEstimate(flops=1 << 28, bytes_accessed=18 << 20, transcendentals=0),
        name="lagged_records",
    )(place, rows, ahead)


def sketch_kernel(count, first, *refs):
    lagged, images = refs[:count], refs[count : 2 * count]
    out = refs[-1]
    total = None
    for left, right in zip(lagged, images):
        term = jnp.dot(left[0], right[...], preferred_element_type=F32)
        total = term if total is None else total + term
    if not first:
        total = total + refs[2 * count][...]
    out[...] = total


def sketch_terms(lagged, pieces, running):
    block = 512
    count = len(pieces)
    places = [k for k, _ in pieces]
    in_specs = [pl.BlockSpec((1, block, ROWS), lambda m, k=k: (k, m, 0)) for k in places]
    in_specs += [pl.BlockSpec((ROWS, HALF_P), lambda m: (0, 0))] * count
    args = [lagged] * count + [image for _, image in pieces]
    aliases = {}
    if running is not None:
        in_specs.append(pl.BlockSpec((block, HALF_P), lambda m: (m, 0)))
        args.append(running)
        aliases = {2 * count: 0}
    return pl.pallas_call(
        functools.partial(sketch_kernel, count, running is None),
        grid=(2 * Q * CDEV // block,),
        out_shape=jax.ShapeDtypeStruct((2 * Q * CDEV, HALF_P), F32),
        in_specs=in_specs,
        out_specs=pl.BlockSpec((block, HALF_P), lambda m: (m, 0)),
        input_output_aliases=aliases,
        compiler_params=pltpu.CompilerParams(vmem_limit_bytes=24 << 20),
        cost_estimate=pl.CostEstimate(flops=count << 29, bytes_accessed=(2 * count + 4) << 20, transcendentals=0),
        name="sketch_terms",
    )(*args)


def final_kernel(factor, place, own, near, far, out):
    mine = pl.ds(pl.multiple_of(place[1] * HALF_P, HALF_P), HALF_P)
    theirs = pl.ds(pl.multiple_of((1 - place[1]) * HALF_P, HALF_P), HALF_P)
    for i in range(LAGS):
        out[:, i, mine] = (own[i] + near[i]) * factor
        out[:, i, theirs] = far[i].astype(F32) * factor


def final_sketch(factor, place, own, near, far):
    return pl.pallas_call(
        functools.partial(final_kernel, factor),
        out_shape=jax.ShapeDtypeStruct((CDEV, LAGS, P_SIZE), F32),
        in_specs=[pl.BlockSpec(memory_space=SMEM)] + [pl.BlockSpec(memory_space=VMEM)] * 3,
        out_specs=pl.BlockSpec(memory_space=VMEM),
        compiler_params=pltpu.CompilerParams(vmem_limit_bytes=16 << 20),
        name="final_sketch",
    )(place, own, near, far)


def per_device(records, ref_blocks, probe_seed):
    tm = lax.axis_index("tm")
    z, core = tm // 2, tm % 2
    hank = lax.axis_index("hank")
    chan = lax.axis_index("chan")
    place = jnp.stack([chan, hank, core]).astype(jnp.int32)

    behind = tm_shift(records[ROWS - Q :], 1)
    rows = []
    for k in range(NZ):
        target = (z + k) % NZ
        piece = lax.dynamic_slice_in_dim(records, target * BLK, BLK, 1)
        rows.append(piece if k == 0 else z_shift(piece, k))
    rows = jnp.stack(rows)

    partial = partial_images(place, ref_blocks, probe_seed, records, behind)
    parts = lax.all_to_all(partial.reshape(NCHAN, ROWS // NCHAN, HALF_P), "chan", 0, 0, tiled=True)
    image = jnp.sum(parts, axis=0).astype(BF16)

    fronts = rows[:, :Q]
    given = core_swap(fronts)
    later = jnp.concatenate([given[NZ - 1 :], given[: NZ - 1]], axis=0)
    last_block = ((z - jnp.arange(NZ)) % NZ == NZ - 1)[:, None, None]
    later = jnp.where(last_block, jnp.zeros_like(later), later)
    ahead = jnp.where(core == 0, given, later)
    lagged = lagged_records(place, rows, ahead)

    for bit in (1, 2, 4):
        other = chan_xor(image, bit)
        upper = (chan & bit) != 0
        image = jnp.concatenate([jnp.where(upper, other, image), jnp.where(upper, image, other)], axis=0)

    running = None
    forward = backward = image
    arrived = [(0, image)]
    for step in range(1, 5):
        forward = z_shift(forward, 1)
        nxt = [(step, forward)]
        if step < 4:
            backward = z_shift(backward, -1)
            nxt.append((NZ - step, backward))
        running = sketch_terms(lagged, arrived, running)
        arrived = nxt
    running = sketch_terms(lagged, arrived, running)

    total = running.reshape(2, 2, LAGS, CDEV, HALF_P)
    near_far = core_swap(total[1, 1])
    far = hank_swap((total[0, 1] + near_far).astype(BF16))
    near = core_swap(total[1, 0])
    factor = 1.0 / math.sqrt(ROWS * 16 * Q * REF)
    return final_sketch(factor, place, total[0, 0], near, far)[None]


def solution(mesh):
    in_specs = (P("tm", "chan"), P(), P())
    out_specs = P("chan", "tm", "hank", None)
    return jax.shard_map(
        per_device, mesh=mesh, in_specs=in_specs, out_specs=out_specs, check_vma=False
    )
```

time: 327 us -> 117 us (0.36)
  waiting for transfers between devices: 181 us -> 25.7 us
  blocking collectives: 65.1 us -> 0 us
  starting transfers between devices: 7.02 us -> 57.3 us
  Pallas kernels: 0 us -> 24 us
  matrix products: 22.6 us -> 0 us
  local copies, waits for them, and re-layouts: 29.4 us -> 7.7 us
  between operations: 14.3 us -> 1.05 us
  other arithmetic: 6.32 us -> 0.41 us
    reduce_scatter x2 -> x0, waiting for transfers between devices: 178 us -> none  [the longest x1 112 us: per_device(): lax.psum_scatter(jnp.einsum('isc,sp->cip', stacked, images, preferred_ele...]
    psum x1 -> x0, blocking collectives: 65.1 us -> none  [per_device(): images = lax.psum(running, 'chan')]
    ppermute x2 -> x22, starting transfers between devices: 6.98 us -> 49.6 us  [the longest x14 25.4 us: z_shift(): lax.ppermute(value, 'tm', [(i, (i + 2 * steps) % 16) for i in range(16)])]
    pallas_call x0 -> x8, Pallas kernels: none -> 24 us  [the longest x1 9.89 us: lagged_records(): pl.pallas_call(lagged_kernel, grid=(NZ,), out_shape=jax.ShapeDtypeStruct(...]
    dot_general x17 -> x0, matrix products: 22.6 us -> none  [the longest x1 11.5 us: per_device(): jnp.einsum('isc,sp->cip', stacked, images, preferred_element_type=jnp.flo...]
    ppermute x2 -> x22, waiting for transfers between devices: 3.29 us -> 25.7 us  [the longest x14 10.6 us: z_shift(): lax.ppermute(value, 'tm', [(i, (i + 2 * steps) % 16) for i in range(16)])]
    transpose x1 -> x0, local copies, waits for them, and re-layouts: 17.6 us -> none  [per_device(): jnp.einsum('isc,sp->cip', stacked, images, preferred_element_type=jnp.flo...]
    all_to_all x0 -> x1, starting transfers between devices: none -> 7.71 us  [per_device(): lax.all_to_all(partial.reshape(NCHAN, ROWS // NCHAN, HALF_P), 'chan', 0,...]
  transfers between devices with their start and end apart: 4 -> 23, of which waited for: 4 -> 11; matrix products, arithmetic and copies ran while one was open for 3% -> 5% of each run, Pallas kernels for 0% -> 14%
where the time goes in v1:
time: 117 us; the launch traced here: 116 us
  starting transfers between devices  57.3 us (49%)
  waiting for transfers between devices  25.7 us (22%)
  Pallas kernels  24 us (21%)
  local copies, waits for them, and re-layouts  7.7 us (7%)
    ppermute x14, starting transfers between devices, z_shift(): lax.ppermute(value, 'tm', [(i, (i + 2 * steps) % 16) for i in range(16)])  25.4 us
    ppermute x3, starting transfers between devices, core_swap(): return lax.ppermute(value, 'tm', [(i, i ^ 1) for i in range(16)])  14.3 us
    ppermute x14, waiting for transfers between devices, z_shift(): lax.ppermute(value, 'tm', [(i, (i + 2 * steps) % 16) for i in range(16)])  10.6 us
    pallas_call x1, Pallas kernels, lagged_records(): pl.pallas_call(lagged_kernel, grid=(NZ,), out_shape=jax.ShapeDtypeStruct(...  9.89 us
    pallas_call x5, Pallas kernels, sketch_terms(): pl.pallas_call(functools.partial(sketch_kernel, count, running is None),...  7.97 us
    all_to_all x1, starting transfers between devices, per_device(): lax.all_to_all(partial.reshape(NCHAN, ROWS // NCHAN, HALF_P), 'chan', 0,...  7.71 us
    ppermute x1, waiting for transfers between devices, hank_swap(): return lax.ppermute(value, 'hank', [(0, 1), (1, 0)])  6.94 us
    unnamed x13, local copies, waits for them, and re-layouts  6.54 us
  transfers between devices with their start and end apart: 23, of which 11 were waited for; matrix products, arithmetic and copies ran while one was open for 5% of the time, Pallas kernels for 14%

profile of v1, /device:TPU:1, one launch (start us, length us, event | category | flops | bytes accessed | tf_op | source)
XLA Modules:
  0.0 116.2 jit_solution(1413984825878725260)
XLA Ops:
  0.0 0.8 slice.27
  0.8 4.9 %collective-permute-start.8 = (bf16[16,1024]{1,0:T(8,128)(2,1)S(1)}, bf16[16,1024]{1,0:T(8,128)(2,1)S(1)}, u32[]{:S(2)}, u32[]{:S(2)}) collective-permute-start(bf16[16,1024]{1,0:T(8,128)(2,1)S(1)} %slice.27), channel_id=1, source_target_pairs={{0,16},{16,32},{32,48},{48,64},{64,80},{80,96},{96,112},{112,128},... | collective-permute-start | bytes 98312 | tf_op jit(solution)/shard_map/ppermute | solution.py:29
  6.5 0.2 collective-permute-done.8.behind
  6.7 1.2 %copy-done = bf16[512,1024]{1,0:T(8,128)(2,1)S(1)} copy-done((bf16[512,1024]{1,0:T(8,128)(2,1)S(1)}, bf16[512,1024]{1,0:T(8,128)(2,1)}, u32[]{:S(2)}) %copy-start) | copy-done | bytes 1048600
  7.9 0.7 copy-done.2
  8.6 4.1 %partial_images.1 = f32[512,256]{1,0:T(8,128)} custom-call(s32[3]{0:T(128)S(1)} %pad_add_fusion.place, s32[16]{0:T(128)S(1)} %copy-done.2, s32[1]{0:T(128)S(6)} %copy.19.seed, bf16[512,1024]{1,0:T(8,128)(2,1)S(1)} %copy-done, bf16[16,1024]{1,0:T(8,128)(2,1)S(1)} %collective-permute-done.8.behind), custom_call_target="tpu_custom_call" | custom-call | flops 3221225472 | bytes 2097152 | tf_op jit(solution)/shard_map/partial_images/pallas_call | solution.py:79
  12.7 7.7 %all-to-all-start = ((f32[8,64,256]{2,1,0:T(8,128)}), f32[8,64,256]{2,1,0:T(8,128)S(1)}, u32[]{:S(2)}, u32[]{:S(2)}) async-start(f32[8,64,256]{2,1,0:T(8,128)} %bitcast.11), calls=%async_computation | async-start | bytes 1048576 | tf_op jit(solution)/shard_map/all_to_all | solution.py:201
  20.4 0.3 constant_dynamic-slice_fusion
  20.6 1.7 %collective-permute-start = (bf16[512,128]{1,0:T(8,128)(2,1)S(1)}, bf16[512,128]{1,0:T(8,128)(2,1)}, u32[]{:S(2)}, u32[]{:S(2)}) collective-permute-start(bf16[512,128]{1,0:T(8,128)(2,1)S(1)} %get-tuple-element.14), channel_id=1, source_target_pairs={{0,32},{16,48},{32,64},{48,80},{64,96},{80,112},{96,128},{112,144}... | collective-permute-start | bytes 393224 | tf_op jit(solution)/shard_map/ppermute | solution.py:33
  22.4 4.2 %collective-permute-start.1 = (bf16[512,128]{1,0:T(8,128)(2,1)S(1)}, bf16[512,128]{1,0:T(8,128)(2,1)}, u32[]{:S(2)}, u32[]{:S(2)}) collective-permute-start(bf16[512,128]{1,0:T(8,128)(2,1)S(1)} %get-tuple-element.13), channel_id=1, source_target_pairs={{0,64},{16,80},{32,96},{48,112},{64,128},{80,144},{96,160},{112,17... | collective-permute-start | bytes 393224 | tf_op jit(solution)/shard_map/ppermute | solution.py:33
  26.6 1.6 %collective-permute-start.2 = (bf16[512,128]{1,0:T(8,128)(2,1)S(1)}, bf16[512,128]{1,0:T(8,128)(2,1)}, u32[]{:S(2)}, u32[]{:S(2)}) collective-permute-start(bf16[512,128]{1,0:T(8,128)(2,1)S(1)} %get-tuple-element.12), channel_id=1, source_target_pairs={{0,96},{16,112},{32,128},{48,144},{64,160},{80,176},{96,192},{112,... | collective-permute-start | bytes 393224 | tf_op jit(solution)/shard_map/ppermute | solution.py:33
  28.2 1.2 collective-permute-start.3
  29.4 3.1 %collective-permute-start.4 = (bf16[512,128]{1,0:T(8,128)(2,1)S(1)}, bf16[512,128]{1,0:T(8,128)(2,1)}, u32[]{:S(2)}, u32[]{:S(2)}) collective-permute-start(bf16[512,128]{1,0:T(8,128)(2,1)S(1)} %get-tuple-element.10), channel_id=1, source_target_pairs={{0,160},{16,176},{32,192},{48,208},{64,224},{80,240},{96,0},{112,1... | collective-permute-start | bytes 393224 | tf_op jit(solution)/shard_map/ppermute | solution.py:33
  32.5 3.1 %collective-permute-start.5 = (bf16[512,128]{1,0:T(8,128)(2,1)S(1)}, bf16[512,128]{1,0:T(8,128)(2,1)S(1)}, u32[]{:S(2)}, u32[]{:S(2)}) collective-permute-start(bf16[512,128]{1,0:T(8,128)(2,1)S(1)} %get-tuple-element.9), channel_id=1, source_target_pairs={{0,192},{16,208},{32,224},{48,240},{64,0},{80,16},{96,32},{112,48}... | collective-permute-start | bytes 393224 | tf_op jit(solution)/shard_map/ppermute | solution.py:33
  35.6 0.9 bitcast_dynamic-update-slice_fusion.6
  36.6 1.5 %collective-permute-start.9 = (bf16[64,256]{1,0:T(8,128)(2,1)S(1)}, bf16[64,256]{1,0:T(8,128)(2,1)S(1)}, u32[]{:S(2)}, u32[]{:S(2)}) collective-permute-start(bf16[64,256]{1,0:T(8,128)(2,1)S(1)} %reduce_sum.9), channel_id=1, source_target_pairs={{0,2},{2,0},{4,6},{6,4},{8,10},{10,8},{12,14},{14,12},{1,3},{3,1},... | collective-permute-start | bytes 98312 | tf_op jit(solution)/shard_map/ppermute | solution.py:45
  38.2 0.9 bitcast_dynamic-update-slice_fusion.5
  39.1 0.4 collective-permute-done.9
  39.5 1.1 collective-permute-start.6
  40.6 1.9 %collective-permute-done.2 = bf16[512,128]{1,0:T(8,128)(2,1)} collective-permute-done((bf16[512,128]{1,0:T(8,128)(2,1)S(1)}, bf16[512,128]{1,0:T(8,128)(2,1)}, u32[]{:S(2)}, u32[]{:S(2)}) %collective-permute-start.2) | collective-permute-done | bytes 131104 | tf_op jit(solution)/shard_map/ppermute | solution.py:33
  42.5 1.7 %collective-permute-start.10 = (bf16[128,256]{1,0:T(8,128)(2,1)S(1)}, bf16[128,256]{1,0:T(8,128)(2,1)S(1)}, u32[]{:S(2)}, u32[]{:S(2)}) collective-permute-start(bf16[128,256]{1,0:T(8,128)(2,1)S(1)} %pad_maximum_fusion.2), channel_id=1, source_target_pairs={{0,4},{2,6},{4,0},{6,2},{8,12},{10,14},{12,8},{14,10},{1,5},{3,7},... | collective-permute-start | bytes 196616 | tf_op jit(solution)/shard_map/ppermute | solution.py:45
  44.2 0.9 bitcast_dynamic-update-slice_fusion.4
  45.1 2.8 %collective-permute-done.10 = bf16[128,256]{1,0:T(8,128)(2,1)S(1)} collective-permute-done((bf16[128,256]{1,0:T(8,128)(2,1)S(1)}, bf16[128,256]{1,0:T(8,128)(2,1)S(1)}, u32[]{:S(2)}, u32[]{:S(2)}) %collective-permute-start.10) | collective-permute-done | bytes 65568 | tf_op jit(solution)/shard_map/ppermute | solution.py:45
  47.9 1.4 %collective-permute-start.11 = (bf16[256,256]{1,0:T(8,128)(2,1)S(1)}, bf16[256,256]{1,0:T(8,128)(2,1)S(1)}, u32[]{:S(2)}, u32[]{:S(2)}) collective-permute-start(bf16[256,256]{1,0:T(8,128)(2,1)S(1)} %pad_maximum_fusion.1), channel_id=1, source_target_pairs={{0,8},{2,10},{4,12},{6,14},{8,0},{10,2},{12,4},{14,6},{1,9},{3,11}... | collective-permute-start | bytes 393224 | tf_op jit(solution)/shard_map/ppermute | solution.py:45
  49.3 0.9 bitcast_dynamic-update-slice_fusion.3
  50.3 3.1 %collective-permute-done.11 = bf16[256,256]{1,0:T(8,128)(2,1)S(1)} collective-permute-done((bf16[256,256]{1,0:T(8,128)(2,1)S(1)}, bf16[256,256]{1,0:T(8,128)(2,1)S(1)}, u32[]{:S(2)}, u32[]{:S(2)}) %collective-permute-start.11) | collective-permute-done | bytes 131104 | tf_op jit(solution)/shard_map/ppermute | solution.py:45
  53.5 0.9 bitcast_dynamic-update-slice_fusion.2
  54.5 2.7 %collective-permute-start.16 = (bf16[512,256]{1,0:T(8,128)(2,1)S(1)}, bf16[512,256]{1,0:T(8,128)(2,1)S(1)}, u32[]{:S(2)}, u32[]{:S(2)}) collective-permute-start(bf16[512,256]{1,0:T(8,128)(2,1)S(1)} %pad_maximum_fusion.refs_1_), channel_id=1, source_target_pairs={{0,224},{16,240},{32,0},{48,16},{64,32},{80,48},{96,64},{112,80},{... | collective-permute-start | bytes 786440 | tf_op jit(solution)/shard_map/ppermute | solution.py:33
  57.2 2.7 %collective-permute-done.12.refs_2_ = bf16[512,256]{1,0:T(8,128)(2,1)S(1)} collective-permute-done((bf16[512,256]{1,0:T(8,128)(2,1)S(1)}, bf16[512,256]{1,0:T(8,128)(2,1)S(1)}, u32[]{:S(2)}, u32[]{:S(2)}) %collective-permute-start.12) | collective-permute-done | bytes 262176 | tf_op jit(solution)/shard_map/ppermute | solution.py:33
  60.0 11.1 %collective-permute-start.7 = (bf16[8,16,128]{2,1,0:T(8,128)(2,1)S(1)}, bf16[8,16,128]{2,1,0:T(8,128)(2,1)S(1)}, u32[]{:S(2)}, u32[]{:S(2)}) collective-permute-start(bf16[8,16,128]{2,1,0:T(8,128)(2,1)S(1)} %slice.32), channel_id=1, source_target_pairs={{0,16},{16,0},{32,48},{48,32},{64,80},{80,64},{96,112},{112,96},{1... | collective-permute-start | bytes 98312 | tf_op jit(solution)/shard_map/ppermute | solution.py:37
  71.1 3.0 %collective-permute-start.17 = (bf16[512,256]{1,0:T(8,128)(2,1)S(1)}, bf16[512,256]{1,0:T(8,128)(2,1)S(1)}, u32[]{:S(2)}, u32[]{:S(2)}) collective-permute-start(bf16[512,256]{1,0:T(8,128)(2,1)S(1)} %collective-permute-done.16.refs_3_), channel_id=1, source_target_pairs={{0,224},{16,240},{32,0},{48,16},{64,32},{80,48},{96,64},{112,80},{... | collective-permute-start | bytes 786440 | tf_op jit(solution)/shard_map/ppermute | solution.py:33
  74.3 4.5 %collective-permute-done.17.refs_3_ = bf16[512,256]{1,0:T(8,128)(2,1)S(1)} collective-permute-done((bf16[512,256]{1,0:T(8,128)(2,1)S(1)}, bf16[512,256]{1,0:T(8,128)(2,1)S(1)}, u32[]{:S(2)}, u32[]{:S(2)}) %collective-permute-start.17) | collective-permute-done | bytes 262176 | tf_op jit(solution)/shard_map/ppermute | solution.py:33
  78.8 3.4 %collective-permute-start.18 = (bf16[512,256]{1,0:T(8,128)(2,1)S(1)}, bf16[512,256]{1,0:T(8,128)(2,1)S(1)}, u32[]{:S(2)}, u32[]{:S(2)}) collective-permute-start(bf16[512,256]{1,0:T(8,128)(2,1)S(1)} %collective-permute-done.17.refs_3_), channel_id=1, source_target_pairs={{0,224},{16,240},{32,0},{48,16},{64,32},{80,48},{96,64},{112,80},{... | collective-permute-start | bytes 786440 | tf_op jit(solution)/shard_map/ppermute | solution.py:33
  82.2 9.9 %lagged_records.1.refs_0_.refs_1_ = bf16[8,2048,512]{2,1,0:T(8,128)(2,1)S(1)} custom-call(s32[3]{0:T(128)S(1)} %pad_add_fusion.place, bf16[8,512,128]{2,1,0:T(8,128)(2,1)S(1)} %bitcast_dynamic-update-slice_fusion.rows, bf16[8,16,128]{2,1,0:T(8,128)(2,1)S(1)} %fusion.2.ahead), custom_call_target="tpu_custom_call" | custom-call | flops 268435456 | bytes 18874368 | tf_op jit(solution)/shard_map/lagged_records/pallas_call | solution.py:112
  92.1 1.2 %sketch_terms.5.refs_4_ = f32[2048,256]{1,0:T(8,128)S(1)} custom-call(bf16[8,2048,512]{2,1,0:T(8,128)(2,1)S(1)} %lagged_records.1.refs_0_.refs_1_, bf16[512,256]{1,0:T(8,128)(2,1)S(1)} %pad_maximum_fusion.refs_1_), custom_call_target="tpu_custom_call" | custom-call | flops 536870912 | bytes 6291456 | tf_op jit(solution)/shard_map/sketch_terms/pallas_call | solution.py:153
  93.5 1.8 %sketch_terms.6.refs_4_ = f32[2048,256]{1,0:T(8,128)S(1)} custom-call(bf16[8,2048,512]{2,1,0:T(8,128)(2,1)S(1)} %lagged_records.1.refs_0_.refs_1_, bf16[8,2048,512]{2,1,0:T(8,128)(2,1)S(1)} %lagged_records.1.refs_0_.refs_1_, bf16[512,256]{1,0:T(8,128)(2,1)S(1)} %collective-permute-done.12.refs_2_, ...), custom_call_target="tpu_custom_call", output_to_operand_aliasing={{}: (4, {})} | custom-call | flops 1073741824 | bytes 8388608 | tf_op jit(solution)/shard_map/sketch_terms/pallas_call | solution.py:153
  95.3 1.8 %sketch_terms.7.refs_4_ = f32[2048,256]{1,0:T(8,128)S(1)} custom-call(bf16[8,2048,512]{2,1,0:T(8,128)(2,1)S(1)} %lagged_records.1.refs_0_.refs_1_, bf16[8,2048,512]{2,1,0:T(8,128)(2,1)S(1)} %lagged_records.1.refs_0_.refs_1_, bf16[512,256]{1,0:T(8,128)(2,1)S(1)} %collective-permute-done.13.refs_2_, ...), custom_call_target="tpu_custom_call", output_to_operand_aliasing={{}: (4, {})} | custom-call | flops 1073741824 | bytes 8388608 | tf_op jit(solution)/shard_map/sketch_terms/pallas_call | solution.py:153
  97.1 1.8 %sketch_terms.8.refs_2_ = f32[2048,256]{1,0:T(8,128)S(1)} custom-call(bf16[8,2048,512]{2,1,0:T(8,128)(2,1)S(1)} %lagged_records.1.refs_0_.refs_1_, bf16[8,2048,512]{2,1,0:T(8,128)(2,1)S(1)} %lagged_records.1.refs_0_.refs_1_, bf16[512,256]{1,0:T(8,128)(2,1)S(1)} %collective-permute-done.14.refs_2_, ...), custom_call_target="tpu_custom_call", output_to_operand_aliasing={{}: (4, {})} | custom-call | flops 1073741824 | bytes 8388608 | tf_op jit(solution)/shard_map/sketch_terms/pallas_call | solution.py:153
  99.0 1.4 %collective-permute-done.15.refs_1_ = bf16[512,256]{1,0:T(8,128)(2,1)S(1)} collective-permute-done((bf16[512,256]{1,0:T(8,128)(2,1)S(1)}, bf16[512,256]{1,0:T(8,128)(2,1)S(1)}, u32[]{:S(2)}, u32[]{:S(2)}) %collective-permute-start.15) | collective-permute-done | bytes 262176 | tf_op jit(solution)/shard_map/ppermute | solution.py:33
  100.4 1.3 %sketch_terms.9 = f32[2048,256]{1,0:T(8,128)S(1)} custom-call(bf16[8,2048,512]{2,1,0:T(8,128)(2,1)S(1)} %lagged_records.1.refs_0_.refs_1_, bf16[512,256]{1,0:T(8,128)(2,1)S(1)} %collective-permute-done.15.refs_1_, f32[2048,256]{1,0:T(8,128)S(1)} %sketch_terms.8.refs_2_), custom_call_target="tpu_custom_call", output_to_operand_aliasing={{}: (2, {})} | custom-call | flops 536870912 | bytes 6291456 | tf_op jit(solution)/shard_map/sketch_terms/pallas_call | solution.py:153
  101.7 0.1 slice_bitcast_fusion
  101.8 3.1 %collective-permute-start.20 = (f32[8,64,256]{2,1,0:T(8,128)S(1)}, f32[8,64,256]{2,1,0:T(8,128)S(1)}, u32[]{:S(2)}, u32[]{:S(2)}) collective-permute-start(f32[8,64,256]{2,1,0:T(8,128)S(1)} %get-tuple-element.5), channel_id=1, source_target_pairs={{0,16},{16,0},{32,48},{48,32},{64,80},{80,64},{96,112},{112,96},{1... | collective-permute-start | bytes 1572872 | tf_op jit(solution)/shard_map/ppermute | solution.py:37
  104.9 0.1 collective-permute-start.19
  105.0 1.4 %collective-permute-done.20 = f32[8,64,256]{2,1,0:T(8,128)S(1)} collective-permute-done((f32[8,64,256]{2,1,0:T(8,128)S(1)}, f32[8,64,256]{2,1,0:T(8,128)S(1)}, u32[]{:S(2)}, u32[]{:S(2)}) %collective-permute-start.20) | collective-permute-done | bytes 524320 | tf_op jit(solution)/shard_map/ppermute | solution.py:37
  106.5 0.4 collective-permute-start.21
  106.8 0.3 collective-permute-done.19.near
  107.1 6.9 %collective-permute-done.21.far = bf16[8,64,256]{2,1,0:T(8,128)(2,1)S(1)} collective-permute-done((bf16[8,64,256]{2,1,0:T(8,128)(2,1)S(1)}, bf16[8,64,256]{2,1,0:T(8,128)(2,1)S(1)}, u32[]{:S(2)}, u32[]{:S(2)}) %collective-permute-start.21) | collective-permute-done | bytes 262176 | tf_op jit(solution)/shard_map/ppermute | solution.py:41
  114.1 2.1 %final_sketch.1 = f32[64,8,512]{2,1,0:T(8,128)} custom-call(s32[3]{0:T(128)S(1)} %pad_add_fusion.place, f32[8,64,256]{2,1,0:T(8,128)S(1)} %get-tuple-element.7.own, f32[8,64,256]{2,1,0:T(8,128)S(1)} %collective-permute-done.19.near, bf16[8,64,256]{2,1,0:T(8,128)(2,1)S(1)} %collective-permute-done.21.far), custom_call_target="tpu_custom_call" | custom-call | tf_op jit(solution)/shard_map/final_sketch/pallas_call | solution.py:175
  (37 shorter events, 0.8 us)
Async XLA Ops:
  0.8 5.9 %collective-permute-start.8 = (bf16[16,1024]{1,0:T(8,128)(2,1)S(1)}, bf16[16,1024]{1,0:T(8,128)(2,1)S(1)}, u32[]{:S(2)}, u32[]{:S(2)}) collective-permute-start(bf16[16,1024]{1,0:T(8,128)(2,1)S(1)} %slice.27), channel_id=1, source_target_pairs={{0,16},{16,32},{32,48},{48,64},{64,80},{80,96},{96,112},{112,128},... | collective-permute-start | bytes 98312 | tf_op jit(solution)/shard_map/ppermute | solution.py:29
  6.7 1.2 %copy-start = (bf16[512,1024]{1,0:T(8,128)(2,1)S(1)}, bf16[512,1024]{1,0:T(8,128)(2,1)}, u32[]{:S(2)}) copy-start(bf16[512,1024]{1,0:T(8,128)(2,1)} %records.1) | copy-start | bytes 3145732
  7.9 0.7 copy-start.2
  8.6 11.8 %copy-start.1 = (bf16[512,1024]{1,0:T(8,128)(2,1)S(1)}, bf16[512,1024]{1,0:T(8,128)(2,1)}, u32[]{:S(2)}) copy-start(bf16[512,1024]{1,0:T(8,128)(2,1)} %records.1) | copy-start | bytes 3145732
  12.7 23.9 %all-to-all-start = ((f32[8,64,256]{2,1,0:T(8,128)}), f32[8,64,256]{2,1,0:T(8,128)S(1)}, u32[]{:S(2)}, u32[]{:S(2)}) async-start(f32[8,64,256]{2,1,0:T(8,128)} %bitcast.11), calls=%async_computation | async-start | bytes 1048576 | tf_op jit(solution)/shard_map/all_to_all | solution.py:201
  20.6 11.9 %collective-permute-start = (bf16[512,128]{1,0:T(8,128)(2,1)S(1)}, bf16[512,128]{1,0:T(8,128)(2,1)}, u32[]{:S(2)}, u32[]{:S(2)}) collective-permute-start(bf16[512,128]{1,0:T(8,128)(2,1)S(1)} %get-tuple-element.14), channel_id=1, source_target_pairs={{0,32},{16,48},{32,64},{48,80},{64,96},{80,112},{96,128},{112,144}... | collective-permute-start | bytes 393224 | tf_op jit(solution)/shard_map/ppermute | solution.py:33
  22.4 14.3 %collective-permute-start.1 = (bf16[512,128]{1,0:T(8,128)(2,1)S(1)}, bf16[512,128]{1,0:T(8,128)(2,1)}, u32[]{:S(2)}, u32[]{:S(2)}) collective-permute-start(bf16[512,128]{1,0:T(8,128)(2,1)S(1)} %get-tuple-element.13), channel_id=1, source_target_pairs={{0,64},{16,80},{32,96},{48,112},{64,128},{80,144},{96,160},{112,17... | collective-permute-start | bytes 393224 | tf_op jit(solution)/shard_map/ppermute | solution.py:33
  26.6 16.0 %collective-permute-start.2 = (bf16[512,128]{1,0:T(8,128)(2,1)S(1)}, bf16[512,128]{1,0:T(8,128)(2,1)}, u32[]{:S(2)}, u32[]{:S(2)}) collective-permute-start(bf16[512,128]{1,0:T(8,128)(2,1)S(1)} %get-tuple-element.12), channel_id=1, source_target_pairs={{0,96},{16,112},{32,128},{48,144},{64,160},{80,176},{96,192},{112,... | collective-permute-start | bytes 393224 | tf_op jit(solution)/shard_map/ppermute | solution.py:33
  28.2 21.1 %collective-permute-start.3 = (bf16[512,128]{1,0:T(8,128)(2,1)S(1)}, bf16[512,128]{1,0:T(8,128)(2,1)}, u32[]{:S(2)}, u32[]{:S(2)}) collective-permute-start(bf16[512,128]{1,0:T(8,128)(2,1)S(1)} %get-tuple-element.11), channel_id=1, source_target_pairs={{0,128},{16,144},{32,160},{48,176},{64,192},{80,208},{96,224},{112... | collective-permute-start | bytes 393224 | tf_op jit(solution)/shard_map/ppermute | solution.py:33
  29.4 24.2 %collective-permute-start.4 = (bf16[512,128]{1,0:T(8,128)(2,1)S(1)}, bf16[512,128]{1,0:T(8,128)(2,1)}, u32[]{:S(2)}, u32[]{:S(2)}) collective-permute-start(bf16[512,128]{1,0:T(8,128)(2,1)S(1)} %get-tuple-element.10), channel_id=1, source_target_pairs={{0,160},{16,176},{32,192},{48,208},{64,224},{80,240},{96,0},{112,1... | collective-permute-start | bytes 393224 | tf_op jit(solution)/shard_map/ppermute | solution.py:33
  32.5 24.7 %collective-permute-start.5 = (bf16[512,128]{1,0:T(8,128)(2,1)S(1)}, bf16[512,128]{1,0:T(8,128)(2,1)S(1)}, u32[]{:S(2)}, u32[]{:S(2)}) collective-permute-start(bf16[512,128]{1,0:T(8,128)(2,1)S(1)} %get-tuple-element.9), channel_id=1, source_target_pairs={{0,192},{16,208},{32,224},{48,240},{64,0},{80,16},{96,32},{112,48}... | collective-permute-start | bytes 393224 | tf_op jit(solution)/shard_map/ppermute | solution.py:33
  36.6 2.9 %collective-permute-start.9 = (bf16[64,256]{1,0:T(8,128)(2,1)S(1)}, bf16[64,256]{1,0:T(8,128)(2,1)S(1)}, u32[]{:S(2)}, u32[]{:S(2)}) collective-permute-start(bf16[64,256]{1,0:T(8,128)(2,1)S(1)} %reduce_sum.9), channel_id=1, source_target_pairs={{0,2},{2,0},{4,6},{6,4},{8,10},{10,8},{12,14},{14,12},{1,3},{3,1},... | collective-permute-start | bytes 98312 | tf_op jit(solution)/shard_map/ppermute | solution.py:45
  39.5 20.5 %collective-permute-start.6 = (bf16[512,128]{1,0:T(8,128)(2,1)S(1)}, bf16[512,128]{1,0:T(8,128)(2,1)S(1)}, u32[]{:S(2)}, u32[]{:S(2)}) collective-permute-start(bf16[512,128]{1,0:T(8,128)(2,1)S(1)} %get-tuple-element.8), channel_id=1, source_target_pairs={{0,224},{16,240},{32,0},{48,16},{64,32},{80,48},{96,64},{112,80},{... | collective-permute-start | bytes 393224 | tf_op jit(solution)/shard_map/ppermute | solution.py:33
  42.5 5.4 %collective-permute-start.10 = (bf16[128,256]{1,0:T(8,128)(2,1)S(1)}, bf16[128,256]{1,0:T(8,128)(2,1)S(1)}, u32[]{:S(2)}, u32[]{:S(2)}) collective-permute-start(bf16[128,256]{1,0:T(8,128)(2,1)S(1)} %pad_maximum_fusion.2), channel_id=1, source_target_pairs={{0,4},{2,6},{4,0},{6,2},{8,12},{10,14},{12,8},{14,10},{1,5},{3,7},... | collective-permute-start | bytes 196616 | tf_op jit(solution)/shard_map/ppermute | solution.py:45
  47.9 5.4 %collective-permute-start.11 = (bf16[256,256]{1,0:T(8,128)(2,1)S(1)}, bf16[256,256]{1,0:T(8,128)(2,1)S(1)}, u32[]{:S(2)}, u32[]{:S(2)}) collective-permute-start(bf16[256,256]{1,0:T(8,128)(2,1)S(1)} %pad_maximum_fusion.1), channel_id=1, source_target_pairs={{0,8},{2,10},{4,12},{6,14},{8,0},{10,2},{12,4},{14,6},{1,9},{3,11}... | collective-permute-start | bytes 393224 | tf_op jit(solution)/shard_map/ppermute | solution.py:45
  53.4 6.5 %collective-permute-start.12 = (bf16[512,256]{1,0:T(8,128)(2,1)S(1)}, bf16[512,256]{1,0:T(8,128)(2,1)S(1)}, u32[]{:S(2)}, u32[]{:S(2)}) collective-permute-start(bf16[512,256]{1,0:T(8,128)(2,1)S(1)} %pad_maximum_fusion.refs_1_), channel_id=1, source_target_pairs={{0,32},{16,48},{32,64},{48,80},{64,96},{80,112},{96,128},{112,144}... | collective-permute-start | bytes 786440 | tf_op jit(solution)/shard_map/ppermute | solution.py:33
  54.5 16.7 %collective-permute-start.16 = (bf16[512,256]{1,0:T(8,128)(2,1)S(1)}, bf16[512,256]{1,0:T(8,128)(2,1)S(1)}, u32[]{:S(2)}, u32[]{:S(2)}) collective-permute-start(bf16[512,256]{1,0:T(8,128)(2,1)S(1)} %pad_maximum_fusion.refs_1_), channel_id=1, source_target_pairs={{0,224},{16,240},{32,0},{48,16},{64,32},{80,48},{96,64},{112,80},{... | collective-permute-start | bytes 786440 | tf_op jit(solution)/shard_map/ppermute | solution.py:33
  59.9 14.2 %collective-permute-start.13 = (bf16[512,256]{1,0:T(8,128)(2,1)S(1)}, bf16[512,256]{1,0:T(8,128)(2,1)S(1)}, u32[]{:S(2)}, u32[]{:S(2)}) collective-permute-start(bf16[512,256]{1,0:T(8,128)(2,1)S(1)} %collective-permute-done.12.refs_2_), channel_id=1, source_target_pairs={{0,32},{16,48},{32,64},{48,80},{64,96},{80,112},{96,128},{112,144}... | collective-permute-start | bytes 786440 | tf_op jit(solution)/shard_map/ppermute | solution.py:33
  60.0 14.1 %collective-permute-start.7 = (bf16[8,16,128]{2,1,0:T(8,128)(2,1)S(1)}, bf16[8,16,128]{2,1,0:T(8,128)(2,1)S(1)}, u32[]{:S(2)}, u32[]{:S(2)}) collective-permute-start(bf16[8,16,128]{2,1,0:T(8,128)(2,1)S(1)} %slice.32), channel_id=1, source_target_pairs={{0,16},{16,0},{32,48},{48,32},{64,80},{80,64},{96,112},{112,96},{1... | collective-permute-start | bytes 98312 | tf_op jit(solution)/shard_map/ppermute | solution.py:37
  71.1 7.7 %collective-permute-start.17 = (bf16[512,256]{1,0:T(8,128)(2,1)S(1)}, bf16[512,256]{1,0:T(8,128)(2,1)S(1)}, u32[]{:S(2)}, u32[]{:S(2)}) collective-permute-start(bf16[512,256]{1,0:T(8,128)(2,1)S(1)} %collective-permute-done.16.refs_3_), channel_id=1, source_target_pairs={{0,224},{16,240},{32,0},{48,16},{64,32},{80,48},{96,64},{112,80},{... | collective-permute-start | bytes 786440 | tf_op jit(solution)/shard_map/ppermute | solution.py:33
  74.1 19.2 %collective-permute-start.14 = (bf16[512,256]{1,0:T(8,128)(2,1)S(1)}, bf16[512,256]{1,0:T(8,128)(2,1)S(1)}, u32[]{:S(2)}, u32[]{:S(2)}) collective-permute-start(bf16[512,256]{1,0:T(8,128)(2,1)S(1)} %collective-permute-done.13.refs_2_), channel_id=1, source_target_pairs={{0,32},{16,48},{32,64},{48,80},{64,96},{80,112},{96,128},{112,144}... | collective-permute-start | bytes 786440 | tf_op jit(solution)/shard_map/ppermute | solution.py:33
  78.8 18.3 %collective-permute-start.18 = (bf16[512,256]{1,0:T(8,128)(2,1)S(1)}, bf16[512,256]{1,0:T(8,128)(2,1)S(1)}, u32[]{:S(2)}, u32[]{:S(2)}) collective-permute-start(bf16[512,256]{1,0:T(8,128)(2,1)S(1)} %collective-permute-done.17.refs_3_), channel_id=1, source_target_pairs={{0,224},{16,240},{32,0},{48,16},{64,32},{80,48},{96,64},{112,80},{... | collective-permute-start | bytes 786440 | tf_op jit(solution)/shard_map/ppermute | solution.py:33
  93.4 7.0 %collective-permute-start.15 = (bf16[512,256]{1,0:T(8,128)(2,1)S(1)}, bf16[512,256]{1,0:T(8,128)(2,1)S(1)}, u32[]{:S(2)}, u32[]{:S(2)}) collective-permute-start(bf16[512,256]{1,0:T(8,128)(2,1)S(1)} %collective-permute-done.14.refs_2_), channel_id=1, source_target_pairs={{0,32},{16,48},{32,64},{48,80},{64,96},{80,112},{96,128},{112,144}... | collective-permute-start | bytes 786440 | tf_op jit(solution)/shard_map/ppermute | solution.py:33
  101.8 4.6 %collective-permute-start.20 = (f32[8,64,256]{2,1,0:T(8,128)S(1)}, f32[8,64,256]{2,1,0:T(8,128)S(1)}, u32[]{:S(2)}, u32[]{:S(2)}) collective-permute-start(f32[8,64,256]{2,1,0:T(8,128)S(1)} %get-tuple-element.5), channel_id=1, source_target_pairs={{0,16},{16,0},{32,48},{48,32},{64,80},{80,64},{96,112},{112,96},{1... | collective-permute-start | bytes 1572872 | tf_op jit(solution)/shard_map/ppermute | solution.py:37
  104.9 2.3 %collective-permute-start.19 = (f32[8,64,256]{2,1,0:T(8,128)S(1)}, f32[8,64,256]{2,1,0:T(8,128)S(1)}, u32[]{:S(2)}, u32[]{:S(2)}) collective-permute-start(f32[8,64,256]{2,1,0:T(8,128)S(1)} %get-tuple-element.6), channel_id=1, source_target_pairs={{0,16},{16,0},{32,48},{48,32},{64,80},{80,64},{96,112},{112,96},{1... | collective-permute-start | bytes 1572872 | tf_op jit(solution)/shard_map/ppermute | solution.py:37
  106.5 7.6 %collective-permute-start.21 = (bf16[8,64,256]{2,1,0:T(8,128)(2,1)S(1)}, bf16[8,64,256]{2,1,0:T(8,128)(2,1)S(1)}, u32[]{:S(2)}, u32[]{:S(2)}) collective-permute-start(bf16[8,64,256]{2,1,0:T(8,128)(2,1)S(1)} %fusion.1), channel_id=1, source_target_pairs={{0,1},{1,0},{2,3},{3,2},{4,5},{5,4},{6,7},{7,6},{8,9},{9,8},{10,11... | collective-permute-start | bytes 786440 | tf_op jit(solution)/shard_map/ppermute | solution.py:41

commit v2 on v0

v2 whole, which is shorter than its diff:
```python
import functools
import math

import jax
import jax.numpy as jnp
from jax import lax
from jax.experimental import pallas as pl
from jax.experimental.pallas import tpu as pltpu
from jax.sharding import PartitionSpec as P

REF = 2048
BLK = 128
Q = 16
P_SIZE = 512
HALF_P = P_SIZE // 2
LAGS = Q // 2
ROWS = 512
NZ = 8
NCHAN = 8
CDEV = 64
SHARE = ROWS // NCHAN
F32 = jnp.float32
BF16 = jnp.bfloat16
VMEM = pltpu.VMEM
SMEM = pltpu.SMEM


def tm_shift(value, steps):
    first, last = max(0, -steps), min(16, 16 - steps)
    return lax.ppermute(value, "tm", [(i, i + steps) for i in range(first, last)])


def z_shift(value, steps):
    return lax.ppermute(value, "tm", [(i, (i + 2 * steps) % 16) for i in range(16)])


def split_shift(value, near, far):
    pairs = []
    for i in range(16):
        pairs.append((2 * i, 2 * ((i + 2 * near) % 16)))
        pairs.append((2 * i + 1, 2 * ((i + 2 * far) % 16) + 1))
    return lax.ppermute(value, ("tm", "hank"), pairs)


def core_swap(value):
    return lax.ppermute(value, "tm", [(i, i ^ 1) for i in range(16)])


def hank_swap(value):
    return lax.ppermute(value, "hank", [(0, 1), (1, 0)])


def y_shift(value, steps):
    return lax.ppermute(value, "chan", [(i, (i & 4) | ((i + steps) & 3)) for i in range(NCHAN)])


def x_swap(value):
    return lax.ppermute(value, "chan", [(i, i ^ 4) for i in range(NCHAN)])


def signs_kernel(place, blocks, seed, signs):
    first_block = place[0] * (1024 // BLK)
    start = seed[0] * 7919 + place[1] * HALF_P

    def step(q, used):
        local = blocks[q] - first_block
        owned = (local >= 0) & (local < 1024 // BLK)

        @pl.when(owned)
        def _():
            index = lax.broadcasted_iota(jnp.int32, (BLK, HALF_P), 0) * P_SIZE
            index = index + lax.broadcasted_iota(jnp.int32, (BLK, HALF_P), 1)
            for j in range(Q):
                mixed = index + (start + (j * REF + q * BLK) * P_SIZE)
                mixed = mixed ^ (mixed >> 15)
                mixed = mixed * 668265263
                mixed = mixed ^ (mixed >> 13)
                sign = jnp.where((mixed & 512) != 0, F32(-1), F32(1))
                signs[used, j * BLK : (j + 1) * BLK, :] = sign.astype(BF16)

        return used + owned.astype(jnp.int32)

    lax.fori_loop(0, REF // BLK, step, jnp.int32(0))


def images_kernel(place, blocks, records, behind, signs, out, staged, shifted):
    first_block = place[0] * (1024 // BLK)
    out[...] = jnp.zeros_like(out)

    def step(q, used):
        local = blocks[q] - first_block
        owned = (local >= 0) & (local < 1024 // BLK)

        @pl.when(owned)
        def _():
            cols = pl.ds(pl.multiple_of(local * BLK, BLK), BLK)
            staged[pl.ds(0, Q), :] = behind[:, cols].astype(F32)
            staged[pl.ds(Q, ROWS), :] = records[:, cols].astype(F32)
            for j in range(Q):
                shifted[:, j * BLK : (j + 1) * BLK] = staged[pl.ds(Q - j, ROWS), :].astype(BF16)
            out[...] += jnp.dot(shifted[...], signs[used], preferred_element_type=F32)

        return used + owned.astype(jnp.int32)

    lax.fori_loop(0, REF // BLK, step, jnp.int32(0))


def probe_signs(place, ref_blocks, probe_seed):
    return pl.pallas_call(
        signs_kernel,
        out_shape=jax.ShapeDtypeStruct((1024 // BLK, Q * BLK, HALF_P), BF16),
        in_specs=[pl.BlockSpec(memory_space=SMEM)] * 3,
        out_specs=pl.BlockSpec(memory_space=VMEM),
        compiler_params=pltpu.CompilerParams(vmem_limit_bytes=16 << 20),
        cost_estimate=pl.CostEstimate(flops=0, bytes_accessed=14 << 20, transcendentals=0),
        name="probe_signs",
    )(place, ref_blocks, probe_seed)


def partial_images(place, ref_blocks, records, behind, signs):
    return pl.pallas_call(
        images_kernel,
        out_shape=jax.ShapeDtypeStruct((ROWS, HALF_P), F32),
        in_specs=[pl.BlockSpec(memory_space=SMEM)] * 2 + [pl.BlockSpec(memory_space=VMEM)] * 3,
        out_specs=pl.BlockSpec(memory_space=VMEM),
        scratch_shapes=[pltpu.VMEM((ROWS + Q, BLK), F32), pltpu.VMEM((ROWS, Q * BLK), BF16)],
        compiler_params=pltpu.CompilerParams(vmem_limit_bytes=24 << 20),
        cost_estimate=pl.CostEstimate(flops=4 << 30, bytes_accessed=2 << 20, transcendentals=0),
        name="partial_images",
    )(place, ref_blocks, records, behind, signs)


def order_kernel(place, *refs):
    out, staged = refs[-2:]
    at = 0
    for ref in refs[:-2]:
        for entry in range(ref.shape[0]):
            k = ((place[0] & 4) ^ (at & 4)) | ((place[0] - at) & 3)
            staged[pl.ds(pl.multiple_of(k * SHARE, SHARE), SHARE), :] = ref[entry].astype(F32)
            at += 1
    out[...] = staged[...].T.astype(BF16)


def turned_image(place, parts):
    return pl.pallas_call(
        order_kernel,
        out_shape=jax.ShapeDtypeStruct((HALF_P, ROWS), BF16),
        in_specs=[pl.BlockSpec(memory_space=SMEM)] + [pl.BlockSpec(memory_space=VMEM)] * len(parts),
        out_specs=pl.BlockSpec(memory_space=VMEM),
        scratch_shapes=[pltpu.VMEM((ROWS, HALF_P), F32)],
        compiler_params=pltpu.CompilerParams(vmem_limit_bytes=8 << 20),
        cost_estimate=pl.CostEstimate(flops=0, bytes_accessed=3 << 20, transcendentals=0),
        name="turned_image",
    )(place, *parts)


def sketch_kernel(count, starts, turn, first, last, *refs):
    place, ahead = refs[:2]
    inputs = len(starts)
    rows, images = refs[2 : 2 + inputs], refs[2 + inputs : 2 + inputs + count]
    staged, total = refs[-2:]
    out = refs[-3]
    running = None if first else refs[2 + inputs + count]
    for n in range(count):
        if inputs == count:
            staged[pl.ds(0, ROWS), :] = rows[n][pl.ds(starts[n], ROWS), :].astype(F32)
        else:
            for m in range(2):
                at = pl.multiple_of((place[1] ^ m) * (ROWS // 2), ROWS // 2)
                staged[pl.ds(at, ROWS // 2), :] = rows[m][pl.ds(starts[m], ROWS // 2), :].astype(F32)
        staged[pl.ds(ROWS, Q), :] = ahead[n].astype(F32)
        image = images[n][...]
        if count == 2:
            image = jnp.where(place[1] == turn, image, images[1 - n][...])
        for m in range(LAGS):
            pair = [staged[pl.ds(2 * m + 1 + i, ROWS), :].astype(BF16) for i in range(2)]
            term = jnp.dot(image, jnp.concatenate(pair, axis=1), preferred_element_type=F32)
            at = slice(2 * m * BLK, (2 * m + 2) * BLK)
            goal = total if last or n < count - 1 else out
            if n == 0:
                goal[:, at] = term if first else running[:, at] + term
            else:
                goal[:, at] = total[:, at] + term
    if last:
        lane = lax.broadcasted_iota(jnp.int32, (HALF_P, BLK), 1)
        for m in range(LAGS):
            even = total[:, 2 * m * BLK : (2 * m + 1) * BLK]
            odd = total[:, (2 * m + 1) * BLK : (2 * m + 2) * BLK]
            low = jnp.where(lane < CDEV, even, pltpu.roll(odd, CDEV, 1))
            high = jnp.where(lane < CDEV, pltpu.roll(even, CDEV, 1), odd)
            side = (m // 4) ^ place[1]
            out[place[2], side, m % 4] = low
            out[1 - place[2], side, m % 4] = high


def sketch_terms(place, ahead, rows, images, turn, running, last=False):
    count, first = len(images), running is None
    starts = [start for _, start in rows]
    rows = [value for value, _ in rows]
    shape = (2, 2, 4, HALF_P, BLK) if last else (HALF_P, Q * BLK)
    args = [place, ahead, *rows, *images] + ([] if first else [running])
    return pl.pallas_call(
        functools.partial(sketch_kernel, count, starts, turn, first, last),
        out_shape=jax.ShapeDtypeStruct(shape, F32),
        in_specs=[pl.BlockSpec(memory_space=SMEM)] + [pl.BlockSpec(memory_space=VMEM)] * (len(args) - 1),
        out_specs=pl.BlockSpec(memory_space=VMEM),
        scratch_shapes=[pltpu.VMEM((ROWS + Q, BLK), F32), pltpu.VMEM((HALF_P, Q * BLK), F32)],
        compiler_params=pltpu.CompilerParams(vmem_limit_bytes=24 << 20),
        cost_estimate=pl.CostEstimate(flops=count << 30, bytes_accessed=2 << 20, transcendentals=0),
        name="sketch_terms",
    )(*args)


def final_kernel(factor, count, place, *refs):
    out = refs[-1]
    for m in range(LAGS // 2):
        value = refs[0][m].astype(F32)
        if count == 2:
            value = value + refs[1][m]
        value = (value * factor).T
        for i in range(2):
            out[:, 2 * m + i, :] = value[i * CDEV : (i + 1) * CDEV]


def final_sketch(factor, place, side, terms, out):
    whole = pl.BlockSpec((LAGS // 2, HALF_P, BLK), lambda i, place: (0, 0, 0))
    goal = pl.BlockSpec((CDEV, LAGS, HALF_P), lambda i, place: (0, 0, place[1] ^ side))
    args = list(terms)
    in_specs = [whole] * len(terms)
    aliases = {}
    if out is not None:
        args.append(out)
        in_specs.append(pl.BlockSpec(memory_space=pl.ANY))
        aliases = {len(terms) + 1: 0}
    return pl.pallas_call(
        functools.partial(final_kernel, factor, len(terms)),
        out_shape=jax.ShapeDtypeStruct((CDEV, LAGS, P_SIZE), F32),
        grid_spec=pltpu.PrefetchScalarGridSpec(
            num_scalar_prefetch=1, grid=(1,), in_specs=in_specs, out_specs=goal
        ),
        input_output_aliases=aliases,
        compiler_params=pltpu.CompilerParams(vmem_limit_bytes=16 << 20),
        name="final_sketch",
    )(place, *args)


def per_device(records, ref_blocks, probe_seed):
    tm = lax.axis_index("tm")
    z, core = tm >> 1, tm & 1
    hank = lax.axis_index("hank")
    chan = lax.axis_index("chan")
    place = jnp.stack([chan, hank, core]).astype(jnp.int32)

    behind = tm_shift(records[ROWS - Q :], 1)
    signs = probe_signs(place, ref_blocks, probe_seed)
    partial = partial_images(place, ref_blocks, records, behind, signs)

    partial, sent = lax.optimization_barrier((partial, records))
    parts = lax.all_to_all(partial.reshape(NCHAN, SHARE, HALF_P), "chan", 0, 0, tiled=True)
    sign = 1 - 2 * hank

    def piece(steps):
        return lax.dynamic_slice_in_dim(sent, ((z + steps) & (NZ - 1)) * BLK, BLK, 1)

    own = piece(0)
    half = lax.dynamic_slice_in_dim(piece(4), hank * (ROWS // 2), ROWS // 2, 0)
    far = split_shift(piece(3 * sign), 3, -3)
    half = split_shift(half, 4, 4)
    middle = split_shift(piece(-2 * sign), -2, 2)
    near = split_shift(piece(-sign), -1, 1)
    parts, far, middle = lax.optimization_barrier((parts, far, middle))

    share = jnp.sum(parts, axis=0).astype(BF16)[None]
    got = [share] + [y_shift(share, k) for k in range(1, 4)]
    got[3], half, near = lax.optimization_barrier((got[3], half, near))
    got.append(x_swap(jnp.concatenate(got)))
    image = turned_image(place, got)
    image, near, middle, far, half = lax.optimization_barrier((image, near, middle, far, half))
    other_first = hank_swap(jnp.concatenate([near, middle]))
    other_last = hank_swap(jnp.concatenate([far, half]))

    even = hank == 0
    ends = other_last[ROWS : ROWS + Q]
    fronts = [None] * NZ
    fronts[0], fronts[4] = own[:Q], jnp.where(even, half[:Q], ends)
    for k, mine, theirs in (
        (7, near[:Q], other_first[:Q]),
        (6, middle[:Q], other_first[ROWS : ROWS + Q]),
        (3, far[:Q], other_last[:Q]),
    ):
        fronts[k] = jnp.where(even, mine, theirs)
        fronts[NZ - k] = jnp.where(even, theirs, mine)
    given = core_swap(jnp.stack(fronts))
    later = jnp.concatenate([given[NZ - 1 :], given[: NZ - 1]], axis=0)
    edge = (((z - jnp.arange(NZ)) & (NZ - 1)) == NZ - 1)[:, None, None]
    ahead = jnp.where(core == 0, given, jnp.where(edge, jnp.zeros_like(later), later))

    def halo(k):
        return jnp.stack([jnp.where(even, ahead[k], ahead[NZ - k]), jnp.where(even, ahead[NZ - k], ahead[k])])

    forward = backward = image
    pieces = (
        [(near, 0), (other_first, 0)],
        [(middle, 0), (other_first, ROWS)],
        [(far, 0), (other_last, 0)],
    )
    running = None
    for step in range(1, 4):
        forward = z_shift(forward, 1)
        backward = z_shift(backward, -1)
        if step == 1:
            running = sketch_terms(place, ahead[:1], [(own, 0)], [image], None, None)
        turn = 0 if step == 3 else 1
        k = NZ - step if turn else step
        running = sketch_terms(place, halo(k), pieces[step - 1], [forward, backward], turn, running)
    top = z_shift(forward[: HALF_P // 2], 1)
    bottom = z_shift(backward[HALF_P // 2 :], -1)
    image = jnp.concatenate([top, bottom], axis=0)
    total = sketch_terms(place, ahead[4:5], [(half, 0), (other_last, ROWS)], [image], None, running, True)

    near_far = core_swap(total[1, 1])
    theirs = hank_swap((total[0, 1] + near_far).astype(BF16))
    factor = 1.0 / math.sqrt(ROWS * 16 * Q * REF)
    out = final_sketch(factor, place, 0, [total[0, 0], core_swap(total[1, 0])], None)
    return final_sketch(factor, place, 1, [theirs], out)[None]


def solution(mesh):
    in_specs = (P("tm", "chan"), P(), P())
    out_specs = P("chan", "tm", "hank", None)
    return jax.shard_map(
        per_device, mesh=mesh, in_specs=in_specs, out_specs=out_specs, check_vma=False
    )
```

time: 327 us -> 106 us (0.32)
  waiting for transfers between devices: 181 us -> 29.5 us
  blocking collectives: 65.1 us -> 0 us
  starting transfers between devices: 7.02 us -> 52.3 us
  local copies, waits for them, and re-layouts: 29.4 us -> 1.8 us
  matrix products: 22.6 us -> 0 us
  Pallas kernels: 0 us -> 19.3 us
  between operations: 14.3 us -> 0.89 us
  other arithmetic: 6.32 us -> 0.44 us
    reduce_scatter x2 -> x0, waiting for transfers between devices: 178 us -> none  [the longest x1 112 us: per_device(): lax.psum_scatter(jnp.einsum('isc,sp->cip', stacked, images, preferred_ele...]
    psum x1 -> x0, blocking collectives: 65.1 us -> none  [per_device(): images = lax.psum(running, 'chan')]
    ppermute x2 -> x23, starting transfers between devices: 6.98 us -> 47.3 us  [the longest x8 12.5 us: z_shift(): lax.ppermute(value, 'tm', [(i, (i + 2 * steps) % 16) for i in range(16)])]
    ppermute x2 -> x23, waiting for transfers between devices: 3.29 us -> 29.5 us  [the longest x3 11.7 us: hank_swap(): return lax.ppermute(value, 'hank', [(0, 1), (1, 0)])]
    dot_general x17 -> x0, matrix products: 22.6 us -> none  [the longest x1 11.5 us: per_device(): jnp.einsum('isc,sp->cip', stacked, images, preferred_element_type=jnp.flo...]
    pallas_call x0 -> x10, Pallas kernels: none -> 19.3 us  [the longest x5 8.6 us: sketch_terms(): pl.pallas_call(functools.partial(sketch_kernel, count, starts, turn, firs...]
    transpose x1 -> x0, local copies, waits for them, and re-layouts: 17.6 us -> none  [per_device(): jnp.einsum('isc,sp->cip', stacked, images, preferred_element_type=jnp.flo...]
    unnamed x12 -> x5, local copies, waits for them, and re-layouts: 8.88 us -> 0.66 us
  transfers between devices with their start and end apart: 4 -> 24, of which waited for: 4 -> 11; matrix products, arithmetic and copies ran while one was open for 3% -> 1% of each run, Pallas kernels for 0% -> 11%
where the time goes in v2:
time: 106 us; the launch traced here: 104 us
  starting transfers between devices  52.3 us (49%)
  waiting for transfers between devices  29.5 us (28%)
  Pallas kernels  19.3 us (18%)
  local copies, waits for them, and re-layouts  1.8 us (2%)
    ppermute x8, starting transfers between devices, z_shift(): lax.ppermute(value, 'tm', [(i, (i + 2 * steps) % 16) for i in range(16)])  12.5 us
    ppermute x3, waiting for transfers between devices, hank_swap(): return lax.ppermute(value, 'hank', [(0, 1), (1, 0)])  11.7 us
    ppermute x4, starting transfers between devices, split_shift(): return lax.ppermute(value, ('tm', 'hank'), pairs)  10.9 us
    pallas_call x5, Pallas kernels, sketch_terms(): pl.pallas_call(functools.partial(sketch_kernel, count, starts, turn, firs...  8.6 us
    ppermute x8, waiting for transfers between devices, z_shift(): lax.ppermute(value, 'tm', [(i, (i + 2 * steps) % 16) for i in range(16)])  8.39 us
    ppermute x3, starting transfers between devices, core_swap(): return lax.ppermute(value, 'tm', [(i, i ^ 1) for i in range(16)])  6.82 us
    all_to_all x1, starting transfers between devices, per_device(): lax.all_to_all(partial.reshape(NCHAN, SHARE, HALF_P), 'chan', 0, 0, tiled...  5.04 us
    ppermute x1, starting transfers between devices, tm_shift(): lax.ppermute(value, 'tm', [(i, i + steps) for i in range(first, last)])  4.92 us
  transfers between devices with their start and end apart: 24, of which 11 were waited for; matrix products, arithmetic and copies ran while one was open for 1% of the time, Pallas kernels for 11%

profile of v2, /device:TPU:1, one launch (start us, length us, event | category | flops | bytes accessed | tf_op | source)
XLA Modules:
  0.0 104.2 jit_solution(2545861976386506158)
XLA Ops:
  0.0 0.8 slice.84
  0.8 4.9 %collective-permute-start = (bf16[16,1024]{1,0:T(8,128)(2,1)S(1)}, bf16[16,1024]{1,0:T(8,128)(2,1)S(1)}, u32[]{:S(2)}, u32[]{:S(2)}) collective-permute-start(bf16[16,1024]{1,0:T(8,128)(2,1)S(1)} %slice.84), channel_id=1, source_target_pairs={{0,16},{16,32},{32,48},{48,64},{64,80},{80,96},{96,112},{112,128},... | collective-permute-start | bytes 98312 | tf_op jit(solution)/shard_map/ppermute | solution.py:30
  5.7 0.1 pad_add_fusion.place.refs_0_
  6.4 0.6 copy-done.1
  7.1 2.8 %probe_signs.1.signs = bf16[8,2048,256]{2,1,0:T(8,128)(2,1)S(1)} custom-call(s32[3]{0:T(128)S(1)} %pad_add_fusion.place.refs_0_, s32[16]{0:T(128)S(1)} %copy-done.1, s32[1]{0:T(128)S(6)} %copy.13.seed), custom_call_target="tpu_custom_call" | custom-call | bytes 14680064 | tf_op jit(solution)/shard_map/probe_signs/pallas_call | solution.py:109
  9.9 4.1 %partial_images.1 = f32[512,256]{1,0:T(8,128)} custom-call(s32[3]{0:T(128)S(1)} %pad_add_fusion.place.refs_0_, s32[16]{0:T(128)S(1)} %copy-done.1, bf16[512,1024]{1,0:T(8,128)(2,1)S(1)} %copy-done, bf16[16,1024]{1,0:T(8,128)(2,1)S(1)} %collective-permute-done.behind, bf16[8,2048,256]{2,1,0:T(8,128)(2,1)S(1)} %probe_signs.1.signs), custom_call_target="tpu_custom_call" | custom-call | flops 4294967296 | bytes 2097152 | tf_op jit(solution)/shard_map/partial_images/pallas_call | solution.py:121
  13.9 5.0 %all-to-all-start = ((f32[8,64,256]{2,1,0:T(8,128)}), f32[8,64,256]{2,1,0:T(8,128)S(1)}, u32[]{:S(2)}, u32[]{:S(2)}) async-start(f32[8,64,256]{2,1,0:T(8,128)} %bitcast.4), calls=%async_computation | async-start | bytes 1048576 | tf_op jit(solution)/shard_map/all_to_all | solution.py:259
  19.0 0.1 constant_dynamic-slice_fusion.3
  19.1 5.6 %collective-permute-start.1 = (bf16[512,128]{1,0:T(8,128)(2,1)S(1)}, bf16[512,128]{1,0:T(8,128)(2,1)S(1)}, u32[]{:S(2)}, u32[]{:S(2)}) collective-permute-start(bf16[512,128]{1,0:T(8,128)(2,1)S(1)} %get-tuple-element.37), channel_id=1, source_target_pairs={{0,96},{1,161},{16,112},{17,177},{32,128},{33,193},{48,144},{49,20... | collective-permute-start | bytes 393224 | tf_op jit(solution)/shard_map/ppermute | solution.py:42
  24.8 0.4 collective-permute-start.7
  25.1 0.1 dynamic_slice.19
  25.3 4.9 %collective-permute-start.6 = (bf16[256,128]{1,0:T(8,128)(2,1)S(1)}, bf16[256,128]{1,0:T(8,128)(2,1)S(1)}, u32[]{:S(2)}, u32[]{:S(2)}) collective-permute-start(bf16[256,128]{1,0:T(8,128)(2,1)S(1)} %dynamic_slice.19), channel_id=1, source_target_pairs={{0,128},{1,129},{16,144},{17,145},{32,160},{33,161},{48,176},{49,1... | collective-permute-start | bytes 196616 | tf_op jit(solution)/shard_map/ppermute | solution.py:42
  30.2 2.5 %collective-permute-done.1.refs_2_ = bf16[512,128]{1,0:T(8,128)(2,1)S(1)} collective-permute-done((bf16[512,128]{1,0:T(8,128)(2,1)S(1)}, bf16[512,128]{1,0:T(8,128)(2,1)S(1)}, u32[]{:S(2)}, u32[]{:S(2)}) %collective-permute-start.1) | collective-permute-done | bytes 131104 | tf_op jit(solution)/shard_map/ppermute | solution.py:42
  32.7 2.9 %collective-permute-start.5 = (bf16[1,64,256]{2,1,0:T(8,128)(2,1)S(1)}, bf16[1,64,256]{2,1,0:T(8,128)(2,1)S(1)}, u32[]{:S(2)}, u32[]{:S(2)}) collective-permute-start(bf16[1,64,256]{2,1,0:T(8,128)(2,1)S(1)} %bitcast.40), channel_id=1, source_target_pairs={{0,6},{2,0},{4,2},{6,4},{8,14},{10,8},{12,10},{14,12},{1,7},{3,1},... | collective-permute-start | bytes 98312 | tf_op jit(solution)/shard_map/ppermute | solution.py:54
  35.6 1.8 %collective-permute-start.4 = (bf16[1,64,256]{2,1,0:T(8,128)(2,1)S(1)}, bf16[1,64,256]{2,1,0:T(8,128)(2,1)S(1)}, u32[]{:S(2)}, u32[]{:S(2)}) collective-permute-start(bf16[1,64,256]{2,1,0:T(8,128)(2,1)S(1)} %bitcast.42), channel_id=1, source_target_pairs={{0,4},{2,6},{4,0},{6,2},{8,12},{10,14},{12,8},{14,10},{1,5},{3,7},... | collective-permute-start | bytes 98312 | tf_op jit(solution)/shard_map/ppermute | solution.py:54
  37.4 2.3 %collective-permute-done.3.refs_1_ = bf16[1,64,256]{2,1,0:T(8,128)(2,1)S(1)} collective-permute-done((bf16[1,64,256]{2,1,0:T(8,128)(2,1)S(1)}, bf16[1,64,256]{2,1,0:T(8,128)(2,1)S(1)}, u32[]{:S(2)}, u32[]{:S(2)}) %collective-permute-start.3) | collective-permute-done | bytes 32800 | tf_op jit(solution)/shard_map/ppermute | solution.py:54
  39.6 0.5 collective-permute-done.4.refs_2_
  40.2 2.8 %collective-permute-start.8 = (bf16[4,64,256]{2,1,0:T(8,128)(2,1)S(1)}, bf16[4,64,256]{2,1,0:T(8,128)(2,1)S(1)}, u32[]{:S(2)}, u32[]{:S(2)}) collective-permute-start(bf16[4,64,256]{2,1,0:T(8,128)(2,1)S(1)} %pad_maximum_fusion.3), channel_id=1, source_target_pairs={{0,8},{2,10},{4,12},{6,14},{8,0},{10,2},{12,4},{14,6},{1,9},{3,11}... | collective-permute-start | bytes 393224 | tf_op jit(solution)/shard_map/ppermute | solution.py:58
  42.9 2.6 %collective-permute-done.8.refs_4_ = bf16[4,64,256]{2,1,0:T(8,128)(2,1)S(1)} collective-permute-done((bf16[4,64,256]{2,1,0:T(8,128)(2,1)S(1)}, bf16[4,64,256]{2,1,0:T(8,128)(2,1)S(1)}, u32[]{:S(2)}, u32[]{:S(2)}) %collective-permute-start.8) | collective-permute-done | bytes 131104 | tf_op jit(solution)/shard_map/ppermute | solution.py:58
  45.6 0.7 turned_image.1.refs_3_
  46.3 2.7 %collective-permute-start.9 = (bf16[1024,128]{1,0:T(8,128)(2,1)S(1)}, bf16[1024,128]{1,0:T(8,128)(2,1)S(1)}, u32[]{:S(2)}, u32[]{:S(2)}) collective-permute-start(bf16[1024,128]{1,0:T(8,128)(2,1)S(1)} %pad_maximum_fusion), channel_id=1, source_target_pairs={{0,1},{1,0},{2,3},{3,2},{4,5},{5,4},{6,7},{7,6},{8,9},{9,8},{10,11... | collective-permute-start | bytes 786440 | tf_op jit(solution)/shard_map/ppermute | solution.py:50
  49.1 1.5 %collective-permute-start.12 = (bf16[256,512]{1,0:T(8,128)(2,1)S(1)}, bf16[256,512]{1,0:T(8,128)(2,1)S(1)}, u32[]{:S(2)}, u32[]{:S(2)}) collective-permute-start(bf16[256,512]{1,0:T(8,128)(2,1)S(1)} %turned_image.1.refs_3_), channel_id=1, source_target_pairs={{0,32},{16,48},{32,64},{48,80},{64,96},{80,112},{96,128},{112,144}... | collective-permute-start | bytes 786440 | tf_op jit(solution)/shard_map/ppermute | solution.py:34
  50.6 0.2 collective-permute-start.10
  50.8 2.8 %collective-permute-done.9.refs_3_ = bf16[1024,128]{1,0:T(8,128)(2,1)S(1)} collective-permute-done((bf16[1024,128]{1,0:T(8,128)(2,1)S(1)}, bf16[1024,128]{1,0:T(8,128)(2,1)S(1)}, u32[]{:S(2)}, u32[]{:S(2)}) %collective-permute-start.9) | collective-permute-done | bytes 262176 | tf_op jit(solution)/shard_map/ppermute | solution.py:50
  53.5 4.3 %collective-permute-done.10.refs_3_ = bf16[768,128]{1,0:T(8,128)(2,1)S(1)} collective-permute-done((bf16[768,128]{1,0:T(8,128)(2,1)S(1)}, bf16[768,128]{1,0:T(8,128)(2,1)S(1)}, u32[]{:S(2)}, u32[]{:S(2)}) %collective-permute-start.10) | collective-permute-done | bytes 196640 | tf_op jit(solution)/shard_map/ppermute | solution.py:50
  57.9 3.5 %collective-permute-start.11 = (bf16[8,16,128]{2,1,0:T(8,128)(2,1)S(1)}, bf16[8,16,128]{2,1,0:T(8,128)(2,1)S(1)}, u32[]{:S(2)}, u32[]{:S(2)}) collective-permute-start(bf16[8,16,128]{2,1,0:T(8,128)(2,1)S(1)} %constant_dynamic-update-slice_fusion), channel_id=1, source_target_pairs={{0,16},{16,0},{32,48},{48,32},{64,80},{80,64},{96,112},{112,96},{1... | collective-permute-start | bytes 98312 | tf_op jit(solution)/shard_map/ppermute | solution.py:46
  61.4 4.1 %collective-permute-start.17 = (bf16[256,512]{1,0:T(8,128)(2,1)S(1)}, bf16[256,512]{1,0:T(8,128)(2,1)S(1)}, u32[]{:S(2)}, u32[]{:S(2)}) collective-permute-start(bf16[256,512]{1,0:T(8,128)(2,1)S(1)} %collective-permute-done.16.refs_5_), channel_id=1, source_target_pairs={{0,224},{16,240},{32,0},{48,16},{64,32},{80,48},{96,64},{112,80},{... | collective-permute-start | bytes 786440 | tf_op jit(solution)/shard_map/ppermute | solution.py:34
  65.5 0.1 fusion.2
  65.6 1.3 %sketch_terms.5.refs_6_ = f32[256,2048]{1,0:T(8,128)S(1)} custom-call(s32[3]{0:T(128)S(1)} %pad_add_fusion.place.refs_0_, bf16[1,16,128]{2,1,0:T(8,128)(2,1)S(1)} %get-tuple-element.38.refs_1_, bf16[512,128]{1,0:T(8,128)(2,1)S(1)} %get-tuple-element.34.refs_2_, bf16[256,512]{1,0:T(8,128)(2,1)S(1)} %turned_image.1.refs_3_), custom_call_target="tpu_custom_call" | custom-call | flops 1073741824 | bytes 2097152 | tf_op jit(solution)/shard_map/sketch_terms/pallas_call | solution.py:202
  66.9 1.9 %sketch_terms.6.refs_6_ = f32[256,2048]{1,0:T(8,128)S(1)} custom-call(s32[3]{0:T(128)S(1)} %pad_add_fusion.place.refs_0_, bf16[2,16,128]{2,1,0:T(8,128)(2,1)S(1)} %pad_maximum_fusion.6.refs_1_, bf16[512,128]{1,0:T(8,128)(2,1)S(1)} %collective-permute-done.7.refs_2_, bf16[1024,128]{1,0:T(8,128)(2,1)S(1)} %collective-permute-done.9.refs_3_, ...), custom_call_target="tpu_custom_call" | custom-call | flops 2147483648 | bytes 2097152 | tf_op jit(solution)/shard_map/sketch_terms/pallas_call | solution.py:202
  68.8 2.3 %collective-permute-done.17.refs_5_ = bf16[256,512]{1,0:T(8,128)(2,1)S(1)} collective-permute-done((bf16[256,512]{1,0:T(8,128)(2,1)S(1)}, bf16[256,512]{1,0:T(8,128)(2,1)S(1)}, u32[]{:S(2)}, u32[]{:S(2)}) %collective-permute-start.17) | collective-permute-done | bytes 262176 | tf_op jit(solution)/shard_map/ppermute | solution.py:34
  71.2 3.4 %collective-permute-start.18 = (bf16[256,512]{1,0:T(8,128)(2,1)S(1)}, bf16[256,512]{1,0:T(8,128)(2,1)S(1)}, u32[]{:S(2)}, u32[]{:S(2)}) collective-permute-start(bf16[256,512]{1,0:T(8,128)(2,1)S(1)} %collective-permute-done.17.refs_5_), channel_id=1, source_target_pairs={{0,224},{16,240},{32,0},{48,16},{64,32},{80,48},{96,64},{112,80},{... | collective-permute-start | bytes 786440 | tf_op jit(solution)/shard_map/ppermute | solution.py:34
  74.6 1.9 %sketch_terms.7.refs_6_ = f32[256,2048]{1,0:T(8,128)S(1)} custom-call(s32[3]{0:T(128)S(1)} %pad_add_fusion.place.refs_0_, bf16[2,16,128]{2,1,0:T(8,128)(2,1)S(1)} %pad_maximum_fusion.5.refs_1_, bf16[512,128]{1,0:T(8,128)(2,1)S(1)} %collective-permute-done.2.refs_2_, bf16[1024,128]{1,0:T(8,128)(2,1)S(1)} %collective-permute-done.9.refs_3_, ...), custom_call_target="tpu_custom_call" | custom-call | flops 2147483648 | bytes 2097152 | tf_op jit(solution)/shard_map/sketch_terms/pallas_call | solution.py:202
  76.5 2.9 %collective-permute-done.18.refs_5_ = bf16[256,512]{1,0:T(8,128)(2,1)S(1)} collective-permute-done((bf16[256,512]{1,0:T(8,128)(2,1)S(1)}, bf16[256,512]{1,0:T(8,128)(2,1)S(1)}, u32[]{:S(2)}, u32[]{:S(2)}) %collective-permute-start.18) | collective-permute-done | bytes 262176 | tf_op jit(solution)/shard_map/ppermute | solution.py:34
  79.4 3.5 %collective-permute-start.19 = (bf16[128,512]{1,0:T(8,128)(2,1)S(1)}, bf16[128,512]{1,0:T(8,128)(2,1)S(1)}, u32[]{:S(2)}, u32[]{:S(2)}) collective-permute-start(bf16[128,512]{1,0:T(8,128)(2,1)S(1)} %slice.118), channel_id=1, source_target_pairs={{0,224},{16,240},{32,0},{48,16},{64,32},{80,48},{96,64},{112,80},{... | collective-permute-start | bytes 393224 | tf_op jit(solution)/shard_map/ppermute | solution.py:34
  82.9 0.1 collective-permute-start.15
  83.0 1.8 %sketch_terms.8.refs_5_ = f32[256,2048]{1,0:T(8,128)S(1)} custom-call(s32[3]{0:T(128)S(1)} %pad_add_fusion.place.refs_0_, bf16[2,16,128]{2,1,0:T(8,128)(2,1)S(1)} %pad_maximum_fusion.4.refs_1_, bf16[512,128]{1,0:T(8,128)(2,1)S(1)} %collective-permute-done.1.refs_2_, bf16[768,128]{1,0:T(8,128)(2,1)S(1)} %collective-permute-done.10.refs_3_, ...), custom_call_target="tpu_custom_call" | custom-call | flops 2147483648 | bytes 2097152 | tf_op jit(solution)/shard_map/sketch_terms/pallas_call | solution.py:202
  84.8 3.2 %collective-permute-done.15 = bf16[128,512]{1,0:T(8,128)(2,1)S(1)} collective-permute-done((bf16[128,512]{1,0:T(8,128)(2,1)S(1)}, bf16[128,512]{1,0:T(8,128)(2,1)S(1)}, u32[]{:S(2)}, u32[]{:S(2)}) %collective-permute-start.15) | collective-permute-done | bytes 131104 | tf_op jit(solution)/shard_map/ppermute | solution.py:34
  88.0 1.7 %sketch_terms.9 = f32[2,2,4,256,128]{4,3,2,1,0:T(8,128)S(1)} custom-call(s32[3]{0:T(128)S(1)} %pad_add_fusion.place.refs_0_, bf16[1,16,128]{2,1,0:T(8,128)(2,1)S(1)} %get-tuple-element.45.refs_1_, bf16[256,128]{1,0:T(8,128)(2,1)S(1)} %collective-permute-done.6.refs_2_, bf16[768,128]{1,0:T(8,128)(2,1)S(1)} %collective-permute-done.10.refs_3_, ...), custom_call_target="tpu_custom_call" | custom-call | flops 1073741824 | bytes 2097152 | tf_op jit(solution)/shard_map/sketch_terms/pallas_call | solution.py:202
  89.7 0.1 slice_bitcast_fusion
  89.8 3.2 %collective-permute-start.20 = (f32[4,256,128]{2,1,0:T(8,128)S(1)}, f32[4,256,128]{2,1,0:T(8,128)S(1)}, u32[]{:S(2)}, u32[]{:S(2)}) collective-permute-start(f32[4,256,128]{2,1,0:T(8,128)S(1)} %get-tuple-element.33), channel_id=1, source_target_pairs={{0,16},{16,0},{32,48},{48,32},{64,80},{80,64},{96,112},{112,96},{1... | collective-permute-start | bytes 1572872 | tf_op jit(solution)/shard_map/ppermute | solution.py:46
  93.0 0.1 collective-permute-start.22
  93.1 1.4 %collective-permute-done.20 = f32[4,256,128]{2,1,0:T(8,128)S(1)} collective-permute-done((f32[4,256,128]{2,1,0:T(8,128)S(1)}, f32[4,256,128]{2,1,0:T(8,128)S(1)}, u32[]{:S(2)}, u32[]{:S(2)}) %collective-permute-start.20) | collective-permute-done | bytes 524320 | tf_op jit(solution)/shard_map/ppermute | solution.py:46
  94.6 0.1 fusion.1
  94.7 1.7 %collective-permute-start.21 = (bf16[4,256,128]{2,1,0:T(8,128)(2,1)S(1)}, bf16[4,256,128]{2,1,0:T(8,128)(2,1)S(1)}, u32[]{:S(2)}, u32[]{:S(2)}) collective-permute-start(bf16[4,256,128]{2,1,0:T(8,128)(2,1)S(1)} %fusion.1), channel_id=1, source_target_pairs={{0,1},{1,0},{2,3},{3,2},{4,5},{5,4},{6,7},{7,6},{8,9},{9,8},{10,11... | collective-permute-start | bytes 786440 | tf_op jit(solution)/shard_map/ppermute | solution.py:50
  96.4 1.6 %final_sketch.2.refs_1_ = f32[64,8,512]{2,1,0:T(8,128)} custom-call(s32[3]{0:T(128)S(1)} %pad_add_fusion.place.refs_0_, f32[4,256,128]{2,1,0:T(8,128)S(1)} %get-tuple-element.32.refs_0_, f32[4,256,128]{2,1,0:T(8,128)S(1)} %collective-permute-done.22.refs_1_), custom_call_target="tpu_custom_call" | custom-call | tf_op jit(solution)/shard_map/final_sketch/pallas_call | solution.py:235
  98.0 4.7 %collective-permute-done.21.refs_0_ = bf16[4,256,128]{2,1,0:T(8,128)(2,1)S(1)} collective-permute-done((bf16[4,256,128]{2,1,0:T(8,128)(2,1)S(1)}, bf16[4,256,128]{2,1,0:T(8,128)(2,1)S(1)}, u32[]{:S(2)}, u32[]{:S(2)}) %collective-permute-start.21) | collective-permute-done | bytes 262176 | tf_op jit(solution)/shard_map/ppermute | solution.py:50
  102.6 1.6 %final_sketch.3 = f32[64,8,512]{2,1,0:T(8,128)} custom-call(s32[3]{0:T(128)S(1)} %pad_add_fusion.place.refs_0_, bf16[4,256,128]{2,1,0:T(8,128)(2,1)S(1)} %collective-permute-done.21.refs_0_, f32[64,8,512]{2,1,0:T(8,128)} %final_sketch.2.refs_1_), custom_call_target="tpu_custom_call", output_to_operand_aliasing={{}: (2, {})} | custom-call | tf_op jit(solution)/shard_map/final_sketch/pallas_call | solution.py:235
  (43 shorter events, 0.3 us)
Async XLA Ops:
  0.8 9.1 %collective-permute-start = (bf16[16,1024]{1,0:T(8,128)(2,1)S(1)}, bf16[16,1024]{1,0:T(8,128)(2,1)S(1)}, u32[]{:S(2)}, u32[]{:S(2)}) collective-permute-start(bf16[16,1024]{1,0:T(8,128)(2,1)S(1)} %slice.84), channel_id=1, source_target_pairs={{0,16},{16,32},{32,48},{48,64},{64,80},{80,96},{96,112},{112,128},... | collective-permute-start | bytes 98312 | tf_op jit(solution)/shard_map/ppermute | solution.py:30
  6.4 0.7 copy-start.1
  7.1 2.8 %copy-start = (bf16[512,1024]{1,0:T(8,128)(2,1)S(1)}, bf16[512,1024]{1,0:T(8,128)(2,1)}, u32[]{:S(2)}) copy-start(bf16[512,1024]{1,0:T(8,128)(2,1)} %records.1) | copy-start | bytes 3145732
  13.9 18.7 %all-to-all-start = ((f32[8,64,256]{2,1,0:T(8,128)}), f32[8,64,256]{2,1,0:T(8,128)S(1)}, u32[]{:S(2)}, u32[]{:S(2)}) async-start(f32[8,64,256]{2,1,0:T(8,128)} %bitcast.4), calls=%async_computation | async-start | bytes 1048576 | tf_op jit(solution)/shard_map/all_to_all | solution.py:259
  19.1 13.5 %collective-permute-start.1 = (bf16[512,128]{1,0:T(8,128)(2,1)S(1)}, bf16[512,128]{1,0:T(8,128)(2,1)S(1)}, u32[]{:S(2)}, u32[]{:S(2)}) collective-permute-start(bf16[512,128]{1,0:T(8,128)(2,1)S(1)} %get-tuple-element.37), channel_id=1, source_target_pairs={{0,96},{1,161},{16,112},{17,177},{32,128},{33,193},{48,144},{49,20... | collective-permute-start | bytes 393224 | tf_op jit(solution)/shard_map/ppermute | solution.py:42
  24.8 7.9 %collective-permute-start.2 = (bf16[512,128]{1,0:T(8,128)(2,1)S(1)}, bf16[512,128]{1,0:T(8,128)(2,1)S(1)}, u32[]{:S(2)}, u32[]{:S(2)}) collective-permute-start(bf16[512,128]{1,0:T(8,128)(2,1)S(1)} %get-tuple-element.36), channel_id=1, source_target_pairs={{0,192},{1,65},{16,208},{17,81},{32,224},{33,97},{48,240},{49,113}... | collective-permute-start | bytes 393224 | tf_op jit(solution)/shard_map/ppermute | solution.py:42
  24.8 12.6 %collective-permute-start.7 = (bf16[512,128]{1,0:T(8,128)(2,1)S(1)}, bf16[512,128]{1,0:T(8,128)(2,1)S(1)}, u32[]{:S(2)}, u32[]{:S(2)}) collective-permute-start(bf16[512,128]{1,0:T(8,128)(2,1)S(1)} %get-tuple-element.35), channel_id=1, source_target_pairs={{0,224},{1,33},{16,240},{17,49},{32,0},{33,65},{48,16},{49,81},{64... | collective-permute-start | bytes 393224 | tf_op jit(solution)/shard_map/ppermute | solution.py:42
  25.3 12.1 %collective-permute-start.6 = (bf16[256,128]{1,0:T(8,128)(2,1)S(1)}, bf16[256,128]{1,0:T(8,128)(2,1)S(1)}, u32[]{:S(2)}, u32[]{:S(2)}) collective-permute-start(bf16[256,128]{1,0:T(8,128)(2,1)S(1)} %dynamic_slice.19), channel_id=1, source_target_pairs={{0,128},{1,129},{16,144},{17,145},{32,160},{33,161},{48,176},{49,1... | collective-permute-start | bytes 196616 | tf_op jit(solution)/shard_map/ppermute | solution.py:42
  32.7 4.6 %collective-permute-start.5 = (bf16[1,64,256]{2,1,0:T(8,128)(2,1)S(1)}, bf16[1,64,256]{2,1,0:T(8,128)(2,1)S(1)}, u32[]{:S(2)}, u32[]{:S(2)}) collective-permute-start(bf16[1,64,256]{2,1,0:T(8,128)(2,1)S(1)} %bitcast.40), channel_id=1, source_target_pairs={{0,6},{2,0},{4,2},{6,4},{8,14},{10,8},{12,10},{14,12},{1,7},{3,1},... | collective-permute-start | bytes 98312 | tf_op jit(solution)/shard_map/ppermute | solution.py:54
  35.6 4.0 %collective-permute-start.3 = (bf16[1,64,256]{2,1,0:T(8,128)(2,1)S(1)}, bf16[1,64,256]{2,1,0:T(8,128)(2,1)S(1)}, u32[]{:S(2)}, u32[]{:S(2)}) collective-permute-start(bf16[1,64,256]{2,1,0:T(8,128)(2,1)S(1)} %bitcast.41), channel_id=1, source_target_pairs={{0,2},{2,4},{4,6},{6,0},{8,10},{10,12},{12,14},{14,8},{1,3},{3,5},... | collective-permute-start | bytes 98312 | tf_op jit(solution)/shard_map/ppermute | solution.py:54
  35.6 4.5 %collective-permute-start.4 = (bf16[1,64,256]{2,1,0:T(8,128)(2,1)S(1)}, bf16[1,64,256]{2,1,0:T(8,128)(2,1)S(1)}, u32[]{:S(2)}, u32[]{:S(2)}) collective-permute-start(bf16[1,64,256]{2,1,0:T(8,128)(2,1)S(1)} %bitcast.42), channel_id=1, source_target_pairs={{0,4},{2,6},{4,0},{6,2},{8,12},{10,14},{12,8},{14,10},{1,5},{3,7},... | collective-permute-start | bytes 98312 | tf_op jit(solution)/shard_map/ppermute | solution.py:54
  40.2 5.4 %collective-permute-start.8 = (bf16[4,64,256]{2,1,0:T(8,128)(2,1)S(1)}, bf16[4,64,256]{2,1,0:T(8,128)(2,1)S(1)}, u32[]{:S(2)}, u32[]{:S(2)}) collective-permute-start(bf16[4,64,256]{2,1,0:T(8,128)(2,1)S(1)} %pad_maximum_fusion.3), channel_id=1, source_target_pairs={{0,8},{2,10},{4,12},{6,14},{8,0},{10,2},{12,4},{14,6},{1,9},{3,11}... | collective-permute-start | bytes 393224 | tf_op jit(solution)/shard_map/ppermute | solution.py:58
  46.3 7.2 %collective-permute-start.9 = (bf16[1024,128]{1,0:T(8,128)(2,1)S(1)}, bf16[1024,128]{1,0:T(8,128)(2,1)S(1)}, u32[]{:S(2)}, u32[]{:S(2)}) collective-permute-start(bf16[1024,128]{1,0:T(8,128)(2,1)S(1)} %pad_maximum_fusion), channel_id=1, source_target_pairs={{0,1},{1,0},{2,3},{3,2},{4,5},{5,4},{6,7},{7,6},{8,9},{9,8},{10,11... | collective-permute-start | bytes 786440 | tf_op jit(solution)/shard_map/ppermute | solution.py:50
  49.1 12.3 %collective-permute-start.16 = (bf16[256,512]{1,0:T(8,128)(2,1)S(1)}, bf16[256,512]{1,0:T(8,128)(2,1)S(1)}, u32[]{:S(2)}, u32[]{:S(2)}) collective-permute-start(bf16[256,512]{1,0:T(8,128)(2,1)S(1)} %turned_image.1.refs_3_), channel_id=1, source_target_pairs={{0,224},{16,240},{32,0},{48,16},{64,32},{80,48},{96,64},{112,80},{... | collective-permute-start | bytes 786440 | tf_op jit(solution)/shard_map/ppermute | solution.py:34
  49.1 16.4 %collective-permute-start.12 = (bf16[256,512]{1,0:T(8,128)(2,1)S(1)}, bf16[256,512]{1,0:T(8,128)(2,1)S(1)}, u32[]{:S(2)}, u32[]{:S(2)}) collective-permute-start(bf16[256,512]{1,0:T(8,128)(2,1)S(1)} %turned_image.1.refs_3_), channel_id=1, source_target_pairs={{0,32},{16,48},{32,64},{48,80},{64,96},{80,112},{96,128},{112,144}... | collective-permute-start | bytes 786440 | tf_op jit(solution)/shard_map/ppermute | solution.py:34
  50.6 7.3 %collective-permute-start.10 = (bf16[768,128]{1,0:T(8,128)(2,1)S(1)}, bf16[768,128]{1,0:T(8,128)(2,1)S(1)}, u32[]{:S(2)}, u32[]{:S(2)}) collective-permute-start(bf16[768,128]{1,0:T(8,128)(2,1)S(1)} %pad_maximum_fusion.2), channel_id=1, source_target_pairs={{0,1},{1,0},{2,3},{3,2},{4,5},{5,4},{6,7},{7,6},{8,9},{9,8},{10,11... | collective-permute-start | bytes 589832 | tf_op jit(solution)/shard_map/ppermute | solution.py:50
  57.9 7.6 %collective-permute-start.11 = (bf16[8,16,128]{2,1,0:T(8,128)(2,1)S(1)}, bf16[8,16,128]{2,1,0:T(8,128)(2,1)S(1)}, u32[]{:S(2)}, u32[]{:S(2)}) collective-permute-start(bf16[8,16,128]{2,1,0:T(8,128)(2,1)S(1)} %constant_dynamic-update-slice_fusion), channel_id=1, source_target_pairs={{0,16},{16,0},{32,48},{48,32},{64,80},{80,64},{96,112},{112,96},{1... | collective-permute-start | bytes 98312 | tf_op jit(solution)/shard_map/ppermute | solution.py:46
  61.4 9.8 %collective-permute-start.17 = (bf16[256,512]{1,0:T(8,128)(2,1)S(1)}, bf16[256,512]{1,0:T(8,128)(2,1)S(1)}, u32[]{:S(2)}, u32[]{:S(2)}) collective-permute-start(bf16[256,512]{1,0:T(8,128)(2,1)S(1)} %collective-permute-done.16.refs_5_), channel_id=1, source_target_pairs={{0,224},{16,240},{32,0},{48,16},{64,32},{80,48},{96,64},{112,80},{... | collective-permute-start | bytes 786440 | tf_op jit(solution)/shard_map/ppermute | solution.py:34
  65.5 9.1 %collective-permute-start.13 = (bf16[256,512]{1,0:T(8,128)(2,1)S(1)}, bf16[256,512]{1,0:T(8,128)(2,1)S(1)}, u32[]{:S(2)}, u32[]{:S(2)}) collective-permute-start(bf16[256,512]{1,0:T(8,128)(2,1)S(1)} %collective-permute-done.12.refs_4_), channel_id=1, source_target_pairs={{0,32},{16,48},{32,64},{48,80},{64,96},{80,112},{96,128},{112,144}... | collective-permute-start | bytes 786440 | tf_op jit(solution)/shard_map/ppermute | solution.py:34
  71.2 8.2 %collective-permute-start.18 = (bf16[256,512]{1,0:T(8,128)(2,1)S(1)}, bf16[256,512]{1,0:T(8,128)(2,1)S(1)}, u32[]{:S(2)}, u32[]{:S(2)}) collective-permute-start(bf16[256,512]{1,0:T(8,128)(2,1)S(1)} %collective-permute-done.17.refs_5_), channel_id=1, source_target_pairs={{0,224},{16,240},{32,0},{48,16},{64,32},{80,48},{96,64},{112,80},{... | collective-permute-start | bytes 786440 | tf_op jit(solution)/shard_map/ppermute | solution.py:34
  74.6 8.3 %collective-permute-start.14 = (bf16[256,512]{1,0:T(8,128)(2,1)S(1)}, bf16[256,512]{1,0:T(8,128)(2,1)S(1)}, u32[]{:S(2)}, u32[]{:S(2)}) collective-permute-start(bf16[256,512]{1,0:T(8,128)(2,1)S(1)} %collective-permute-done.13.refs_4_), channel_id=1, source_target_pairs={{0,32},{16,48},{32,64},{48,80},{64,96},{80,112},{96,128},{112,144}... | collective-permute-start | bytes 786440 | tf_op jit(solution)/shard_map/ppermute | solution.py:34
  79.4 5.4 %collective-permute-start.19 = (bf16[128,512]{1,0:T(8,128)(2,1)S(1)}, bf16[128,512]{1,0:T(8,128)(2,1)S(1)}, u32[]{:S(2)}, u32[]{:S(2)}) collective-permute-start(bf16[128,512]{1,0:T(8,128)(2,1)S(1)} %slice.118), channel_id=1, source_target_pairs={{0,224},{16,240},{32,0},{48,16},{64,32},{80,48},{96,64},{112,80},{... | collective-permute-start | bytes 393224 | tf_op jit(solution)/shard_map/ppermute | solution.py:34
  82.9 5.1 %collective-permute-start.15 = (bf16[128,512]{1,0:T(8,128)(2,1)S(1)}, bf16[128,512]{1,0:T(8,128)(2,1)S(1)}, u32[]{:S(2)}, u32[]{:S(2)}) collective-permute-start(bf16[128,512]{1,0:T(8,128)(2,1)S(1)} %slice.117), channel_id=1, source_target_pairs={{0,32},{16,48},{32,64},{48,80},{64,96},{80,112},{96,128},{112,144}... | collective-permute-start | bytes 393224 | tf_op jit(solution)/shard_map/ppermute | solution.py:34
  89.8 4.8 %collective-permute-start.20 = (f32[4,256,128]{2,1,0:T(8,128)S(1)}, f32[4,256,128]{2,1,0:T(8,128)S(1)}, u32[]{:S(2)}, u32[]{:S(2)}) collective-permute-start(f32[4,256,128]{2,1,0:T(8,128)S(1)} %get-tuple-element.33), channel_id=1, source_target_pairs={{0,16},{16,0},{32,48},{48,32},{64,80},{80,64},{96,112},{112,96},{1... | collective-permute-start | bytes 1572872 | tf_op jit(solution)/shard_map/ppermute | solution.py:46
  93.0 3.3 %collective-permute-start.22 = (f32[4,256,128]{2,1,0:T(8,128)S(1)}, f32[4,256,128]{2,1,0:T(8,128)S(1)}, u32[]{:S(2)}, u32[]{:S(2)}) collective-permute-start(f32[4,256,128]{2,1,0:T(8,128)S(1)} %get-tuple-element.31), channel_id=1, source_target_pairs={{0,16},{16,0},{32,48},{48,32},{64,80},{80,64},{96,112},{112,96},{1... | collective-permute-start | bytes 1572872 | tf_op jit(solution)/shard_map/ppermute | solution.py:46
  94.7 8.0 %collective-permute-start.21 = (bf16[4,256,128]{2,1,0:T(8,128)(2,1)S(1)}, bf16[4,256,128]{2,1,0:T(8,128)(2,1)S(1)}, u32[]{:S(2)}, u32[]{:S(2)}) collective-permute-start(bf16[4,256,128]{2,1,0:T(8,128)(2,1)S(1)} %fusion.1), channel_id=1, source_target_pairs={{0,1},{1,0},{2,3},{3,2},{4,5},{5,4},{6,7},{7,6},{8,9},{9,8},{10,11... | collective-permute-start | bytes 786440 | tf_op jit(solution)/shard_map/ppermute | solution.py:50

commit v3 on v2

--- a/solution.py
+++ b/solution.py
@@ -268,11 +268,11 @@
     half = split_shift(half, 4, 4)
     middle = split_shift(piece(-2 * sign), -2, 2)
     near = split_shift(piece(-sign), -1, 1)
-    parts, far, middle = lax.optimization_barrier((parts, far, middle))
+    parts, near = lax.optimization_barrier((parts, near))
 
     share = jnp.sum(parts, axis=0).astype(BF16)[None]
     got = [share] + [y_shift(share, k) for k in range(1, 4)]
-    got[3], half, near = lax.optimization_barrier((got[3], half, near))
+    got[3], middle, far = lax.optimization_barrier((got[3], middle, far))
     got.append(x_swap(jnp.concatenate(got)))
     image = turned_image(place, got)
     image, near, middle, far, half = lax.optimization_barrier((image, near, middle, far, half))

time: 106 us -> 102 us (0.962); the launches traced: 104 us -> 101 us
  waiting for transfers between devices: 29.5 us -> 34.6 us
  starting transfers between devices: 52.3 us -> 47.5 us
  Pallas kernels: 19.3 us -> 16.2 us
    ppermute x4, waiting for transfers between devices: 2.51 us -> 8.32 us  [split_shift(): return lax.ppermute(value, ('tm', 'hank'), pairs)]
    all_to_all x1, waiting for transfers between devices: 0.01 us -> 4.13 us  [per_device(): lax.all_to_all(partial.reshape(NCHAN, SHARE, HALF_P), 'chan', 0, 0, tiled...]
    all_to_all x1, starting transfers between devices: 5.04 us -> 8.43 us  [per_device(): lax.all_to_all(partial.reshape(NCHAN, SHARE, HALF_P), 'chan', 0, 0, tiled...]
    ppermute x3, waiting for transfers between devices: 2.78 us -> 0.01 us  [y_shift(): lax.ppermute(value, 'chan', [(i, i & 4 | i + steps & 3) for i in range(NC...]
    ppermute x3, starting transfers between devices: 4.67 us -> 2.01 us  [hank_swap(): return lax.ppermute(value, 'hank', [(0, 1), (1, 0)])]
    ppermute x1, waiting for transfers between devices: 2.63 us -> 0.23 us  [x_swap(): return lax.ppermute(value, 'chan', [(i, i ^ 4) for i in range(NCHAN)])]
    ppermute x4, starting transfers between devices: 10.9 us -> 8.88 us  [split_shift(): return lax.ppermute(value, ('tm', 'hank'), pairs)]
    ppermute x3, starting transfers between devices: 4.64 us -> 2.82 us  [y_shift(): lax.ppermute(value, 'chan', [(i, i & 4 | i + steps & 3) for i in range(NC...]
  transfers between devices with their start and end apart: 24 -> 24, of which waited for: 11 -> 13; matrix products, arithmetic and copies ran while one was open for 1% -> 1% of each run, Pallas kernels for 11% -> 10%
where the time goes in v3:
time: 102 us; the launch traced here: 101 us
  starting transfers between devices  47.5 us (47%)
  waiting for transfers between devices  34.6 us (34%)
  Pallas kernels  16.2 us (16%)
  local copies, waits for them, and re-layouts  1.81 us (2%)
    ppermute x8, starting transfers between devices, z_shift(): lax.ppermute(value, 'tm', [(i, (i + 2 * steps) % 16) for i in range(16)])  12 us
    ppermute x3, waiting for transfers between devices, hank_swap(): return lax.ppermute(value, 'hank', [(0, 1), (1, 0)])  10.2 us
    ppermute x8, waiting for transfers between devices, z_shift(): lax.ppermute(value, 'tm', [(i, (i + 2 * steps) % 16) for i in range(16)])  10.1 us
    ppermute x4, starting transfers between devices, split_shift(): return lax.ppermute(value, ('tm', 'hank'), pairs)  8.88 us
    pallas_call x5, Pallas kernels, sketch_terms(): pl.pallas_call(functools.partial(sketch_kernel, count, starts, turn, firs...  8.52 us
    all_to_all x1, starting transfers between devices, per_device(): lax.all_to_all(partial.reshape(NCHAN, SHARE, HALF_P), 'chan', 0, 0, tiled...  8.43 us
    ppermute x4, waiting for transfers between devices, split_shift(): return lax.ppermute(value, ('tm', 'hank'), pairs)  8.32 us
    ppermute x3, starting transfers between devices, core_swap(): return lax.ppermute(value, 'tm', [(i, i ^ 1) for i in range(16)])  5.23 us
  transfers between devices with their start and end apart: 24, of which 13 were waited for; matrix products, arithmetic and copies ran while one was open for 1% of the time, Pallas kernels for 10%

profile of v3, /device:TPU:1, one launch (start us, length us, event | category | flops | bytes accessed | tf_op | source)
XLA Modules:
  0.0 101.4 jit_solution(8468485332731007118)
XLA Ops:
  0.0 0.8 slice.84
  0.8 4.9 %collective-permute-start = (bf16[16,1024]{1,0:T(8,128)(2,1)S(1)}, bf16[16,1024]{1,0:T(8,128)(2,1)S(1)}, u32[]{:S(2)}, u32[]{:S(2)}) collective-permute-start(bf16[16,1024]{1,0:T(8,128)(2,1)S(1)} %slice.84), channel_id=1, source_target_pairs={{0,16},{16,32},{32,48},{48,64},{64,80},{80,96},{96,112},{112,128},... | collective-permute-start | bytes 98312 | tf_op jit(solution)/shard_map/ppermute | solution.py:30
  6.4 0.6 copy-done.1
  7.1 1.4 %probe_signs.1.signs = bf16[8,2048,256]{2,1,0:T(8,128)(2,1)S(1)} custom-call(s32[3]{0:T(128)S(1)} %pad_add_fusion.place.refs_0_, s32[16]{0:T(128)S(1)} %copy-done.1, s32[1]{0:T(128)S(6)} %copy.13.seed), custom_call_target="tpu_custom_call" | custom-call | bytes 14680064 | tf_op jit(solution)/shard_map/probe_signs/pallas_call | solution.py:109
  8.6 2.4 %partial_images.1 = f32[512,256]{1,0:T(8,128)} custom-call(s32[3]{0:T(128)S(1)} %pad_add_fusion.place.refs_0_, s32[16]{0:T(128)S(1)} %copy-done.1, bf16[512,1024]{1,0:T(8,128)(2,1)S(1)} %copy-done, bf16[16,1024]{1,0:T(8,128)(2,1)S(1)} %collective-permute-done.behind, bf16[8,2048,256]{2,1,0:T(8,128)(2,1)S(1)} %probe_signs.1.signs), custom_call_target="tpu_custom_call" | custom-call | flops 4294967296 | bytes 2097152 | tf_op jit(solution)/shard_map/partial_images/pallas_call | solution.py:121
  11.0 8.4 %all-to-all-start = ((f32[8,64,256]{2,1,0:T(8,128)}), f32[8,64,256]{2,1,0:T(8,128)S(1)}, u32[]{:S(2)}, u32[]{:S(2)}) async-start(f32[8,64,256]{2,1,0:T(8,128)} %bitcast.4), calls=%async_computation | async-start | bytes 1048576 | tf_op jit(solution)/shard_map/all_to_all | solution.py:259
  19.4 0.1 constant_dynamic-slice_fusion.3
  19.6 2.8 %collective-permute-start.1 = (bf16[512,128]{1,0:T(8,128)(2,1)S(1)}, bf16[512,128]{1,0:T(8,128)(2,1)S(1)}, u32[]{:S(2)}, u32[]{:S(2)}) collective-permute-start(bf16[512,128]{1,0:T(8,128)(2,1)S(1)} %get-tuple-element.35), channel_id=1, source_target_pairs={{0,224},{1,33},{16,240},{17,49},{32,0},{33,65},{48,16},{49,81},{64... | collective-permute-start | bytes 393224 | tf_op jit(solution)/shard_map/ppermute | solution.py:42
  22.4 3.1 %collective-permute-start.5 = (bf16[512,128]{1,0:T(8,128)(2,1)S(1)}, bf16[512,128]{1,0:T(8,128)(2,1)S(1)}, u32[]{:S(2)}, u32[]{:S(2)}) collective-permute-start(bf16[512,128]{1,0:T(8,128)(2,1)S(1)} %get-tuple-element.34), channel_id=1, source_target_pairs={{0,192},{1,65},{16,208},{17,81},{32,224},{33,97},{48,240},{49,113}... | collective-permute-start | bytes 393224 | tf_op jit(solution)/shard_map/ppermute | solution.py:42
  25.5 4.1 %all-to-all-done = f32[8,64,256]{2,1,0:T(8,128)S(1)} async-done(((f32[8,64,256]{2,1,0:T(8,128)}), f32[8,64,256]{2,1,0:T(8,128)S(1)}, u32[]{:S(2)}, u32[]{:S(2)}) %all-to-all-start) | async-done | bytes 524320 | tf_op jit(solution)/shard_map/all_to_all | solution.py:259
  29.7 1.1 %collective-permute-start.4 = (bf16[1,64,256]{2,1,0:T(8,128)(2,1)S(1)}, bf16[1,64,256]{2,1,0:T(8,128)(2,1)S(1)}, u32[]{:S(2)}, u32[]{:S(2)}) collective-permute-start(bf16[1,64,256]{2,1,0:T(8,128)(2,1)S(1)} %bitcast.40), channel_id=1, source_target_pairs={{0,6},{2,0},{4,2},{6,4},{8,14},{10,8},{12,10},{14,12},{1,7},{3,1},... | collective-permute-start | bytes 98312 | tf_op jit(solution)/shard_map/ppermute | solution.py:54
  30.7 0.5 collective-permute-start.2
  31.2 1.3 %collective-permute-start.3 = (bf16[1,64,256]{2,1,0:T(8,128)(2,1)S(1)}, bf16[1,64,256]{2,1,0:T(8,128)(2,1)S(1)}, u32[]{:S(2)}, u32[]{:S(2)}) collective-permute-start(bf16[1,64,256]{2,1,0:T(8,128)(2,1)S(1)} %bitcast.42), channel_id=1, source_target_pairs={{0,4},{2,6},{4,0},{6,2},{8,12},{10,14},{12,8},{14,10},{1,5},{3,7},... | collective-permute-start | bytes 98312 | tf_op jit(solution)/shard_map/ppermute | solution.py:54
  32.5 5.0 %collective-permute-done.6.refs_2_ = bf16[512,128]{1,0:T(8,128)(2,1)S(1)} collective-permute-done((bf16[512,128]{1,0:T(8,128)(2,1)S(1)}, bf16[512,128]{1,0:T(8,128)(2,1)S(1)}, u32[]{:S(2)}, u32[]{:S(2)}) %collective-permute-start.6) | collective-permute-done | bytes 131104 | tf_op jit(solution)/shard_map/ppermute | solution.py:42
  37.5 3.2 %collective-permute-start.7 = (bf16[4,64,256]{2,1,0:T(8,128)(2,1)S(1)}, bf16[4,64,256]{2,1,0:T(8,128)(2,1)S(1)}, u32[]{:S(2)}, u32[]{:S(2)}) collective-permute-start(bf16[4,64,256]{2,1,0:T(8,128)(2,1)S(1)} %pad_maximum_fusion.3), channel_id=1, source_target_pairs={{0,8},{2,10},{4,12},{6,14},{8,0},{10,2},{12,4},{14,6},{1,9},{3,11}... | collective-permute-start | bytes 393224 | tf_op jit(solution)/shard_map/ppermute | solution.py:58
  40.7 0.1 dynamic_slice.20
  40.8 3.0 %collective-permute-start.8 = (bf16[256,128]{1,0:T(8,128)(2,1)S(1)}, bf16[256,128]{1,0:T(8,128)(2,1)S(1)}, u32[]{:S(2)}, u32[]{:S(2)}) collective-permute-start(bf16[256,128]{1,0:T(8,128)(2,1)S(1)} %dynamic_slice.20), channel_id=1, source_target_pairs={{0,128},{1,129},{16,144},{17,145},{32,160},{33,161},{48,176},{49,1... | collective-permute-start | bytes 196616 | tf_op jit(solution)/shard_map/ppermute | solution.py:42
  43.8 0.2 collective-permute-done.7.refs_4_
  44.0 0.7 turned_image.1.refs_3_
  44.7 3.3 %collective-permute-done.8.refs_2_ = bf16[256,128]{1,0:T(8,128)(2,1)S(1)} collective-permute-done((bf16[256,128]{1,0:T(8,128)(2,1)S(1)}, bf16[256,128]{1,0:T(8,128)(2,1)S(1)}, u32[]{:S(2)}, u32[]{:S(2)}) %collective-permute-start.8) | collective-permute-done | bytes 65568 | tf_op jit(solution)/shard_map/ppermute | solution.py:42
  48.2 1.3 %collective-permute-start.16 = (bf16[256,512]{1,0:T(8,128)(2,1)S(1)}, bf16[256,512]{1,0:T(8,128)(2,1)S(1)}, u32[]{:S(2)}, u32[]{:S(2)}) collective-permute-start(bf16[256,512]{1,0:T(8,128)(2,1)S(1)} %turned_image.1.refs_3_), channel_id=1, source_target_pairs={{0,224},{16,240},{32,0},{48,16},{64,32},{80,48},{96,64},{112,80},{... | collective-permute-start | bytes 786440 | tf_op jit(solution)/shard_map/ppermute | solution.py:34
  49.5 3.0 %collective-permute-start.12 = (bf16[256,512]{1,0:T(8,128)(2,1)S(1)}, bf16[256,512]{1,0:T(8,128)(2,1)S(1)}, u32[]{:S(2)}, u32[]{:S(2)}) collective-permute-start(bf16[256,512]{1,0:T(8,128)(2,1)S(1)} %turned_image.1.refs_3_), channel_id=1, source_target_pairs={{0,32},{16,48},{32,64},{48,80},{64,96},{80,112},{96,128},{112,144}... | collective-permute-start | bytes 786440 | tf_op jit(solution)/shard_map/ppermute | solution.py:34
  52.5 1.4 %collective-permute-start.10 = (bf16[768,128]{1,0:T(8,128)(2,1)S(1)}, bf16[768,128]{1,0:T(8,128)(2,1)S(1)}, u32[]{:S(2)}, u32[]{:S(2)}) collective-permute-start(bf16[768,128]{1,0:T(8,128)(2,1)S(1)} %pad_maximum_fusion.2), channel_id=1, source_target_pairs={{0,1},{1,0},{2,3},{3,2},{4,5},{5,4},{6,7},{7,6},{8,9},{9,8},{10,11... | collective-permute-start | bytes 589832 | tf_op jit(solution)/shard_map/ppermute | solution.py:50
  53.9 0.3 collective-permute-done.9.refs_3_
  54.2 4.6 %collective-permute-done.10.refs_3_ = bf16[768,128]{1,0:T(8,128)(2,1)S(1)} collective-permute-done((bf16[768,128]{1,0:T(8,128)(2,1)S(1)}, bf16[768,128]{1,0:T(8,128)(2,1)S(1)}, u32[]{:S(2)}, u32[]{:S(2)}) %collective-permute-start.10) | collective-permute-done | bytes 196640 | tf_op jit(solution)/shard_map/ppermute | solution.py:50
  58.8 2.4 %collective-permute-start.11 = (bf16[8,16,128]{2,1,0:T(8,128)(2,1)S(1)}, bf16[8,16,128]{2,1,0:T(8,128)(2,1)S(1)}, u32[]{:S(2)}, u32[]{:S(2)}) collective-permute-start(bf16[8,16,128]{2,1,0:T(8,128)(2,1)S(1)} %constant_dynamic-update-slice_fusion), channel_id=1, source_target_pairs={{0,16},{16,0},{32,48},{48,32},{64,80},{80,64},{96,112},{112,96},{1... | collective-permute-start | bytes 98312 | tf_op jit(solution)/shard_map/ppermute | solution.py:46
  61.3 1.3 %collective-permute-start.17 = (bf16[256,512]{1,0:T(8,128)(2,1)S(1)}, bf16[256,512]{1,0:T(8,128)(2,1)S(1)}, u32[]{:S(2)}, u32[]{:S(2)}) collective-permute-start(bf16[256,512]{1,0:T(8,128)(2,1)S(1)} %collective-permute-done.16.refs_5_), channel_id=1, source_target_pairs={{0,224},{16,240},{32,0},{48,16},{64,32},{80,48},{96,64},{112,80},{... | collective-permute-start | bytes 786440 | tf_op jit(solution)/shard_map/ppermute | solution.py:34
  62.6 3.2 %collective-permute-start.13 = (bf16[256,512]{1,0:T(8,128)(2,1)S(1)}, bf16[256,512]{1,0:T(8,128)(2,1)S(1)}, u32[]{:S(2)}, u32[]{:S(2)}) collective-permute-start(bf16[256,512]{1,0:T(8,128)(2,1)S(1)} %collective-permute-done.12.refs_4_), channel_id=1, source_target_pairs={{0,32},{16,48},{32,64},{48,80},{64,96},{80,112},{96,128},{112,144}... | collective-permute-start | bytes 786440 | tf_op jit(solution)/shard_map/ppermute | solution.py:34
  65.9 1.3 %sketch_terms.5.refs_6_ = f32[256,2048]{1,0:T(8,128)S(1)} custom-call(s32[3]{0:T(128)S(1)} %pad_add_fusion.place.refs_0_, bf16[1,16,128]{2,1,0:T(8,128)(2,1)S(1)} %get-tuple-element.36.refs_1_, bf16[512,128]{1,0:T(8,128)(2,1)S(1)} %get-tuple-element.32.refs_2_, bf16[256,512]{1,0:T(8,128)(2,1)S(1)} %turned_image.1.refs_3_), custom_call_target="tpu_custom_call" | custom-call | flops 1073741824 | bytes 2097152 | tf_op jit(solution)/shard_map/sketch_terms/pallas_call | solution.py:202
  67.2 1.9 %sketch_terms.6.refs_6_ = f32[256,2048]{1,0:T(8,128)S(1)} custom-call(s32[3]{0:T(128)S(1)} %pad_add_fusion.place.refs_0_, bf16[2,16,128]{2,1,0:T(8,128)(2,1)S(1)} %pad_maximum_fusion.6.refs_1_, bf16[512,128]{1,0:T(8,128)(2,1)S(1)} %collective-permute-done.1.refs_2_, bf16[1024,128]{1,0:T(8,128)(2,1)S(1)} %collective-permute-done.9.refs_3_, ...), custom_call_target="tpu_custom_call" | custom-call | flops 2147483648 | bytes 2097152 | tf_op jit(solution)/shard_map/sketch_terms/pallas_call | solution.py:202
  69.0 3.1 %collective-permute-done.17.refs_5_ = bf16[256,512]{1,0:T(8,128)(2,1)S(1)} collective-permute-done((bf16[256,512]{1,0:T(8,128)(2,1)S(1)}, bf16[256,512]{1,0:T(8,128)(2,1)S(1)}, u32[]{:S(2)}, u32[]{:S(2)}) %collective-permute-start.17) | collective-permute-done | bytes 262176 | tf_op jit(solution)/shard_map/ppermute | solution.py:34
  72.1 1.5 %collective-permute-start.14 = (bf16[256,512]{1,0:T(8,128)(2,1)S(1)}, bf16[256,512]{1,0:T(8,128)(2,1)S(1)}, u32[]{:S(2)}, u32[]{:S(2)}) collective-permute-start(bf16[256,512]{1,0:T(8,128)(2,1)S(1)} %collective-permute-done.13.refs_4_), channel_id=1, source_target_pairs={{0,32},{16,48},{32,64},{48,80},{64,96},{80,112},{96,128},{112,144}... | collective-permute-start | bytes 786440 | tf_op jit(solution)/shard_map/ppermute | solution.py:34
  73.7 1.9 %sketch_terms.7.refs_6_ = f32[256,2048]{1,0:T(8,128)S(1)} custom-call(s32[3]{0:T(128)S(1)} %pad_add_fusion.place.refs_0_, bf16[2,16,128]{2,1,0:T(8,128)(2,1)S(1)} %pad_maximum_fusion.5.refs_1_, bf16[512,128]{1,0:T(8,128)(2,1)S(1)} %collective-permute-done.5.refs_2_, bf16[1024,128]{1,0:T(8,128)(2,1)S(1)} %collective-permute-done.9.refs_3_, ...), custom_call_target="tpu_custom_call" | custom-call | flops 2147483648 | bytes 2097152 | tf_op jit(solution)/shard_map/sketch_terms/pallas_call | solution.py:202
  75.5 3.8 %collective-permute-done.18.refs_5_ = bf16[256,512]{1,0:T(8,128)(2,1)S(1)} collective-permute-done((bf16[256,512]{1,0:T(8,128)(2,1)S(1)}, bf16[256,512]{1,0:T(8,128)(2,1)S(1)}, u32[]{:S(2)}, u32[]{:S(2)}) %collective-permute-start.18) | collective-permute-done | bytes 262176 | tf_op jit(solution)/shard_map/ppermute | solution.py:34
  79.4 1.6 %collective-permute-start.19 = (bf16[128,512]{1,0:T(8,128)(2,1)S(1)}, bf16[128,512]{1,0:T(8,128)(2,1)S(1)}, u32[]{:S(2)}, u32[]{:S(2)}) collective-permute-start(bf16[128,512]{1,0:T(8,128)(2,1)S(1)} %slice.118), channel_id=1, source_target_pairs={{0,224},{16,240},{32,0},{48,16},{64,32},{80,48},{96,64},{112,80},{... | collective-permute-start | bytes 393224 | tf_op jit(solution)/shard_map/ppermute | solution.py:34
  81.1 1.8 %sketch_terms.8.refs_5_ = f32[256,2048]{1,0:T(8,128)S(1)} custom-call(s32[3]{0:T(128)S(1)} %pad_add_fusion.place.refs_0_, bf16[2,16,128]{2,1,0:T(8,128)(2,1)S(1)} %pad_maximum_fusion.4.refs_1_, bf16[512,128]{1,0:T(8,128)(2,1)S(1)} %collective-permute-done.6.refs_2_, bf16[768,128]{1,0:T(8,128)(2,1)S(1)} %collective-permute-done.10.refs_3_, ...), custom_call_target="tpu_custom_call" | custom-call | flops 2147483648 | bytes 2097152 | tf_op jit(solution)/shard_map/sketch_terms/pallas_call | solution.py:202
  82.9 0.4 collective-permute-done.19
  83.3 2.8 %collective-permute-done.15 = bf16[128,512]{1,0:T(8,128)(2,1)S(1)} collective-permute-done((bf16[128,512]{1,0:T(8,128)(2,1)S(1)}, bf16[128,512]{1,0:T(8,128)(2,1)S(1)}, u32[]{:S(2)}, u32[]{:S(2)}) %collective-permute-start.15) | collective-permute-done | bytes 131104 | tf_op jit(solution)/shard_map/ppermute | solution.py:34
  86.1 1.7 %sketch_terms.9 = f32[2,2,4,256,128]{4,3,2,1,0:T(8,128)S(1)} custom-call(s32[3]{0:T(128)S(1)} %pad_add_fusion.place.refs_0_, bf16[1,16,128]{2,1,0:T(8,128)(2,1)S(1)} %get-tuple-element.43.refs_1_, bf16[256,128]{1,0:T(8,128)(2,1)S(1)} %collective-permute-done.8.refs_2_, bf16[768,128]{1,0:T(8,128)(2,1)S(1)} %collective-permute-done.10.refs_3_, ...), custom_call_target="tpu_custom_call" | custom-call | flops 1073741824 | bytes 2097152 | tf_op jit(solution)/shard_map/sketch_terms/pallas_call | solution.py:202
  87.8 0.1 slice_bitcast_fusion
  87.9 2.7 %collective-permute-start.20 = (f32[4,256,128]{2,1,0:T(8,128)S(1)}, f32[4,256,128]{2,1,0:T(8,128)S(1)}, u32[]{:S(2)}, u32[]{:S(2)}) collective-permute-start(f32[4,256,128]{2,1,0:T(8,128)S(1)} %get-tuple-element.31), channel_id=1, source_target_pairs={{0,16},{16,0},{32,48},{48,32},{64,80},{80,64},{96,112},{112,96},{1... | collective-permute-start | bytes 1572872 | tf_op jit(solution)/shard_map/ppermute | solution.py:46
  90.6 0.1 collective-permute-start.22
  90.7 1.4 %collective-permute-done.20 = f32[4,256,128]{2,1,0:T(8,128)S(1)} collective-permute-done((f32[4,256,128]{2,1,0:T(8,128)S(1)}, f32[4,256,128]{2,1,0:T(8,128)S(1)}, u32[]{:S(2)}, u32[]{:S(2)}) %collective-permute-start.20) | collective-permute-done | bytes 524320 | tf_op jit(solution)/shard_map/ppermute | solution.py:46
  92.2 0.6 collective-permute-start.21
  92.8 0.1 collective-permute-done.22.refs_1_
  92.9 1.6 %final_sketch.2.refs_1_ = f32[64,8,512]{2,1,0:T(8,128)} custom-call(s32[3]{0:T(128)S(1)} %pad_add_fusion.place.refs_0_, f32[4,256,128]{2,1,0:T(8,128)S(1)} %get-tuple-element.30.refs_0_, f32[4,256,128]{2,1,0:T(8,128)S(1)} %collective-permute-done.22.refs_1_), custom_call_target="tpu_custom_call" | custom-call | tf_op jit(solution)/shard_map/final_sketch/pallas_call | solution.py:235
  94.5 5.4 %collective-permute-done.21.refs_0_ = bf16[4,256,128]{2,1,0:T(8,128)(2,1)S(1)} collective-permute-done((bf16[4,256,128]{2,1,0:T(8,128)(2,1)S(1)}, bf16[4,256,128]{2,1,0:T(8,128)(2,1)S(1)}, u32[]{:S(2)}, u32[]{:S(2)}) %collective-permute-start.21) | collective-permute-done | bytes 262176 | tf_op jit(solution)/shard_map/ppermute | solution.py:50
  99.8 1.6 %final_sketch.3 = f32[64,8,512]{2,1,0:T(8,128)} custom-call(s32[3]{0:T(128)S(1)} %pad_add_fusion.place.refs_0_, bf16[4,256,128]{2,1,0:T(8,128)(2,1)S(1)} %collective-permute-done.21.refs_0_, f32[64,8,512]{2,1,0:T(8,128)} %final_sketch.2.refs_1_), custom_call_target="tpu_custom_call", output_to_operand_aliasing={{}: (2, {})} | custom-call | tf_op jit(solution)/shard_map/final_sketch/pallas_call | solution.py:235
  (43 shorter events, 0.7 us)
Async XLA Ops:
  0.8 7.8 %collective-permute-start = (bf16[16,1024]{1,0:T(8,128)(2,1)S(1)}, bf16[16,1024]{1,0:T(8,128)(2,1)S(1)}, u32[]{:S(2)}, u32[]{:S(2)}) collective-permute-start(bf16[16,1024]{1,0:T(8,128)(2,1)S(1)} %slice.84), channel_id=1, source_target_pairs={{0,16},{16,32},{32,48},{48,64},{64,80},{80,96},{96,112},{112,128},... | collective-permute-start | bytes 98312 | tf_op jit(solution)/shard_map/ppermute | solution.py:30
  6.4 0.7 copy-start.1
  7.1 1.5 %copy-start = (bf16[512,1024]{1,0:T(8,128)(2,1)S(1)}, bf16[512,1024]{1,0:T(8,128)(2,1)}, u32[]{:S(2)}) copy-start(bf16[512,1024]{1,0:T(8,128)(2,1)} %records.1) | copy-start | bytes 3145732
  11.0 18.6 %all-to-all-start = ((f32[8,64,256]{2,1,0:T(8,128)}), f32[8,64,256]{2,1,0:T(8,128)S(1)}, u32[]{:S(2)}, u32[]{:S(2)}) async-start(f32[8,64,256]{2,1,0:T(8,128)} %bitcast.4), calls=%async_computation | async-start | bytes 1048576 | tf_op jit(solution)/shard_map/all_to_all | solution.py:259
  19.6 5.9 %collective-permute-start.1 = (bf16[512,128]{1,0:T(8,128)(2,1)S(1)}, bf16[512,128]{1,0:T(8,128)(2,1)S(1)}, u32[]{:S(2)}, u32[]{:S(2)}) collective-permute-start(bf16[512,128]{1,0:T(8,128)(2,1)S(1)} %get-tuple-element.35), channel_id=1, source_target_pairs={{0,224},{1,33},{16,240},{17,49},{32,0},{33,65},{48,16},{49,81},{64... | collective-permute-start | bytes 393224 | tf_op jit(solution)/shard_map/ppermute | solution.py:42
  22.4 10.1 %collective-permute-start.5 = (bf16[512,128]{1,0:T(8,128)(2,1)S(1)}, bf16[512,128]{1,0:T(8,128)(2,1)S(1)}, u32[]{:S(2)}, u32[]{:S(2)}) collective-permute-start(bf16[512,128]{1,0:T(8,128)(2,1)S(1)} %get-tuple-element.34), channel_id=1, source_target_pairs={{0,192},{1,65},{16,208},{17,81},{32,224},{33,97},{48,240},{49,113}... | collective-permute-start | bytes 393224 | tf_op jit(solution)/shard_map/ppermute | solution.py:42
  25.5 12.0 %collective-permute-start.6 = (bf16[512,128]{1,0:T(8,128)(2,1)S(1)}, bf16[512,128]{1,0:T(8,128)(2,1)S(1)}, u32[]{:S(2)}, u32[]{:S(2)}) collective-permute-start(bf16[512,128]{1,0:T(8,128)(2,1)S(1)} %get-tuple-element.33), channel_id=1, source_target_pairs={{0,96},{1,161},{16,112},{17,177},{32,128},{33,193},{48,144},{49,20... | collective-permute-start | bytes 393224 | tf_op jit(solution)/shard_map/ppermute | solution.py:42
  29.7 7.8 %collective-permute-start.4 = (bf16[1,64,256]{2,1,0:T(8,128)(2,1)S(1)}, bf16[1,64,256]{2,1,0:T(8,128)(2,1)S(1)}, u32[]{:S(2)}, u32[]{:S(2)}) collective-permute-start(bf16[1,64,256]{2,1,0:T(8,128)(2,1)S(1)} %bitcast.40), channel_id=1, source_target_pairs={{0,6},{2,0},{4,2},{6,4},{8,14},{10,8},{12,10},{14,12},{1,7},{3,1},... | collective-permute-start | bytes 98312 | tf_op jit(solution)/shard_map/ppermute | solution.py:54
  30.7 6.8 %collective-permute-start.2 = (bf16[1,64,256]{2,1,0:T(8,128)(2,1)S(1)}, bf16[1,64,256]{2,1,0:T(8,128)(2,1)S(1)}, u32[]{:S(2)}, u32[]{:S(2)}) collective-permute-start(bf16[1,64,256]{2,1,0:T(8,128)(2,1)S(1)} %bitcast.41), channel_id=1, source_target_pairs={{0,2},{2,4},{4,6},{6,0},{8,10},{10,12},{12,14},{14,8},{1,3},{3,5},... | collective-permute-start | bytes 98312 | tf_op jit(solution)/shard_map/ppermute | solution.py:54
  31.2 6.3 %collective-permute-start.3 = (bf16[1,64,256]{2,1,0:T(8,128)(2,1)S(1)}, bf16[1,64,256]{2,1,0:T(8,128)(2,1)S(1)}, u32[]{:S(2)}, u32[]{:S(2)}) collective-permute-start(bf16[1,64,256]{2,1,0:T(8,128)(2,1)S(1)} %bitcast.42), channel_id=1, source_target_pairs={{0,4},{2,6},{4,0},{6,2},{8,12},{10,14},{12,8},{14,10},{1,5},{3,7},... | collective-permute-start | bytes 98312 | tf_op jit(solution)/shard_map/ppermute | solution.py:54
  37.5 6.5 %collective-permute-start.7 = (bf16[4,64,256]{2,1,0:T(8,128)(2,1)S(1)}, bf16[4,64,256]{2,1,0:T(8,128)(2,1)S(1)}, u32[]{:S(2)}, u32[]{:S(2)}) collective-permute-start(bf16[4,64,256]{2,1,0:T(8,128)(2,1)S(1)} %pad_maximum_fusion.3), channel_id=1, source_target_pairs={{0,8},{2,10},{4,12},{6,14},{8,0},{10,2},{12,4},{14,6},{1,9},{3,11}... | collective-permute-start | bytes 393224 | tf_op jit(solution)/shard_map/ppermute | solution.py:58
  40.8 7.2 %collective-permute-start.8 = (bf16[256,128]{1,0:T(8,128)(2,1)S(1)}, bf16[256,128]{1,0:T(8,128)(2,1)S(1)}, u32[]{:S(2)}, u32[]{:S(2)}) collective-permute-start(bf16[256,128]{1,0:T(8,128)(2,1)S(1)} %dynamic_slice.20), channel_id=1, source_target_pairs={{0,128},{1,129},{16,144},{17,145},{32,160},{33,161},{48,176},{49,1... | collective-permute-start | bytes 196616 | tf_op jit(solution)/shard_map/ppermute | solution.py:42
  48.1 6.1 %collective-permute-start.9 = (bf16[1024,128]{1,0:T(8,128)(2,1)S(1)}, bf16[1024,128]{1,0:T(8,128)(2,1)S(1)}, u32[]{:S(2)}, u32[]{:S(2)}) collective-permute-start(bf16[1024,128]{1,0:T(8,128)(2,1)S(1)} %pad_maximum_fusion), channel_id=1, source_target_pairs={{0,1},{1,0},{2,3},{3,2},{4,5},{5,4},{6,7},{7,6},{8,9},{9,8},{10,11... | collective-permute-start | bytes 786440 | tf_op jit(solution)/shard_map/ppermute | solution.py:50
  48.2 13.1 %collective-permute-start.16 = (bf16[256,512]{1,0:T(8,128)(2,1)S(1)}, bf16[256,512]{1,0:T(8,128)(2,1)S(1)}, u32[]{:S(2)}, u32[]{:S(2)}) collective-permute-start(bf16[256,512]{1,0:T(8,128)(2,1)S(1)} %turned_image.1.refs_3_), channel_id=1, source_target_pairs={{0,224},{16,240},{32,0},{48,16},{64,32},{80,48},{96,64},{112,80},{... | collective-permute-start | bytes 786440 | tf_op jit(solution)/shard_map/ppermute | solution.py:34
  49.5 13.0 %collective-permute-start.12 = (bf16[256,512]{1,0:T(8,128)(2,1)S(1)}, bf16[256,512]{1,0:T(8,128)(2,1)S(1)}, u32[]{:S(2)}, u32[]{:S(2)}) collective-permute-start(bf16[256,512]{1,0:T(8,128)(2,1)S(1)} %turned_image.1.refs_3_), channel_id=1, source_target_pairs={{0,32},{16,48},{32,64},{48,80},{64,96},{80,112},{96,128},{112,144}... | collective-permute-start | bytes 786440 | tf_op jit(solution)/shard_map/ppermute | solution.py:34
  52.5 6.2 %collective-permute-start.10 = (bf16[768,128]{1,0:T(8,128)(2,1)S(1)}, bf16[768,128]{1,0:T(8,128)(2,1)S(1)}, u32[]{:S(2)}, u32[]{:S(2)}) collective-permute-start(bf16[768,128]{1,0:T(8,128)(2,1)S(1)} %pad_maximum_fusion.2), channel_id=1, source_target_pairs={{0,1},{1,0},{2,3},{3,2},{4,5},{5,4},{6,7},{7,6},{8,9},{9,8},{10,11... | collective-permute-start | bytes 589832 | tf_op jit(solution)/shard_map/ppermute | solution.py:50
  58.8 6.9 %collective-permute-start.11 = (bf16[8,16,128]{2,1,0:T(8,128)(2,1)S(1)}, bf16[8,16,128]{2,1,0:T(8,128)(2,1)S(1)}, u32[]{:S(2)}, u32[]{:S(2)}) collective-permute-start(bf16[8,16,128]{2,1,0:T(8,128)(2,1)S(1)} %constant_dynamic-update-slice_fusion), channel_id=1, source_target_pairs={{0,16},{16,0},{32,48},{48,32},{64,80},{80,64},{96,112},{112,96},{1... | collective-permute-start | bytes 98312 | tf_op jit(solution)/shard_map/ppermute | solution.py:46
  61.3 10.9 %collective-permute-start.17 = (bf16[256,512]{1,0:T(8,128)(2,1)S(1)}, bf16[256,512]{1,0:T(8,128)(2,1)S(1)}, u32[]{:S(2)}, u32[]{:S(2)}) collective-permute-start(bf16[256,512]{1,0:T(8,128)(2,1)S(1)} %collective-permute-done.16.refs_5_), channel_id=1, source_target_pairs={{0,224},{16,240},{32,0},{48,16},{64,32},{80,48},{96,64},{112,80},{... | collective-permute-start | bytes 786440 | tf_op jit(solution)/shard_map/ppermute | solution.py:34
  62.6 9.6 %collective-permute-start.13 = (bf16[256,512]{1,0:T(8,128)(2,1)S(1)}, bf16[256,512]{1,0:T(8,128)(2,1)S(1)}, u32[]{:S(2)}, u32[]{:S(2)}) collective-permute-start(bf16[256,512]{1,0:T(8,128)(2,1)S(1)} %collective-permute-done.12.refs_4_), channel_id=1, source_target_pairs={{0,32},{16,48},{32,64},{48,80},{64,96},{80,112},{96,128},{112,144}... | collective-permute-start | bytes 786440 | tf_op jit(solution)/shard_map/ppermute | solution.py:34
  72.1 7.3 %collective-permute-start.18 = (bf16[256,512]{1,0:T(8,128)(2,1)S(1)}, bf16[256,512]{1,0:T(8,128)(2,1)S(1)}, u32[]{:S(2)}, u32[]{:S(2)}) collective-permute-start(bf16[256,512]{1,0:T(8,128)(2,1)S(1)} %collective-permute-done.17.refs_5_), channel_id=1, source_target_pairs={{0,224},{16,240},{32,0},{48,16},{64,32},{80,48},{96,64},{112,80},{... | collective-permute-start | bytes 786440 | tf_op jit(solution)/shard_map/ppermute | solution.py:34
  72.1 8.8 %collective-permute-start.14 = (bf16[256,512]{1,0:T(8,128)(2,1)S(1)}, bf16[256,512]{1,0:T(8,128)(2,1)S(1)}, u32[]{:S(2)}, u32[]{:S(2)}) collective-permute-start(bf16[256,512]{1,0:T(8,128)(2,1)S(1)} %collective-permute-done.13.refs_4_), channel_id=1, source_target_pairs={{0,32},{16,48},{32,64},{48,80},{64,96},{80,112},{96,128},{112,144}... | collective-permute-start | bytes 786440 | tf_op jit(solution)/shard_map/ppermute | solution.py:34
  79.4 3.9 %collective-permute-start.19 = (bf16[128,512]{1,0:T(8,128)(2,1)S(1)}, bf16[128,512]{1,0:T(8,128)(2,1)S(1)}, u32[]{:S(2)}, u32[]{:S(2)}) collective-permute-start(bf16[128,512]{1,0:T(8,128)(2,1)S(1)} %slice.118), channel_id=1, source_target_pairs={{0,224},{16,240},{32,0},{48,16},{64,32},{80,48},{96,64},{112,80},{... | collective-permute-start | bytes 393224 | tf_op jit(solution)/shard_map/ppermute | solution.py:34
  81.0 5.1 %collective-permute-start.15 = (bf16[128,512]{1,0:T(8,128)(2,1)S(1)}, bf16[128,512]{1,0:T(8,128)(2,1)S(1)}, u32[]{:S(2)}, u32[]{:S(2)}) collective-permute-start(bf16[128,512]{1,0:T(8,128)(2,1)S(1)} %slice.117), channel_id=1, source_target_pairs={{0,32},{16,48},{32,64},{48,80},{64,96},{80,112},{96,128},{112,144}... | collective-permute-start | bytes 393224 | tf_op jit(solution)/shard_map/ppermute | solution.py:34
  87.9 4.2 %collective-permute-start.20 = (f32[4,256,128]{2,1,0:T(8,128)S(1)}, f32[4,256,128]{2,1,0:T(8,128)S(1)}, u32[]{:S(2)}, u32[]{:S(2)}) collective-permute-start(f32[4,256,128]{2,1,0:T(8,128)S(1)} %get-tuple-element.31), channel_id=1, source_target_pairs={{0,16},{16,0},{32,48},{48,32},{64,80},{80,64},{96,112},{112,96},{1... | collective-permute-start | bytes 1572872 | tf_op jit(solution)/shard_map/ppermute | solution.py:46
  90.6 2.3 %collective-permute-start.22 = (f32[4,256,128]{2,1,0:T(8,128)S(1)}, f32[4,256,128]{2,1,0:T(8,128)S(1)}, u32[]{:S(2)}, u32[]{:S(2)}) collective-permute-start(f32[4,256,128]{2,1,0:T(8,128)S(1)} %get-tuple-element.29), channel_id=1, source_target_pairs={{0,16},{16,0},{32,48},{48,32},{64,80},{80,64},{96,112},{112,96},{1... | collective-permute-start | bytes 1572872 | tf_op jit(solution)/shard_map/ppermute | solution.py:46
  92.2 7.6 %collective-permute-start.21 = (bf16[4,256,128]{2,1,0:T(8,128)(2,1)S(1)}, bf16[4,256,128]{2,1,0:T(8,128)(2,1)S(1)}, u32[]{:S(2)}, u32[]{:S(2)}) collective-permute-start(bf16[4,256,128]{2,1,0:T(8,128)(2,1)S(1)} %fusion.1), channel_id=1, source_target_pairs={{0,1},{1,0},{2,3},{3,2},{4,5},{5,4},{6,7},{7,6},{8,9},{9,8},{10,11... | collective-permute-start | bytes 786440 | tf_op jit(solution)/shard_map/ppermute | solution.py:50

commit v4 on v3

--- a/solution.py
+++ b/solution.py
@@ -50,12 +50,8 @@
     return lax.ppermute(value, "hank", [(0, 1), (1, 0)])
 
 
-def y_shift(value, steps):
-    return lax.ppermute(value, "chan", [(i, (i & 4) | ((i + steps) & 3)) for i in range(NCHAN)])
-
-
-def x_swap(value):
-    return lax.ppermute(value, "chan", [(i, i ^ 4) for i in range(NCHAN)])
+def chan_xor(value, bit):
+    return lax.ppermute(value, "chan", [(i, i ^ bit) for i in range(NCHAN)])
 
 
 def signs_kernel(place, blocks, seed, signs):
@@ -135,7 +131,7 @@
     at = 0
     for ref in refs[:-2]:
         for entry in range(ref.shape[0]):
-            k = ((place[0] & 4) ^ (at & 4)) | ((place[0] - at) & 3)
+            k = place[0] ^ at
             staged[pl.ds(pl.multiple_of(k * SHARE, SHARE), SHARE), :] = ref[entry].astype(F32)
             at += 1
     out[...] = staged[...].T.astype(BF16)
@@ -271,9 +267,11 @@
     parts, near = lax.optimization_barrier((parts, near))
 
     share = jnp.sum(parts, axis=0).astype(BF16)[None]
-    got = [share] + [y_shift(share, k) for k in range(1, 4)]
-    got[3], middle, far = lax.optimization_barrier((got[3], middle, far))
-    got.append(x_swap(jnp.concatenate(got)))
+    got = [share, chan_xor(share, 1)]
+    got[1], middle, far = lax.optimization_barrier((got[1], middle, far))
+    got.append(chan_xor(jnp.concatenate(got), 2))
+    got[2], half = lax.optimization_barrier((got[2], half))
+    got.append(chan_xor(jnp.concatenate(got), 4))
     image = turned_image(place, got)
     image, near, middle, far, half = lax.optimization_barrier((image, near, middle, far, half))
     other_first = hank_swap(jnp.concatenate([near, middle]))

time: 102 us -> 105 us (1.029); the launches traced: 101 us -> 106 us
  waiting for transfers between devices: 34.6 us -> 36.9 us
  Pallas kernels: 16.2 us -> 17.8 us
    ppermute x8, starting transfers between devices: 12 us -> 6.44 us  [z_shift(): lax.ppermute(value, 'tm', [(i, (i + 2 * steps) % 16) for i in range(16)])]
    ppermute x4, waiting for transfers between devices: 8.32 us -> 3.36 us  [split_shift(): return lax.ppermute(value, ('tm', 'hank'), pairs)]
    ppermute x4 -> x3, waiting for transfers between devices: 0.23 us -> 4.42 us  [chan_xor(): return lax.ppermute(value, 'chan', [(i, i ^ bit) for i in range(NCHAN)])]
    ppermute x4, starting transfers between devices: 8.88 us -> 12.9 us  [split_shift(): return lax.ppermute(value, ('tm', 'hank'), pairs)]
    ppermute x3, starting transfers between devices: 5.23 us -> 6.87 us  [core_swap(): return lax.ppermute(value, 'tm', [(i, i ^ 1) for i in range(16)])]
    ppermute x3, waiting for transfers between devices: 10.2 us -> 11.5 us  [hank_swap(): return lax.ppermute(value, 'hank', [(0, 1), (1, 0)])]
    ppermute x8, waiting for transfers between devices: 10.1 us -> 11.4 us  [z_shift(): lax.ppermute(value, 'tm', [(i, (i + 2 * steps) % 16) for i in range(16)])]
    ppermute x4 -> x3, starting transfers between devices: 6.01 us -> 5.79 us  [chan_xor(): return lax.ppermute(value, 'chan', [(i, i ^ bit) for i in range(NCHAN)])]
  transfers between devices with their start and end apart: 24 -> 23, of which waited for: 13 -> 14; matrix products, arithmetic and copies ran while one was open for 1% -> 1% of each run, Pallas kernels for 10% -> 10%
where the time goes in v4:
time: 105 us; the launch traced here: 106 us
  starting transfers between devices  48 us (46%)
  waiting for transfers between devices  36.9 us (35%)
  Pallas kernels  17.8 us (17%)
  local copies, waits for them, and re-layouts  1.81 us (2%)
    ppermute x4, starting transfers between devices, split_shift(): return lax.ppermute(value, ('tm', 'hank'), pairs)  12.9 us
    ppermute x3, waiting for transfers between devices, hank_swap(): return lax.ppermute(value, 'hank', [(0, 1), (1, 0)])  11.5 us
    ppermute x8, waiting for transfers between devices, z_shift(): lax.ppermute(value, 'tm', [(i, (i + 2 * steps) % 16) for i in range(16)])  11.4 us
    all_to_all x1, starting transfers between devices, per_device(): lax.all_to_all(partial.reshape(NCHAN, SHARE, HALF_P), 'chan', 0, 0, tiled...  9.42 us
    pallas_call x5, Pallas kernels, sketch_terms(): pl.pallas_call(functools.partial(sketch_kernel, count, starts, turn, firs...  8.6 us
    ppermute x3, starting transfers between devices, core_swap(): return lax.ppermute(value, 'tm', [(i, i ^ 1) for i in range(16)])  6.87 us
    ppermute x8, starting transfers between devices, z_shift(): lax.ppermute(value, 'tm', [(i, (i + 2 * steps) % 16) for i in range(16)])  6.44 us
    ppermute x3, starting transfers between devices, chan_xor(): return lax.ppermute(value, 'chan', [(i, i ^ bit) for i in range(NCHAN)])  5.79 us
  transfers between devices with their start and end apart: 23, of which 14 were waited for; matrix products, arithmetic and copies ran while one was open for 1% of the time, Pallas kernels for 10%

profile of v4, /device:TPU:1, one launch (start us, length us, event | category | flops | bytes accessed | tf_op | source)
XLA Modules:
  0.0 105.8 jit_solution(12779683427159915734)
XLA Ops:
  0.0 0.8 slice.84
  0.8 4.9 %collective-permute-start = (bf16[16,1024]{1,0:T(8,128)(2,1)S(1)}, bf16[16,1024]{1,0:T(8,128)(2,1)S(1)}, u32[]{:S(2)}, u32[]{:S(2)}) collective-permute-start(bf16[16,1024]{1,0:T(8,128)(2,1)S(1)} %slice.84), channel_id=1, source_target_pairs={{0,16},{16,32},{32,48},{48,64},{64,80},{80,96},{96,112},{112,128},... | collective-permute-start | bytes 98312 | tf_op jit(solution)/shard_map/ppermute | solution.py:30
  6.4 0.6 copy-done.1
  7.1 2.1 %probe_signs.1.signs = bf16[8,2048,256]{2,1,0:T(8,128)(2,1)S(1)} custom-call(s32[3]{0:T(128)S(1)} %pad_add_fusion.place.refs_0_, s32[16]{0:T(128)S(1)} %copy-done.1, s32[1]{0:T(128)S(6)} %copy.13.seed), custom_call_target="tpu_custom_call" | custom-call | bytes 14680064 | tf_op jit(solution)/shard_map/probe_signs/pallas_call | solution.py:105
  9.2 3.3 %partial_images.1 = f32[512,256]{1,0:T(8,128)} custom-call(s32[3]{0:T(128)S(1)} %pad_add_fusion.place.refs_0_, s32[16]{0:T(128)S(1)} %copy-done.1, bf16[512,1024]{1,0:T(8,128)(2,1)S(1)} %copy-done, bf16[16,1024]{1,0:T(8,128)(2,1)S(1)} %collective-permute-done.behind, bf16[8,2048,256]{2,1,0:T(8,128)(2,1)S(1)} %probe_signs.1.signs), custom_call_target="tpu_custom_call" | custom-call | flops 4294967296 | bytes 2097152 | tf_op jit(solution)/shard_map/partial_images/pallas_call | solution.py:117
  12.5 9.4 %all-to-all-start = ((f32[8,64,256]{2,1,0:T(8,128)}), f32[8,64,256]{2,1,0:T(8,128)S(1)}, u32[]{:S(2)}, u32[]{:S(2)}) async-start(f32[8,64,256]{2,1,0:T(8,128)} %bitcast.4), calls=%async_computation | async-start | bytes 1048576 | tf_op jit(solution)/shard_map/all_to_all | solution.py:255
  21.9 0.1 constant_dynamic-slice_fusion.3
  22.0 2.8 %collective-permute-start.1 = (bf16[512,128]{1,0:T(8,128)(2,1)S(1)}, bf16[512,128]{1,0:T(8,128)(2,1)S(1)}, u32[]{:S(2)}, u32[]{:S(2)}) collective-permute-start(bf16[512,128]{1,0:T(8,128)(2,1)S(1)} %get-tuple-element.39), channel_id=1, source_target_pairs={{0,224},{1,33},{16,240},{17,49},{32,0},{33,65},{48,16},{49,81},{64... | collective-permute-start | bytes 393224 | tf_op jit(solution)/shard_map/ppermute | solution.py:42
  24.9 3.1 %collective-permute-start.3 = (bf16[512,128]{1,0:T(8,128)(2,1)S(1)}, bf16[512,128]{1,0:T(8,128)(2,1)S(1)}, u32[]{:S(2)}, u32[]{:S(2)}) collective-permute-start(bf16[512,128]{1,0:T(8,128)(2,1)S(1)} %get-tuple-element.38), channel_id=1, source_target_pairs={{0,192},{1,65},{16,208},{17,81},{32,224},{33,97},{48,240},{49,113}... | collective-permute-start | bytes 393224 | tf_op jit(solution)/shard_map/ppermute | solution.py:42
  28.0 4.1 %all-to-all-done = f32[8,64,256]{2,1,0:T(8,128)S(1)} async-done(((f32[8,64,256]{2,1,0:T(8,128)}), f32[8,64,256]{2,1,0:T(8,128)S(1)}, u32[]{:S(2)}, u32[]{:S(2)}) %all-to-all-start) | async-done | bytes 524320 | tf_op jit(solution)/shard_map/all_to_all | solution.py:255
  32.1 0.1 collective-permute-start.2
  32.3 0.1 dynamic_slice.20
  32.4 7.0 %collective-permute-start.6 = (bf16[256,128]{1,0:T(8,128)(2,1)S(1)}, bf16[256,128]{1,0:T(8,128)(2,1)S(1)}, u32[]{:S(2)}, u32[]{:S(2)}) collective-permute-start(bf16[256,128]{1,0:T(8,128)(2,1)S(1)} %dynamic_slice.20), channel_id=1, source_target_pairs={{0,128},{1,129},{16,144},{17,145},{32,160},{33,161},{48,176},{49,1... | collective-permute-start | bytes 196616 | tf_op jit(solution)/shard_map/ppermute | solution.py:42
  39.3 3.4 %collective-permute-done.4.refs_2_ = bf16[512,128]{1,0:T(8,128)(2,1)S(1)} collective-permute-done((bf16[512,128]{1,0:T(8,128)(2,1)S(1)}, bf16[512,128]{1,0:T(8,128)(2,1)S(1)}, u32[]{:S(2)}, u32[]{:S(2)}) %collective-permute-start.4) | collective-permute-done | bytes 131104 | tf_op jit(solution)/shard_map/ppermute | solution.py:42
  42.7 2.8 %collective-permute-start.5 = (bf16[2,64,256]{2,1,0:T(8,128)(2,1)S(1)}, bf16[2,64,256]{2,1,0:T(8,128)(2,1)S(1)}, u32[]{:S(2)}, u32[]{:S(2)}) collective-permute-start(bf16[2,64,256]{2,1,0:T(8,128)(2,1)S(1)} %pad_maximum_fusion.4), channel_id=1, source_target_pairs={{0,4},{2,6},{4,0},{6,2},{8,12},{10,14},{12,8},{14,10},{1,5},{3,7},... | collective-permute-start | bytes 196616 | tf_op jit(solution)/shard_map/ppermute | solution.py:54
  45.6 1.9 %collective-permute-done.5.refs_2_ = bf16[2,64,256]{2,1,0:T(8,128)(2,1)S(1)} collective-permute-done((bf16[2,64,256]{2,1,0:T(8,128)(2,1)S(1)}, bf16[2,64,256]{2,1,0:T(8,128)(2,1)S(1)}, u32[]{:S(2)}, u32[]{:S(2)}) %collective-permute-start.5) | collective-permute-done | bytes 65568 | tf_op jit(solution)/shard_map/ppermute | solution.py:54
  47.4 2.9 %collective-permute-start.7 = (bf16[4,64,256]{2,1,0:T(8,128)(2,1)S(1)}, bf16[4,64,256]{2,1,0:T(8,128)(2,1)S(1)}, u32[]{:S(2)}, u32[]{:S(2)}) collective-permute-start(bf16[4,64,256]{2,1,0:T(8,128)(2,1)S(1)} %pad_maximum_fusion.3), channel_id=1, source_target_pairs={{0,8},{2,10},{4,12},{6,14},{8,0},{10,2},{12,4},{14,6},{1,9},{3,11}... | collective-permute-start | bytes 393224 | tf_op jit(solution)/shard_map/ppermute | solution.py:54
  50.3 2.6 %collective-permute-done.7.refs_3_ = bf16[4,64,256]{2,1,0:T(8,128)(2,1)S(1)} collective-permute-done((bf16[4,64,256]{2,1,0:T(8,128)(2,1)S(1)}, bf16[4,64,256]{2,1,0:T(8,128)(2,1)S(1)}, u32[]{:S(2)}, u32[]{:S(2)}) %collective-permute-start.7) | collective-permute-done | bytes 131104 | tf_op jit(solution)/shard_map/ppermute | solution.py:54
  52.8 0.7 turned_image.1.refs_3_
  53.6 0.1 collective-permute-start.8
  53.8 1.5 %collective-permute-start.11 = (bf16[256,512]{1,0:T(8,128)(2,1)S(1)}, bf16[256,512]{1,0:T(8,128)(2,1)S(1)}, u32[]{:S(2)}, u32[]{:S(2)}) collective-permute-start(bf16[256,512]{1,0:T(8,128)(2,1)S(1)} %turned_image.1.refs_3_), channel_id=1, source_target_pairs={{0,32},{16,48},{32,64},{48,80},{64,96},{80,112},{96,128},{112,144}... | collective-permute-start | bytes 786440 | tf_op jit(solution)/shard_map/ppermute | solution.py:34
  55.3 1.4 %collective-permute-start.9 = (bf16[768,128]{1,0:T(8,128)(2,1)S(1)}, bf16[768,128]{1,0:T(8,128)(2,1)S(1)}, u32[]{:S(2)}, u32[]{:S(2)}) collective-permute-start(bf16[768,128]{1,0:T(8,128)(2,1)S(1)} %pad_maximum_fusion.2), channel_id=1, source_target_pairs={{0,1},{1,0},{2,3},{3,2},{4,5},{5,4},{6,7},{7,6},{8,9},{9,8},{10,11... | collective-permute-start | bytes 589832 | tf_op jit(solution)/shard_map/ppermute | solution.py:50
  56.7 2.2 %collective-permute-done.8.refs_3_ = bf16[1024,128]{1,0:T(8,128)(2,1)S(1)} collective-permute-done((bf16[1024,128]{1,0:T(8,128)(2,1)S(1)}, bf16[1024,128]{1,0:T(8,128)(2,1)S(1)}, u32[]{:S(2)}, u32[]{:S(2)}) %collective-permute-start.8) | collective-permute-done | bytes 262176 | tf_op jit(solution)/shard_map/ppermute | solution.py:50
  58.9 4.0 %collective-permute-done.9.refs_3_ = bf16[768,128]{1,0:T(8,128)(2,1)S(1)} collective-permute-done((bf16[768,128]{1,0:T(8,128)(2,1)S(1)}, bf16[768,128]{1,0:T(8,128)(2,1)S(1)}, u32[]{:S(2)}, u32[]{:S(2)}) %collective-permute-start.9) | collective-permute-done | bytes 196640 | tf_op jit(solution)/shard_map/ppermute | solution.py:50
  63.0 3.8 %collective-permute-start.10 = (bf16[8,16,128]{2,1,0:T(8,128)(2,1)S(1)}, bf16[8,16,128]{2,1,0:T(8,128)(2,1)S(1)}, u32[]{:S(2)}, u32[]{:S(2)}) collective-permute-start(bf16[8,16,128]{2,1,0:T(8,128)(2,1)S(1)} %constant_dynamic-update-slice_fusion), channel_id=1, source_target_pairs={{0,16},{16,0},{32,48},{48,32},{64,80},{80,64},{96,112},{112,96},{1... | collective-permute-start | bytes 98312 | tf_op jit(solution)/shard_map/ppermute | solution.py:46
  66.9 2.3 %collective-permute-start.12 = (bf16[256,512]{1,0:T(8,128)(2,1)S(1)}, bf16[256,512]{1,0:T(8,128)(2,1)S(1)}, u32[]{:S(2)}, u32[]{:S(2)}) collective-permute-start(bf16[256,512]{1,0:T(8,128)(2,1)S(1)} %collective-permute-done.11.refs_4_), channel_id=1, source_target_pairs={{0,32},{16,48},{32,64},{48,80},{64,96},{80,112},{96,128},{112,144}... | collective-permute-start | bytes 786440 | tf_op jit(solution)/shard_map/ppermute | solution.py:34
  69.3 1.3 %sketch_terms.5.refs_6_ = f32[256,2048]{1,0:T(8,128)S(1)} custom-call(s32[3]{0:T(128)S(1)} %pad_add_fusion.place.refs_0_, bf16[1,16,128]{2,1,0:T(8,128)(2,1)S(1)} %get-tuple-element.40.refs_1_, bf16[512,128]{1,0:T(8,128)(2,1)S(1)} %get-tuple-element.36.refs_2_, bf16[256,512]{1,0:T(8,128)(2,1)S(1)} %turned_image.1.refs_3_), custom_call_target="tpu_custom_call" | custom-call | flops 1073741824 | bytes 2097152 | tf_op jit(solution)/shard_map/sketch_terms/pallas_call | solution.py:198
  70.6 1.9 %sketch_terms.6.refs_6_ = f32[256,2048]{1,0:T(8,128)S(1)} custom-call(s32[3]{0:T(128)S(1)} %pad_add_fusion.place.refs_0_, bf16[2,16,128]{2,1,0:T(8,128)(2,1)S(1)} %pad_maximum_fusion.7.refs_1_, bf16[512,128]{1,0:T(8,128)(2,1)S(1)} %collective-permute-done.1.refs_2_, bf16[1024,128]{1,0:T(8,128)(2,1)S(1)} %collective-permute-done.8.refs_3_, ...), custom_call_target="tpu_custom_call" | custom-call | flops 2147483648 | bytes 2097152 | tf_op jit(solution)/shard_map/sketch_terms/pallas_call | solution.py:198
  72.5 3.0 %collective-permute-done.16.refs_5_ = bf16[256,512]{1,0:T(8,128)(2,1)S(1)} collective-permute-done((bf16[256,512]{1,0:T(8,128)(2,1)S(1)}, bf16[256,512]{1,0:T(8,128)(2,1)S(1)}, u32[]{:S(2)}, u32[]{:S(2)}) %collective-permute-start.16) | collective-permute-done | bytes 262176 | tf_op jit(solution)/shard_map/ppermute | solution.py:34
  75.5 0.7 collective-permute-start.17
  76.2 0.7 collective-permute-done.12.refs_4_
  76.9 0.1 collective-permute-start.13
  77.1 1.9 %sketch_terms.7.refs_6_ = f32[256,2048]{1,0:T(8,128)S(1)} custom-call(s32[3]{0:T(128)S(1)} %pad_add_fusion.place.refs_0_, bf16[2,16,128]{2,1,0:T(8,128)(2,1)S(1)} %pad_maximum_fusion.6.refs_1_, bf16[512,128]{1,0:T(8,128)(2,1)S(1)} %collective-permute-done.3.refs_2_, bf16[1024,128]{1,0:T(8,128)(2,1)S(1)} %collective-permute-done.8.refs_3_, ...), custom_call_target="tpu_custom_call" | custom-call | flops 2147483648 | bytes 2097152 | tf_op jit(solution)/shard_map/sketch_terms/pallas_call | solution.py:198
  79.0 3.8 %collective-permute-done.17.refs_5_ = bf16[256,512]{1,0:T(8,128)(2,1)S(1)} collective-permute-done((bf16[256,512]{1,0:T(8,128)(2,1)S(1)}, bf16[256,512]{1,0:T(8,128)(2,1)S(1)}, u32[]{:S(2)}, u32[]{:S(2)}) %collective-permute-start.17) | collective-permute-done | bytes 262176 | tf_op jit(solution)/shard_map/ppermute | solution.py:34
  82.8 1.7 %collective-permute-start.18 = (bf16[128,512]{1,0:T(8,128)(2,1)S(1)}, bf16[128,512]{1,0:T(8,128)(2,1)S(1)}, u32[]{:S(2)}, u32[]{:S(2)}) collective-permute-start(bf16[128,512]{1,0:T(8,128)(2,1)S(1)} %slice.118), channel_id=1, source_target_pairs={{0,224},{16,240},{32,0},{48,16},{64,32},{80,48},{96,64},{112,80},{... | collective-permute-start | bytes 393224 | tf_op jit(solution)/shard_map/ppermute | solution.py:34
  84.5 0.7 collective-permute-done.13.refs_4_
  85.2 1.8 %sketch_terms.8.refs_5_ = f32[256,2048]{1,0:T(8,128)S(1)} custom-call(s32[3]{0:T(128)S(1)} %pad_add_fusion.place.refs_0_, bf16[2,16,128]{2,1,0:T(8,128)(2,1)S(1)} %pad_maximum_fusion.5.refs_1_, bf16[512,128]{1,0:T(8,128)(2,1)S(1)} %collective-permute-done.4.refs_2_, bf16[768,128]{1,0:T(8,128)(2,1)S(1)} %collective-permute-done.9.refs_3_, ...), custom_call_target="tpu_custom_call" | custom-call | flops 2147483648 | bytes 2097152 | tf_op jit(solution)/shard_map/sketch_terms/pallas_call | solution.py:198
  87.1 3.2 %collective-permute-done.14 = bf16[128,512]{1,0:T(8,128)(2,1)S(1)} collective-permute-done((bf16[128,512]{1,0:T(8,128)(2,1)S(1)}, bf16[128,512]{1,0:T(8,128)(2,1)S(1)}, u32[]{:S(2)}, u32[]{:S(2)}) %collective-permute-start.14) | collective-permute-done | bytes 131104 | tf_op jit(solution)/shard_map/ppermute | solution.py:34
  90.2 1.7 %sketch_terms.9 = f32[2,2,4,256,128]{4,3,2,1,0:T(8,128)S(1)} custom-call(s32[3]{0:T(128)S(1)} %pad_add_fusion.place.refs_0_, bf16[1,16,128]{2,1,0:T(8,128)(2,1)S(1)} %get-tuple-element.47.refs_1_, bf16[256,128]{1,0:T(8,128)(2,1)S(1)} %collective-permute-done.6.refs_2_, bf16[768,128]{1,0:T(8,128)(2,1)S(1)} %collective-permute-done.9.refs_3_, ...), custom_call_target="tpu_custom_call" | custom-call | flops 1073741824 | bytes 2097152 | tf_op jit(solution)/shard_map/sketch_terms/pallas_call | solution.py:198
  91.9 0.1 slice_bitcast_fusion
  92.0 3.0 %collective-permute-start.19 = (f32[4,256,128]{2,1,0:T(8,128)S(1)}, f32[4,256,128]{2,1,0:T(8,128)S(1)}, u32[]{:S(2)}, u32[]{:S(2)}) collective-permute-start(f32[4,256,128]{2,1,0:T(8,128)S(1)} %get-tuple-element.35), channel_id=1, source_target_pairs={{0,16},{16,0},{32,48},{48,32},{64,80},{80,64},{96,112},{112,96},{1... | collective-permute-start | bytes 1572872 | tf_op jit(solution)/shard_map/ppermute | solution.py:46
  95.0 0.1 collective-permute-start.21
  95.1 1.4 %collective-permute-done.19 = f32[4,256,128]{2,1,0:T(8,128)S(1)} collective-permute-done((f32[4,256,128]{2,1,0:T(8,128)S(1)}, f32[4,256,128]{2,1,0:T(8,128)S(1)}, u32[]{:S(2)}, u32[]{:S(2)}) %collective-permute-start.19) | collective-permute-done | bytes 524320 | tf_op jit(solution)/shard_map/ppermute | solution.py:46
  96.7 0.1 collective-permute-start.20
  96.8 0.6 collective-permute-done.21.refs_1_
  97.3 1.6 %final_sketch.2.refs_1_ = f32[64,8,512]{2,1,0:T(8,128)} custom-call(s32[3]{0:T(128)S(1)} %pad_add_fusion.place.refs_0_, f32[4,256,128]{2,1,0:T(8,128)S(1)} %get-tuple-element.34.refs_0_, f32[4,256,128]{2,1,0:T(8,128)S(1)} %collective-permute-done.21.refs_1_), custom_call_target="tpu_custom_call" | custom-call | tf_op jit(solution)/shard_map/final_sketch/pallas_call | solution.py:231
  98.9 5.4 %collective-permute-done.20.refs_0_ = bf16[4,256,128]{2,1,0:T(8,128)(2,1)S(1)} collective-permute-done((bf16[4,256,128]{2,1,0:T(8,128)(2,1)S(1)}, bf16[4,256,128]{2,1,0:T(8,128)(2,1)S(1)}, u32[]{:S(2)}, u32[]{:S(2)}) %collective-permute-start.20) | collective-permute-done | bytes 262176 | tf_op jit(solution)/shard_map/ppermute | solution.py:50
  104.3 1.6 %final_sketch.3 = f32[64,8,512]{2,1,0:T(8,128)} custom-call(s32[3]{0:T(128)S(1)} %pad_add_fusion.place.refs_0_, bf16[4,256,128]{2,1,0:T(8,128)(2,1)S(1)} %collective-permute-done.20.refs_0_, f32[64,8,512]{2,1,0:T(8,128)} %final_sketch.2.refs_1_), custom_call_target="tpu_custom_call", output_to_operand_aliasing={{}: (2, {})} | custom-call | tf_op jit(solution)/shard_map/final_sketch/pallas_call | solution.py:231
  (42 shorter events, 0.8 us)
Async XLA Ops:
  0.8 8.4 %collective-permute-start = (bf16[16,1024]{1,0:T(8,128)(2,1)S(1)}, bf16[16,1024]{1,0:T(8,128)(2,1)S(1)}, u32[]{:S(2)}, u32[]{:S(2)}) collective-permute-start(bf16[16,1024]{1,0:T(8,128)(2,1)S(1)} %slice.84), channel_id=1, source_target_pairs={{0,16},{16,32},{32,48},{48,64},{64,80},{80,96},{96,112},{112,128},... | collective-permute-start | bytes 98312 | tf_op jit(solution)/shard_map/ppermute | solution.py:30
  6.4 0.7 copy-start.1
  7.1 2.1 %copy-start = (bf16[512,1024]{1,0:T(8,128)(2,1)S(1)}, bf16[512,1024]{1,0:T(8,128)(2,1)}, u32[]{:S(2)}) copy-start(bf16[512,1024]{1,0:T(8,128)(2,1)} %records.1) | copy-start | bytes 3145732
  12.5 19.6 %all-to-all-start = ((f32[8,64,256]{2,1,0:T(8,128)}), f32[8,64,256]{2,1,0:T(8,128)S(1)}, u32[]{:S(2)}, u32[]{:S(2)}) async-start(f32[8,64,256]{2,1,0:T(8,128)} %bitcast.4), calls=%async_computation | async-start | bytes 1048576 | tf_op jit(solution)/shard_map/all_to_all | solution.py:255
  22.0 5.9 %collective-permute-start.1 = (bf16[512,128]{1,0:T(8,128)(2,1)S(1)}, bf16[512,128]{1,0:T(8,128)(2,1)S(1)}, u32[]{:S(2)}, u32[]{:S(2)}) collective-permute-start(bf16[512,128]{1,0:T(8,128)(2,1)S(1)} %get-tuple-element.39), channel_id=1, source_target_pairs={{0,224},{1,33},{16,240},{17,49},{32,0},{33,65},{48,16},{49,81},{64... | collective-permute-start | bytes 393224 | tf_op jit(solution)/shard_map/ppermute | solution.py:42
  24.9 14.5 %collective-permute-start.3 = (bf16[512,128]{1,0:T(8,128)(2,1)S(1)}, bf16[512,128]{1,0:T(8,128)(2,1)S(1)}, u32[]{:S(2)}, u32[]{:S(2)}) collective-permute-start(bf16[512,128]{1,0:T(8,128)(2,1)S(1)} %get-tuple-element.38), channel_id=1, source_target_pairs={{0,192},{1,65},{16,208},{17,81},{32,224},{33,97},{48,240},{49,113}... | collective-permute-start | bytes 393224 | tf_op jit(solution)/shard_map/ppermute | solution.py:42
  28.0 14.7 %collective-permute-start.4 = (bf16[512,128]{1,0:T(8,128)(2,1)S(1)}, bf16[512,128]{1,0:T(8,128)(2,1)S(1)}, u32[]{:S(2)}, u32[]{:S(2)}) collective-permute-start(bf16[512,128]{1,0:T(8,128)(2,1)S(1)} %get-tuple-element.37), channel_id=1, source_target_pairs={{0,96},{1,161},{16,112},{17,177},{32,128},{33,193},{48,144},{49,20... | collective-permute-start | bytes 393224 | tf_op jit(solution)/shard_map/ppermute | solution.py:42
  32.1 10.5 %collective-permute-start.2 = (bf16[1,64,256]{2,1,0:T(8,128)(2,1)S(1)}, bf16[1,64,256]{2,1,0:T(8,128)(2,1)S(1)}, u32[]{:S(2)}, u32[]{:S(2)}) collective-permute-start(bf16[1,64,256]{2,1,0:T(8,128)(2,1)S(1)} %bitcast.40), channel_id=1, source_target_pairs={{0,2},{2,0},{4,6},{6,4},{8,10},{10,8},{12,14},{14,12},{1,3},{3,1},... | collective-permute-start | bytes 98312 | tf_op jit(solution)/shard_map/ppermute | solution.py:54
  32.4 13.2 %collective-permute-start.6 = (bf16[256,128]{1,0:T(8,128)(2,1)S(1)}, bf16[256,128]{1,0:T(8,128)(2,1)S(1)}, u32[]{:S(2)}, u32[]{:S(2)}) collective-permute-start(bf16[256,128]{1,0:T(8,128)(2,1)S(1)} %dynamic_slice.20), channel_id=1, source_target_pairs={{0,128},{1,129},{16,144},{17,145},{32,160},{33,161},{48,176},{49,1... | collective-permute-start | bytes 196616 | tf_op jit(solution)/shard_map/ppermute | solution.py:42
  42.7 4.7 %collective-permute-start.5 = (bf16[2,64,256]{2,1,0:T(8,128)(2,1)S(1)}, bf16[2,64,256]{2,1,0:T(8,128)(2,1)S(1)}, u32[]{:S(2)}, u32[]{:S(2)}) collective-permute-start(bf16[2,64,256]{2,1,0:T(8,128)(2,1)S(1)} %pad_maximum_fusion.4), channel_id=1, source_target_pairs={{0,4},{2,6},{4,0},{6,2},{8,12},{10,14},{12,8},{14,10},{1,5},{3,7},... | collective-permute-start | bytes 196616 | tf_op jit(solution)/shard_map/ppermute | solution.py:54
  47.4 5.4 %collective-permute-start.7 = (bf16[4,64,256]{2,1,0:T(8,128)(2,1)S(1)}, bf16[4,64,256]{2,1,0:T(8,128)(2,1)S(1)}, u32[]{:S(2)}, u32[]{:S(2)}) collective-permute-start(bf16[4,64,256]{2,1,0:T(8,128)(2,1)S(1)} %pad_maximum_fusion.3), channel_id=1, source_target_pairs={{0,8},{2,10},{4,12},{6,14},{8,0},{10,2},{12,4},{14,6},{1,9},{3,11}... | collective-permute-start | bytes 393224 | tf_op jit(solution)/shard_map/ppermute | solution.py:54
  53.6 5.3 %collective-permute-start.8 = (bf16[1024,128]{1,0:T(8,128)(2,1)S(1)}, bf16[1024,128]{1,0:T(8,128)(2,1)S(1)}, u32[]{:S(2)}, u32[]{:S(2)}) collective-permute-start(bf16[1024,128]{1,0:T(8,128)(2,1)S(1)} %pad_maximum_fusion), channel_id=1, source_target_pairs={{0,1},{1,0},{2,3},{3,2},{4,5},{5,4},{6,7},{7,6},{8,9},{9,8},{10,11... | collective-permute-start | bytes 786440 | tf_op jit(solution)/shard_map/ppermute | solution.py:50
  53.7 13.1 %collective-permute-start.15 = (bf16[256,512]{1,0:T(8,128)(2,1)S(1)}, bf16[256,512]{1,0:T(8,128)(2,1)S(1)}, u32[]{:S(2)}, u32[]{:S(2)}) collective-permute-start(bf16[256,512]{1,0:T(8,128)(2,1)S(1)} %turned_image.1.refs_3_), channel_id=1, source_target_pairs={{0,224},{16,240},{32,0},{48,16},{64,32},{80,48},{96,64},{112,80},{... | collective-permute-start | bytes 786440 | tf_op jit(solution)/shard_map/ppermute | solution.py:34
  53.8 13.1 %collective-permute-start.11 = (bf16[256,512]{1,0:T(8,128)(2,1)S(1)}, bf16[256,512]{1,0:T(8,128)(2,1)S(1)}, u32[]{:S(2)}, u32[]{:S(2)}) collective-permute-start(bf16[256,512]{1,0:T(8,128)(2,1)S(1)} %turned_image.1.refs_3_), channel_id=1, source_target_pairs={{0,32},{16,48},{32,64},{48,80},{64,96},{80,112},{96,128},{112,144}... | collective-permute-start | bytes 786440 | tf_op jit(solution)/shard_map/ppermute | solution.py:34
  55.3 7.7 %collective-permute-start.9 = (bf16[768,128]{1,0:T(8,128)(2,1)S(1)}, bf16[768,128]{1,0:T(8,128)(2,1)S(1)}, u32[]{:S(2)}, u32[]{:S(2)}) collective-permute-start(bf16[768,128]{1,0:T(8,128)(2,1)S(1)} %pad_maximum_fusion.2), channel_id=1, source_target_pairs={{0,1},{1,0},{2,3},{3,2},{4,5},{5,4},{6,7},{7,6},{8,9},{9,8},{10,11... | collective-permute-start | bytes 589832 | tf_op jit(solution)/shard_map/ppermute | solution.py:50
  63.0 6.2 %collective-permute-start.10 = (bf16[8,16,128]{2,1,0:T(8,128)(2,1)S(1)}, bf16[8,16,128]{2,1,0:T(8,128)(2,1)S(1)}, u32[]{:S(2)}, u32[]{:S(2)}) collective-permute-start(bf16[8,16,128]{2,1,0:T(8,128)(2,1)S(1)} %constant_dynamic-update-slice_fusion), channel_id=1, source_target_pairs={{0,16},{16,0},{32,48},{48,32},{64,80},{80,64},{96,112},{112,96},{1... | collective-permute-start | bytes 98312 | tf_op jit(solution)/shard_map/ppermute | solution.py:46
  66.8 8.8 %collective-permute-start.16 = (bf16[256,512]{1,0:T(8,128)(2,1)S(1)}, bf16[256,512]{1,0:T(8,128)(2,1)S(1)}, u32[]{:S(2)}, u32[]{:S(2)}) collective-permute-start(bf16[256,512]{1,0:T(8,128)(2,1)S(1)} %collective-permute-done.15.refs_5_), channel_id=1, source_target_pairs={{0,224},{16,240},{32,0},{48,16},{64,32},{80,48},{96,64},{112,80},{... | collective-permute-start | bytes 786440 | tf_op jit(solution)/shard_map/ppermute | solution.py:34
  66.9 10.1 %collective-permute-start.12 = (bf16[256,512]{1,0:T(8,128)(2,1)S(1)}, bf16[256,512]{1,0:T(8,128)(2,1)S(1)}, u32[]{:S(2)}, u32[]{:S(2)}) collective-permute-start(bf16[256,512]{1,0:T(8,128)(2,1)S(1)} %collective-permute-done.11.refs_4_), channel_id=1, source_target_pairs={{0,32},{16,48},{32,64},{48,80},{64,96},{80,112},{96,128},{112,144}... | collective-permute-start | bytes 786440 | tf_op jit(solution)/shard_map/ppermute | solution.py:34
  75.5 7.3 %collective-permute-start.17 = (bf16[256,512]{1,0:T(8,128)(2,1)S(1)}, bf16[256,512]{1,0:T(8,128)(2,1)S(1)}, u32[]{:S(2)}, u32[]{:S(2)}) collective-permute-start(bf16[256,512]{1,0:T(8,128)(2,1)S(1)} %collective-permute-done.16.refs_5_), channel_id=1, source_target_pairs={{0,224},{16,240},{32,0},{48,16},{64,32},{80,48},{96,64},{112,80},{... | collective-permute-start | bytes 786440 | tf_op jit(solution)/shard_map/ppermute | solution.py:34
  76.9 8.2 %collective-permute-start.13 = (bf16[256,512]{1,0:T(8,128)(2,1)S(1)}, bf16[256,512]{1,0:T(8,128)(2,1)S(1)}, u32[]{:S(2)}, u32[]{:S(2)}) collective-permute-start(bf16[256,512]{1,0:T(8,128)(2,1)S(1)} %collective-permute-done.12.refs_4_), channel_id=1, source_target_pairs={{0,32},{16,48},{32,64},{48,80},{64,96},{80,112},{96,128},{112,144}... | collective-permute-start | bytes 786440 | tf_op jit(solution)/shard_map/ppermute | solution.py:34
  82.8 4.3 %collective-permute-start.18 = (bf16[128,512]{1,0:T(8,128)(2,1)S(1)}, bf16[128,512]{1,0:T(8,128)(2,1)S(1)}, u32[]{:S(2)}, u32[]{:S(2)}) collective-permute-start(bf16[128,512]{1,0:T(8,128)(2,1)S(1)} %slice.118), channel_id=1, source_target_pairs={{0,224},{16,240},{32,0},{48,16},{64,32},{80,48},{96,64},{112,80},{... | collective-permute-start | bytes 393224 | tf_op jit(solution)/shard_map/ppermute | solution.py:34
  85.1 5.1 %collective-permute-start.14 = (bf16[128,512]{1,0:T(8,128)(2,1)S(1)}, bf16[128,512]{1,0:T(8,128)(2,1)S(1)}, u32[]{:S(2)}, u32[]{:S(2)}) collective-permute-start(bf16[128,512]{1,0:T(8,128)(2,1)S(1)} %slice.117), channel_id=1, source_target_pairs={{0,32},{16,48},{32,64},{48,80},{64,96},{80,112},{96,128},{112,144}... | collective-permute-start | bytes 393224 | tf_op jit(solution)/shard_map/ppermute | solution.py:34
  92.0 4.5 %collective-permute-start.19 = (f32[4,256,128]{2,1,0:T(8,128)S(1)}, f32[4,256,128]{2,1,0:T(8,128)S(1)}, u32[]{:S(2)}, u32[]{:S(2)}) collective-permute-start(f32[4,256,128]{2,1,0:T(8,128)S(1)} %get-tuple-element.35), channel_id=1, source_target_pairs={{0,16},{16,0},{32,48},{48,32},{64,80},{80,64},{96,112},{112,96},{1... | collective-permute-start | bytes 1572872 | tf_op jit(solution)/shard_map/ppermute | solution.py:46
  95.0 2.3 %collective-permute-start.21 = (f32[4,256,128]{2,1,0:T(8,128)S(1)}, f32[4,256,128]{2,1,0:T(8,128)S(1)}, u32[]{:S(2)}, u32[]{:S(2)}) collective-permute-start(f32[4,256,128]{2,1,0:T(8,128)S(1)} %get-tuple-element.33), channel_id=1, source_target_pairs={{0,16},{16,0},{32,48},{48,32},{64,80},{80,64},{96,112},{112,96},{1... | collective-permute-start | bytes 1572872 | tf_op jit(solution)/shard_map/ppermute | solution.py:46
  96.7 7.6 %collective-permute-start.20 = (bf16[4,256,128]{2,1,0:T(8,128)(2,1)S(1)}, bf16[4,256,128]{2,1,0:T(8,128)(2,1)S(1)}, u32[]{:S(2)}, u32[]{:S(2)}) collective-permute-start(bf16[4,256,128]{2,1,0:T(8,128)(2,1)S(1)} %fusion.1), channel_id=1, source_target_pairs={{0,1},{1,0},{2,3},{3,2},{4,5},{5,4},{6,7},{7,6},{8,9},{9,8},{10,11... | collective-permute-start | bytes 786440 | tf_op jit(solution)/shard_map/ppermute | solution.py:50

commit v5 on v3

--- a/solution.py
+++ b/solution.py
@@ -268,7 +268,7 @@
     half = split_shift(half, 4, 4)
     middle = split_shift(piece(-2 * sign), -2, 2)
     near = split_shift(piece(-sign), -1, 1)
-    parts, near = lax.optimization_barrier((parts, near))
+    parts, half = lax.optimization_barrier((parts, half))
 
     share = jnp.sum(parts, axis=0).astype(BF16)[None]
     got = [share] + [y_shift(share, k) for k in range(1, 4)]

time: 102 us -> 109 us (1.069)
  waiting for transfers between devices: 34.6 us -> 37.9 us
  Pallas kernels: 16.2 us -> 17.8 us
  starting transfers between devices: 47.5 us -> 48.9 us
    all_to_all x1, waiting for transfers between devices: 4.13 us -> 0.01 us  [per_device(): lax.all_to_all(partial.reshape(NCHAN, SHARE, HALF_P), 'chan', 0, 0, tiled...]
    ppermute x4, waiting for transfers between devices: 8.32 us -> 11.1 us  [split_shift(): return lax.ppermute(value, ('tm', 'hank'), pairs)]
    ppermute x3, waiting for transfers between devices: 0.01 us -> 2.56 us  [y_shift(): lax.ppermute(value, 'chan', [(i, i & 4 | i + steps & 3) for i in range(NC...]
    ppermute x1, waiting for transfers between devices: 0.23 us -> 2.63 us  [x_swap(): return lax.ppermute(value, 'chan', [(i, i ^ 4) for i in range(NCHAN)])]
    ppermute x3, starting transfers between devices: 5.23 us -> 7.46 us  [core_swap(): return lax.ppermute(value, 'tm', [(i, i ^ 1) for i in range(16)])]
    ppermute x8, starting transfers between devices: 12 us -> 9.83 us  [z_shift(): lax.ppermute(value, 'tm', [(i, (i + 2 * steps) % 16) for i in range(16)])]
    ppermute x3, starting transfers between devices: 2.82 us -> 4.22 us  [y_shift(): lax.ppermute(value, 'chan', [(i, i & 4 | i + steps & 3) for i in range(NC...]
  transfers between devices with their start and end apart: 24 -> 24, of which waited for: 13 -> 12; matrix products, arithmetic and copies ran while one was open for 1% -> 1% of each run, Pallas kernels for 10% -> 10%
where the time goes in v5:
time: 109 us; the launch traced here: 108 us
  starting transfers between devices  48.9 us (45%)
  waiting for transfers between devices  37.9 us (35%)
  Pallas kernels  17.8 us (16%)
  local copies, waits for them, and re-layouts  1.8 us (2%)
    ppermute x4, waiting for transfers between devices, split_shift(): return lax.ppermute(value, ('tm', 'hank'), pairs)  11.1 us
    ppermute x3, waiting for transfers between devices, hank_swap(): return lax.ppermute(value, 'hank', [(0, 1), (1, 0)])  11 us
    ppermute x8, starting transfers between devices, z_shift(): lax.ppermute(value, 'tm', [(i, (i + 2 * steps) % 16) for i in range(16)])  9.83 us
    ppermute x8, waiting for transfers between devices, z_shift(): lax.ppermute(value, 'tm', [(i, (i + 2 * steps) % 16) for i in range(16)])  9.16 us
    ppermute x4, starting transfers between devices, split_shift(): return lax.ppermute(value, ('tm', 'hank'), pairs)  8.99 us
    pallas_call x5, Pallas kernels, sketch_terms(): pl.pallas_call(functools.partial(sketch_kernel, count, starts, turn, firs...  8.61 us
    all_to_all x1, starting transfers between devices, per_device(): lax.all_to_all(partial.reshape(NCHAN, SHARE, HALF_P), 'chan', 0, 0, tiled...  7.94 us
    ppermute x3, starting transfers between devices, core_swap(): return lax.ppermute(value, 'tm', [(i, i ^ 1) for i in range(16)])  7.46 us
  transfers between devices with their start and end apart: 24, of which 12 were waited for; matrix products, arithmetic and copies ran while one was open for 1% of the time, Pallas kernels for 10%

profile of v5, /device:TPU:1, one launch (start us, length us, event | category | flops | bytes accessed | tf_op | source)
XLA Modules:
  0.0 107.8 jit_solution(7367861293202577046)
XLA Ops:
  0.0 0.8 slice.84
  0.8 4.9 %collective-permute-start = (bf16[16,1024]{1,0:T(8,128)(2,1)S(1)}, bf16[16,1024]{1,0:T(8,128)(2,1)S(1)}, u32[]{:S(2)}, u32[]{:S(2)}) collective-permute-start(bf16[16,1024]{1,0:T(8,128)(2,1)S(1)} %slice.84), channel_id=1, source_target_pairs={{0,16},{16,32},{32,48},{48,64},{64,80},{80,96},{96,112},{112,128},... | collective-permute-start | bytes 98312 | tf_op jit(solution)/shard_map/ppermute | solution.py:30
  6.4 0.6 copy-done.1
  7.1 2.1 %probe_signs.1.signs = bf16[8,2048,256]{2,1,0:T(8,128)(2,1)S(1)} custom-call(s32[3]{0:T(128)S(1)} %pad_add_fusion.place.refs_0_, s32[16]{0:T(128)S(1)} %copy-done.1, s32[1]{0:T(128)S(6)} %copy.13.seed), custom_call_target="tpu_custom_call" | custom-call | bytes 14680064 | tf_op jit(solution)/shard_map/probe_signs/pallas_call | solution.py:109
  9.2 3.3 %partial_images.1 = f32[512,256]{1,0:T(8,128)} custom-call(s32[3]{0:T(128)S(1)} %pad_add_fusion.place.refs_0_, s32[16]{0:T(128)S(1)} %copy-done.1, bf16[512,1024]{1,0:T(8,128)(2,1)S(1)} %copy-done, bf16[16,1024]{1,0:T(8,128)(2,1)S(1)} %collective-permute-done.behind, bf16[8,2048,256]{2,1,0:T(8,128)(2,1)S(1)} %probe_signs.1.signs), custom_call_target="tpu_custom_call" | custom-call | flops 4294967296 | bytes 2097152 | tf_op jit(solution)/shard_map/partial_images/pallas_call | solution.py:121
  12.5 7.9 %all-to-all-start = ((f32[8,64,256]{2,1,0:T(8,128)}), f32[8,64,256]{2,1,0:T(8,128)S(1)}, u32[]{:S(2)}, u32[]{:S(2)}) async-start(f32[8,64,256]{2,1,0:T(8,128)} %bitcast.4), calls=%async_computation | async-start | bytes 1048576 | tf_op jit(solution)/shard_map/all_to_all | solution.py:259
  20.4 0.1 constant_dynamic-slice_fusion.3
  20.6 5.2 %collective-permute-start.5 = (bf16[512,128]{1,0:T(8,128)(2,1)S(1)}, bf16[512,128]{1,0:T(8,128)(2,1)S(1)}, u32[]{:S(2)}, u32[]{:S(2)}) collective-permute-start(bf16[512,128]{1,0:T(8,128)(2,1)S(1)} %get-tuple-element.35), channel_id=1, source_target_pairs={{0,192},{1,65},{16,208},{17,81},{32,224},{33,97},{48,240},{49,113}... | collective-permute-start | bytes 393224 | tf_op jit(solution)/shard_map/ppermute | solution.py:42
  25.8 0.5 collective-permute-start.6
  26.3 0.1 dynamic_slice.17
  26.4 3.3 %collective-permute-start.1 = (bf16[256,128]{1,0:T(8,128)(2,1)S(1)}, bf16[256,128]{1,0:T(8,128)(2,1)S(1)}, u32[]{:S(2)}, u32[]{:S(2)}) collective-permute-start(bf16[256,128]{1,0:T(8,128)(2,1)S(1)} %dynamic_slice.17), channel_id=1, source_target_pairs={{0,128},{1,129},{16,144},{17,145},{32,160},{33,161},{48,176},{49,1... | collective-permute-start | bytes 196616 | tf_op jit(solution)/shard_map/ppermute | solution.py:42
  29.7 10.7 %collective-permute-done.1.refs_2_ = bf16[256,128]{1,0:T(8,128)(2,1)S(1)} collective-permute-done((bf16[256,128]{1,0:T(8,128)(2,1)S(1)}, bf16[256,128]{1,0:T(8,128)(2,1)S(1)}, u32[]{:S(2)}, u32[]{:S(2)}) %collective-permute-start.1) | collective-permute-done | bytes 65568 | tf_op jit(solution)/shard_map/ppermute | solution.py:42
  40.4 2.5 %collective-permute-start.4 = (bf16[1,64,256]{2,1,0:T(8,128)(2,1)S(1)}, bf16[1,64,256]{2,1,0:T(8,128)(2,1)S(1)}, u32[]{:S(2)}, u32[]{:S(2)}) collective-permute-start(bf16[1,64,256]{2,1,0:T(8,128)(2,1)S(1)} %bitcast.40), channel_id=1, source_target_pairs={{0,6},{2,0},{4,2},{6,4},{8,14},{10,8},{12,10},{14,12},{1,7},{3,1},... | collective-permute-start | bytes 98312 | tf_op jit(solution)/shard_map/ppermute | solution.py:54
  42.8 1.8 %collective-permute-start.3 = (bf16[1,64,256]{2,1,0:T(8,128)(2,1)S(1)}, bf16[1,64,256]{2,1,0:T(8,128)(2,1)S(1)}, u32[]{:S(2)}, u32[]{:S(2)}) collective-permute-start(bf16[1,64,256]{2,1,0:T(8,128)(2,1)S(1)} %bitcast.42), channel_id=1, source_target_pairs={{0,4},{2,6},{4,0},{6,2},{8,12},{10,14},{12,8},{14,10},{1,5},{3,7},... | collective-permute-start | bytes 98312 | tf_op jit(solution)/shard_map/ppermute | solution.py:54
  44.6 2.2 %collective-permute-done.2.refs_1_ = bf16[1,64,256]{2,1,0:T(8,128)(2,1)S(1)} collective-permute-done((bf16[1,64,256]{2,1,0:T(8,128)(2,1)S(1)}, bf16[1,64,256]{2,1,0:T(8,128)(2,1)S(1)}, u32[]{:S(2)}, u32[]{:S(2)}) %collective-permute-start.2) | collective-permute-done | bytes 32800 | tf_op jit(solution)/shard_map/ppermute | solution.py:54
  46.8 0.3 collective-permute-done.3.refs_2_
  47.2 2.8 %collective-permute-start.7 = (bf16[4,64,256]{2,1,0:T(8,128)(2,1)S(1)}, bf16[4,64,256]{2,1,0:T(8,128)(2,1)S(1)}, u32[]{:S(2)}, u32[]{:S(2)}) collective-permute-start(bf16[4,64,256]{2,1,0:T(8,128)(2,1)S(1)} %pad_maximum_fusion.3), channel_id=1, source_target_pairs={{0,8},{2,10},{4,12},{6,14},{8,0},{10,2},{12,4},{14,6},{1,9},{3,11}... | collective-permute-start | bytes 393224 | tf_op jit(solution)/shard_map/ppermute | solution.py:58
  50.0 2.6 %collective-permute-done.7.refs_4_ = bf16[4,64,256]{2,1,0:T(8,128)(2,1)S(1)} collective-permute-done((bf16[4,64,256]{2,1,0:T(8,128)(2,1)S(1)}, bf16[4,64,256]{2,1,0:T(8,128)(2,1)S(1)}, u32[]{:S(2)}, u32[]{:S(2)}) %collective-permute-start.7) | collective-permute-done | bytes 131104 | tf_op jit(solution)/shard_map/ppermute | solution.py:58
  52.6 0.7 turned_image.1.refs_3_
  53.3 0.5 collective-permute-done.8.refs_2_
  53.8 1.6 %collective-permute-start.9 = (bf16[1024,128]{1,0:T(8,128)(2,1)S(1)}, bf16[1024,128]{1,0:T(8,128)(2,1)S(1)}, u32[]{:S(2)}, u32[]{:S(2)}) collective-permute-start(bf16[1024,128]{1,0:T(8,128)(2,1)S(1)} %pad_maximum_fusion), channel_id=1, source_target_pairs={{0,1},{1,0},{2,3},{3,2},{4,5},{5,4},{6,7},{7,6},{8,9},{9,8},{10,11... | collective-permute-start | bytes 786440 | tf_op jit(solution)/shard_map/ppermute | solution.py:50
  55.4 0.8 collective-permute-start.16
  56.2 1.1 collective-permute-start.12
  57.3 0.4 collective-permute-start.10
  57.7 1.5 %collective-permute-done.9.refs_3_ = bf16[1024,128]{1,0:T(8,128)(2,1)S(1)} collective-permute-done((bf16[1024,128]{1,0:T(8,128)(2,1)S(1)}, bf16[1024,128]{1,0:T(8,128)(2,1)S(1)}, u32[]{:S(2)}, u32[]{:S(2)}) %collective-permute-start.9) | collective-permute-done | bytes 262176 | tf_op jit(solution)/shard_map/ppermute | solution.py:50
  59.2 4.3 %collective-permute-done.10.refs_3_ = bf16[768,128]{1,0:T(8,128)(2,1)S(1)} collective-permute-done((bf16[768,128]{1,0:T(8,128)(2,1)S(1)}, bf16[768,128]{1,0:T(8,128)(2,1)S(1)}, u32[]{:S(2)}, u32[]{:S(2)}) %collective-permute-start.10) | collective-permute-done | bytes 196640 | tf_op jit(solution)/shard_map/ppermute | solution.py:50
  63.5 4.1 %collective-permute-start.11 = (bf16[8,16,128]{2,1,0:T(8,128)(2,1)S(1)}, bf16[8,16,128]{2,1,0:T(8,128)(2,1)S(1)}, u32[]{:S(2)}, u32[]{:S(2)}) collective-permute-start(bf16[8,16,128]{2,1,0:T(8,128)(2,1)S(1)} %constant_dynamic-update-slice_fusion), channel_id=1, source_target_pairs={{0,16},{16,0},{32,48},{48,32},{64,80},{80,64},{96,112},{112,96},{1... | collective-permute-start | bytes 98312 | tf_op jit(solution)/shard_map/ppermute | solution.py:46
  67.7 1.7 %collective-permute-start.17 = (bf16[256,512]{1,0:T(8,128)(2,1)S(1)}, bf16[256,512]{1,0:T(8,128)(2,1)S(1)}, u32[]{:S(2)}, u32[]{:S(2)}) collective-permute-start(bf16[256,512]{1,0:T(8,128)(2,1)S(1)} %collective-permute-done.16.refs_5_), channel_id=1, source_target_pairs={{0,224},{16,240},{32,0},{48,16},{64,32},{80,48},{96,64},{112,80},{... | collective-permute-start | bytes 786440 | tf_op jit(solution)/shard_map/ppermute | solution.py:34
  69.4 0.4 collective-permute-start.13
  69.9 1.3 %sketch_terms.5.refs_6_ = f32[256,2048]{1,0:T(8,128)S(1)} custom-call(s32[3]{0:T(128)S(1)} %pad_add_fusion.place.refs_0_, bf16[1,16,128]{2,1,0:T(8,128)(2,1)S(1)} %get-tuple-element.36.refs_1_, bf16[512,128]{1,0:T(8,128)(2,1)S(1)} %get-tuple-element.32.refs_2_, bf16[256,512]{1,0:T(8,128)(2,1)S(1)} %turned_image.1.refs_3_), custom_call_target="tpu_custom_call" | custom-call | flops 1073741824 | bytes 2097152 | tf_op jit(solution)/shard_map/sketch_terms/pallas_call | solution.py:202
  71.2 1.9 %sketch_terms.6.refs_6_ = f32[256,2048]{1,0:T(8,128)S(1)} custom-call(s32[3]{0:T(128)S(1)} %pad_add_fusion.place.refs_0_, bf16[2,16,128]{2,1,0:T(8,128)(2,1)S(1)} %pad_maximum_fusion.6.refs_1_, bf16[512,128]{1,0:T(8,128)(2,1)S(1)} %collective-permute-done.8.refs_2_, bf16[1024,128]{1,0:T(8,128)(2,1)S(1)} %collective-permute-done.9.refs_3_, ...), custom_call_target="tpu_custom_call" | custom-call | flops 2147483648 | bytes 2097152 | tf_op jit(solution)/shard_map/sketch_terms/pallas_call | solution.py:202
  73.1 3.0 %collective-permute-done.17.refs_5_ = bf16[256,512]{1,0:T(8,128)(2,1)S(1)} collective-permute-done((bf16[256,512]{1,0:T(8,128)(2,1)S(1)}, bf16[256,512]{1,0:T(8,128)(2,1)S(1)}, u32[]{:S(2)}, u32[]{:S(2)}) %collective-permute-start.17) | collective-permute-done | bytes 262176 | tf_op jit(solution)/shard_map/ppermute | solution.py:34
  76.1 2.4 %collective-permute-start.18 = (bf16[256,512]{1,0:T(8,128)(2,1)S(1)}, bf16[256,512]{1,0:T(8,128)(2,1)S(1)}, u32[]{:S(2)}, u32[]{:S(2)}) collective-permute-start(bf16[256,512]{1,0:T(8,128)(2,1)S(1)} %collective-permute-done.17.refs_5_), channel_id=1, source_target_pairs={{0,224},{16,240},{32,0},{48,16},{64,32},{80,48},{96,64},{112,80},{... | collective-permute-start | bytes 786440 | tf_op jit(solution)/shard_map/ppermute | solution.py:34
  78.5 1.9 %sketch_terms.7.refs_6_ = f32[256,2048]{1,0:T(8,128)S(1)} custom-call(s32[3]{0:T(128)S(1)} %pad_add_fusion.place.refs_0_, bf16[2,16,128]{2,1,0:T(8,128)(2,1)S(1)} %pad_maximum_fusion.5.refs_1_, bf16[512,128]{1,0:T(8,128)(2,1)S(1)} %collective-permute-done.5.refs_2_, bf16[1024,128]{1,0:T(8,128)(2,1)S(1)} %collective-permute-done.9.refs_3_, ...), custom_call_target="tpu_custom_call" | custom-call | flops 2147483648 | bytes 2097152 | tf_op jit(solution)/shard_map/sketch_terms/pallas_call | solution.py:202
  80.4 3.0 %collective-permute-done.18.refs_5_ = bf16[256,512]{1,0:T(8,128)(2,1)S(1)} collective-permute-done((bf16[256,512]{1,0:T(8,128)(2,1)S(1)}, bf16[256,512]{1,0:T(8,128)(2,1)S(1)}, u32[]{:S(2)}, u32[]{:S(2)}) %collective-permute-start.18) | collective-permute-done | bytes 262176 | tf_op jit(solution)/shard_map/ppermute | solution.py:34
  83.4 3.4 %collective-permute-start.19 = (bf16[128,512]{1,0:T(8,128)(2,1)S(1)}, bf16[128,512]{1,0:T(8,128)(2,1)S(1)}, u32[]{:S(2)}, u32[]{:S(2)}) collective-permute-start(bf16[128,512]{1,0:T(8,128)(2,1)S(1)} %slice.118), channel_id=1, source_target_pairs={{0,224},{16,240},{32,0},{48,16},{64,32},{80,48},{96,64},{112,80},{... | collective-permute-start | bytes 393224 | tf_op jit(solution)/shard_map/ppermute | solution.py:34
  86.8 0.1 collective-permute-start.15
  86.9 1.8 %sketch_terms.8.refs_5_ = f32[256,2048]{1,0:T(8,128)S(1)} custom-call(s32[3]{0:T(128)S(1)} %pad_add_fusion.place.refs_0_, bf16[2,16,128]{2,1,0:T(8,128)(2,1)S(1)} %pad_maximum_fusion.4.refs_1_, bf16[512,128]{1,0:T(8,128)(2,1)S(1)} %collective-permute-done.6.refs_2_, bf16[768,128]{1,0:T(8,128)(2,1)S(1)} %collective-permute-done.10.refs_3_, ...), custom_call_target="tpu_custom_call" | custom-call | flops 2147483648 | bytes 2097152 | tf_op jit(solution)/shard_map/sketch_terms/pallas_call | solution.py:202
  88.8 3.2 %collective-permute-done.15 = bf16[128,512]{1,0:T(8,128)(2,1)S(1)} collective-permute-done((bf16[128,512]{1,0:T(8,128)(2,1)S(1)}, bf16[128,512]{1,0:T(8,128)(2,1)S(1)}, u32[]{:S(2)}, u32[]{:S(2)}) %collective-permute-start.15) | collective-permute-done | bytes 131104 | tf_op jit(solution)/shard_map/ppermute | solution.py:34
  92.0 1.7 %sketch_terms.9 = f32[2,2,4,256,128]{4,3,2,1,0:T(8,128)S(1)} custom-call(s32[3]{0:T(128)S(1)} %pad_add_fusion.place.refs_0_, bf16[1,16,128]{2,1,0:T(8,128)(2,1)S(1)} %get-tuple-element.43.refs_1_, bf16[256,128]{1,0:T(8,128)(2,1)S(1)} %collective-permute-done.1.refs_2_, bf16[768,128]{1,0:T(8,128)(2,1)S(1)} %collective-permute-done.10.refs_3_, ...), custom_call_target="tpu_custom_call" | custom-call | flops 1073741824 | bytes 2097152 | tf_op jit(solution)/shard_map/sketch_terms/pallas_call | solution.py:202
  93.6 0.1 slice_bitcast_fusion
  93.8 3.2 %collective-permute-start.20 = (f32[4,256,128]{2,1,0:T(8,128)S(1)}, f32[4,256,128]{2,1,0:T(8,128)S(1)}, u32[]{:S(2)}, u32[]{:S(2)}) collective-permute-start(f32[4,256,128]{2,1,0:T(8,128)S(1)} %get-tuple-element.31), channel_id=1, source_target_pairs={{0,16},{16,0},{32,48},{48,32},{64,80},{80,64},{96,112},{112,96},{1... | collective-permute-start | bytes 1572872 | tf_op jit(solution)/shard_map/ppermute | solution.py:46
  97.0 0.1 collective-permute-start.22
  97.1 1.4 %collective-permute-done.20 = f32[4,256,128]{2,1,0:T(8,128)S(1)} collective-permute-done((f32[4,256,128]{2,1,0:T(8,128)S(1)}, f32[4,256,128]{2,1,0:T(8,128)S(1)}, u32[]{:S(2)}, u32[]{:S(2)}) %collective-permute-start.20) | collective-permute-done | bytes 524320 | tf_op jit(solution)/shard_map/ppermute | solution.py:46
  98.6 0.8 collective-permute-start.21
  99.4 1.6 %final_sketch.2.refs_1_ = f32[64,8,512]{2,1,0:T(8,128)} custom-call(s32[3]{0:T(128)S(1)} %pad_add_fusion.place.refs_0_, f32[4,256,128]{2,1,0:T(8,128)S(1)} %get-tuple-element.30.refs_0_, f32[4,256,128]{2,1,0:T(8,128)S(1)} %collective-permute-done.22.refs_1_), custom_call_target="tpu_custom_call" | custom-call | tf_op jit(solution)/shard_map/final_sketch/pallas_call | solution.py:235
  101.0 5.2 %collective-permute-done.21.refs_0_ = bf16[4,256,128]{2,1,0:T(8,128)(2,1)S(1)} collective-permute-done((bf16[4,256,128]{2,1,0:T(8,128)(2,1)S(1)}, bf16[4,256,128]{2,1,0:T(8,128)(2,1)S(1)}, u32[]{:S(2)}, u32[]{:S(2)}) %collective-permute-start.21) | collective-permute-done | bytes 262176 | tf_op jit(solution)/shard_map/ppermute | solution.py:50
  106.2 1.6 %final_sketch.3 = f32[64,8,512]{2,1,0:T(8,128)} custom-call(s32[3]{0:T(128)S(1)} %pad_add_fusion.place.refs_0_, bf16[4,256,128]{2,1,0:T(8,128)(2,1)S(1)} %collective-permute-done.21.refs_0_, f32[64,8,512]{2,1,0:T(8,128)} %final_sketch.2.refs_1_), custom_call_target="tpu_custom_call", output_to_operand_aliasing={{}: (2, {})} | custom-call | tf_op jit(solution)/shard_map/final_sketch/pallas_call | solution.py:235
  (43 shorter events, 0.5 us)
Async XLA Ops:
  0.8 8.4 %collective-permute-start = (bf16[16,1024]{1,0:T(8,128)(2,1)S(1)}, bf16[16,1024]{1,0:T(8,128)(2,1)S(1)}, u32[]{:S(2)}, u32[]{:S(2)}) collective-permute-start(bf16[16,1024]{1,0:T(8,128)(2,1)S(1)} %slice.84), channel_id=1, source_target_pairs={{0,16},{16,32},{32,48},{48,64},{64,80},{80,96},{96,112},{112,128},... | collective-permute-start | bytes 98312 | tf_op jit(solution)/shard_map/ppermute | solution.py:30
  6.4 0.7 copy-start.1
  7.1 2.1 %copy-start = (bf16[512,1024]{1,0:T(8,128)(2,1)S(1)}, bf16[512,1024]{1,0:T(8,128)(2,1)}, u32[]{:S(2)}) copy-start(bf16[512,1024]{1,0:T(8,128)(2,1)} %records.1) | copy-start | bytes 3145732
  12.5 27.8 %all-to-all-start = ((f32[8,64,256]{2,1,0:T(8,128)}), f32[8,64,256]{2,1,0:T(8,128)S(1)}, u32[]{:S(2)}, u32[]{:S(2)}) async-start(f32[8,64,256]{2,1,0:T(8,128)} %bitcast.4), calls=%async_computation | async-start | bytes 1048576 | tf_op jit(solution)/shard_map/all_to_all | solution.py:259
  20.6 24.0 %collective-permute-start.5 = (bf16[512,128]{1,0:T(8,128)(2,1)S(1)}, bf16[512,128]{1,0:T(8,128)(2,1)S(1)}, u32[]{:S(2)}, u32[]{:S(2)}) collective-permute-start(bf16[512,128]{1,0:T(8,128)(2,1)S(1)} %get-tuple-element.35), channel_id=1, source_target_pairs={{0,192},{1,65},{16,208},{17,81},{32,224},{33,97},{48,240},{49,113}... | collective-permute-start | bytes 393224 | tf_op jit(solution)/shard_map/ppermute | solution.py:42
  25.8 18.8 %collective-permute-start.6 = (bf16[512,128]{1,0:T(8,128)(2,1)S(1)}, bf16[512,128]{1,0:T(8,128)(2,1)S(1)}, u32[]{:S(2)}, u32[]{:S(2)}) collective-permute-start(bf16[512,128]{1,0:T(8,128)(2,1)S(1)} %get-tuple-element.34), channel_id=1, source_target_pairs={{0,96},{1,161},{16,112},{17,177},{32,128},{33,193},{48,144},{49,20... | collective-permute-start | bytes 393224 | tf_op jit(solution)/shard_map/ppermute | solution.py:42
  26.4 13.9 %collective-permute-start.1 = (bf16[256,128]{1,0:T(8,128)(2,1)S(1)}, bf16[256,128]{1,0:T(8,128)(2,1)S(1)}, u32[]{:S(2)}, u32[]{:S(2)}) collective-permute-start(bf16[256,128]{1,0:T(8,128)(2,1)S(1)} %dynamic_slice.17), channel_id=1, source_target_pairs={{0,128},{1,129},{16,144},{17,145},{32,160},{33,161},{48,176},{49,1... | collective-permute-start | bytes 196616 | tf_op jit(solution)/shard_map/ppermute | solution.py:42
  40.4 4.2 %collective-permute-start.4 = (bf16[1,64,256]{2,1,0:T(8,128)(2,1)S(1)}, bf16[1,64,256]{2,1,0:T(8,128)(2,1)S(1)}, u32[]{:S(2)}, u32[]{:S(2)}) collective-permute-start(bf16[1,64,256]{2,1,0:T(8,128)(2,1)S(1)} %bitcast.40), channel_id=1, source_target_pairs={{0,6},{2,0},{4,2},{6,4},{8,14},{10,8},{12,10},{14,12},{1,7},{3,1},... | collective-permute-start | bytes 98312 | tf_op jit(solution)/shard_map/ppermute | solution.py:54
  42.8 4.0 %collective-permute-start.2 = (bf16[1,64,256]{2,1,0:T(8,128)(2,1)S(1)}, bf16[1,64,256]{2,1,0:T(8,128)(2,1)S(1)}, u32[]{:S(2)}, u32[]{:S(2)}) collective-permute-start(bf16[1,64,256]{2,1,0:T(8,128)(2,1)S(1)} %bitcast.41), channel_id=1, source_target_pairs={{0,2},{2,4},{4,6},{6,0},{8,10},{10,12},{12,14},{14,8},{1,3},{3,5},... | collective-permute-start | bytes 98312 | tf_op jit(solution)/shard_map/ppermute | solution.py:54
  42.8 4.3 %collective-permute-start.3 = (bf16[1,64,256]{2,1,0:T(8,128)(2,1)S(1)}, bf16[1,64,256]{2,1,0:T(8,128)(2,1)S(1)}, u32[]{:S(2)}, u32[]{:S(2)}) collective-permute-start(bf16[1,64,256]{2,1,0:T(8,128)(2,1)S(1)} %bitcast.42), channel_id=1, source_target_pairs={{0,4},{2,6},{4,0},{6,2},{8,12},{10,14},{12,8},{14,10},{1,5},{3,7},... | collective-permute-start | bytes 98312 | tf_op jit(solution)/shard_map/ppermute | solution.py:54
  47.2 5.4 %collective-permute-start.7 = (bf16[4,64,256]{2,1,0:T(8,128)(2,1)S(1)}, bf16[4,64,256]{2,1,0:T(8,128)(2,1)S(1)}, u32[]{:S(2)}, u32[]{:S(2)}) collective-permute-start(bf16[4,64,256]{2,1,0:T(8,128)(2,1)S(1)} %pad_maximum_fusion.3), channel_id=1, source_target_pairs={{0,8},{2,10},{4,12},{6,14},{8,0},{10,2},{12,4},{14,6},{1,9},{3,11}... | collective-permute-start | bytes 393224 | tf_op jit(solution)/shard_map/ppermute | solution.py:58
  50.0 3.8 %collective-permute-start.8 = (bf16[512,128]{1,0:T(8,128)(2,1)S(1)}, bf16[512,128]{1,0:T(8,128)(2,1)S(1)}, u32[]{:S(2)}, u32[]{:S(2)}) collective-permute-start(bf16[512,128]{1,0:T(8,128)(2,1)S(1)} %get-tuple-element.33), channel_id=1, source_target_pairs={{0,224},{1,33},{16,240},{17,49},{32,0},{33,65},{48,16},{49,81},{64... | collective-permute-start | bytes 393224 | tf_op jit(solution)/shard_map/ppermute | solution.py:42
  53.8 5.4 %collective-permute-start.9 = (bf16[1024,128]{1,0:T(8,128)(2,1)S(1)}, bf16[1024,128]{1,0:T(8,128)(2,1)S(1)}, u32[]{:S(2)}, u32[]{:S(2)}) collective-permute-start(bf16[1024,128]{1,0:T(8,128)(2,1)S(1)} %pad_maximum_fusion), channel_id=1, source_target_pairs={{0,1},{1,0},{2,3},{3,2},{4,5},{5,4},{6,7},{7,6},{8,9},{9,8},{10,11... | collective-permute-start | bytes 786440 | tf_op jit(solution)/shard_map/ppermute | solution.py:50
  55.4 12.3 %collective-permute-start.16 = (bf16[256,512]{1,0:T(8,128)(2,1)S(1)}, bf16[256,512]{1,0:T(8,128)(2,1)S(1)}, u32[]{:S(2)}, u32[]{:S(2)}) collective-permute-start(bf16[256,512]{1,0:T(8,128)(2,1)S(1)} %turned_image.1.refs_3_), channel_id=1, source_target_pairs={{0,224},{16,240},{32,0},{48,16},{64,32},{80,48},{96,64},{112,80},{... | collective-permute-start | bytes 786440 | tf_op jit(solution)/shard_map/ppermute | solution.py:34
  56.2 13.2 %collective-permute-start.12 = (bf16[256,512]{1,0:T(8,128)(2,1)S(1)}, bf16[256,512]{1,0:T(8,128)(2,1)S(1)}, u32[]{:S(2)}, u32[]{:S(2)}) collective-permute-start(bf16[256,512]{1,0:T(8,128)(2,1)S(1)} %turned_image.1.refs_3_), channel_id=1, source_target_pairs={{0,32},{16,48},{32,64},{48,80},{64,96},{80,112},{96,128},{112,144}... | collective-permute-start | bytes 786440 | tf_op jit(solution)/shard_map/ppermute | solution.py:34
  57.3 6.2 %collective-permute-start.10 = (bf16[768,128]{1,0:T(8,128)(2,1)S(1)}, bf16[768,128]{1,0:T(8,128)(2,1)S(1)}, u32[]{:S(2)}, u32[]{:S(2)}) collective-permute-start(bf16[768,128]{1,0:T(8,128)(2,1)S(1)} %pad_maximum_fusion.2), channel_id=1, source_target_pairs={{0,1},{1,0},{2,3},{3,2},{4,5},{5,4},{6,7},{7,6},{8,9},{9,8},{10,11... | collective-permute-start | bytes 589832 | tf_op jit(solution)/shard_map/ppermute | solution.py:50
  63.5 6.2 %collective-permute-start.11 = (bf16[8,16,128]{2,1,0:T(8,128)(2,1)S(1)}, bf16[8,16,128]{2,1,0:T(8,128)(2,1)S(1)}, u32[]{:S(2)}, u32[]{:S(2)}) collective-permute-start(bf16[8,16,128]{2,1,0:T(8,128)(2,1)S(1)} %constant_dynamic-update-slice_fusion), channel_id=1, source_target_pairs={{0,16},{16,0},{32,48},{48,32},{64,80},{80,64},{96,112},{112,96},{1... | collective-permute-start | bytes 98312 | tf_op jit(solution)/shard_map/ppermute | solution.py:46
  67.7 8.5 %collective-permute-start.17 = (bf16[256,512]{1,0:T(8,128)(2,1)S(1)}, bf16[256,512]{1,0:T(8,128)(2,1)S(1)}, u32[]{:S(2)}, u32[]{:S(2)}) collective-permute-start(bf16[256,512]{1,0:T(8,128)(2,1)S(1)} %collective-permute-done.16.refs_5_), channel_id=1, source_target_pairs={{0,224},{16,240},{32,0},{48,16},{64,32},{80,48},{96,64},{112,80},{... | collective-permute-start | bytes 786440 | tf_op jit(solution)/shard_map/ppermute | solution.py:34
  69.4 9.1 %collective-permute-start.13 = (bf16[256,512]{1,0:T(8,128)(2,1)S(1)}, bf16[256,512]{1,0:T(8,128)(2,1)S(1)}, u32[]{:S(2)}, u32[]{:S(2)}) collective-permute-start(bf16[256,512]{1,0:T(8,128)(2,1)S(1)} %collective-permute-done.12.refs_4_), channel_id=1, source_target_pairs={{0,32},{16,48},{32,64},{48,80},{64,96},{80,112},{96,128},{112,144}... | collective-permute-start | bytes 786440 | tf_op jit(solution)/shard_map/ppermute | solution.py:34
  76.1 7.3 %collective-permute-start.18 = (bf16[256,512]{1,0:T(8,128)(2,1)S(1)}, bf16[256,512]{1,0:T(8,128)(2,1)S(1)}, u32[]{:S(2)}, u32[]{:S(2)}) collective-permute-start(bf16[256,512]{1,0:T(8,128)(2,1)S(1)} %collective-permute-done.17.refs_5_), channel_id=1, source_target_pairs={{0,224},{16,240},{32,0},{48,16},{64,32},{80,48},{96,64},{112,80},{... | collective-permute-start | bytes 786440 | tf_op jit(solution)/shard_map/ppermute | solution.py:34
  78.5 8.3 %collective-permute-start.14 = (bf16[256,512]{1,0:T(8,128)(2,1)S(1)}, bf16[256,512]{1,0:T(8,128)(2,1)S(1)}, u32[]{:S(2)}, u32[]{:S(2)}) collective-permute-start(bf16[256,512]{1,0:T(8,128)(2,1)S(1)} %collective-permute-done.13.refs_4_), channel_id=1, source_target_pairs={{0,32},{16,48},{32,64},{48,80},{64,96},{80,112},{96,128},{112,144}... | collective-permute-start | bytes 786440 | tf_op jit(solution)/shard_map/ppermute | solution.py:34
  83.4 5.4 %collective-permute-start.19 = (bf16[128,512]{1,0:T(8,128)(2,1)S(1)}, bf16[128,512]{1,0:T(8,128)(2,1)S(1)}, u32[]{:S(2)}, u32[]{:S(2)}) collective-permute-start(bf16[128,512]{1,0:T(8,128)(2,1)S(1)} %slice.118), channel_id=1, source_target_pairs={{0,224},{16,240},{32,0},{48,16},{64,32},{80,48},{96,64},{112,80},{... | collective-permute-start | bytes 393224 | tf_op jit(solution)/shard_map/ppermute | solution.py:34
  86.8 5.1 %collective-permute-start.15 = (bf16[128,512]{1,0:T(8,128)(2,1)S(1)}, bf16[128,512]{1,0:T(8,128)(2,1)S(1)}, u32[]{:S(2)}, u32[]{:S(2)}) collective-permute-start(bf16[128,512]{1,0:T(8,128)(2,1)S(1)} %slice.117), channel_id=1, source_target_pairs={{0,32},{16,48},{32,64},{48,80},{64,96},{80,112},{96,128},{112,144}... | collective-permute-start | bytes 393224 | tf_op jit(solution)/shard_map/ppermute | solution.py:34
  93.8 4.8 %collective-permute-start.20 = (f32[4,256,128]{2,1,0:T(8,128)S(1)}, f32[4,256,128]{2,1,0:T(8,128)S(1)}, u32[]{:S(2)}, u32[]{:S(2)}) collective-permute-start(f32[4,256,128]{2,1,0:T(8,128)S(1)} %get-tuple-element.31), channel_id=1, source_target_pairs={{0,16},{16,0},{32,48},{48,32},{64,80},{80,64},{96,112},{112,96},{1... | collective-permute-start | bytes 1572872 | tf_op jit(solution)/shard_map/ppermute | solution.py:46
  97.0 2.4 %collective-permute-start.22 = (f32[4,256,128]{2,1,0:T(8,128)S(1)}, f32[4,256,128]{2,1,0:T(8,128)S(1)}, u32[]{:S(2)}, u32[]{:S(2)}) collective-permute-start(f32[4,256,128]{2,1,0:T(8,128)S(1)} %get-tuple-element.29), channel_id=1, source_target_pairs={{0,16},{16,0},{32,48},{48,32},{64,80},{80,64},{96,112},{112,96},{1... | collective-permute-start | bytes 1572872 | tf_op jit(solution)/shard_map/ppermute | solution.py:46
  98.6 7.6 %collective-permute-start.21 = (bf16[4,256,128]{2,1,0:T(8,128)(2,1)S(1)}, bf16[4,256,128]{2,1,0:T(8,128)(2,1)S(1)}, u32[]{:S(2)}, u32[]{:S(2)}) collective-permute-start(bf16[4,256,128]{2,1,0:T(8,128)(2,1)S(1)} %fusion.1), channel_id=1, source_target_pairs={{0,1},{1,0},{2,3},{3,2},{4,5},{5,4},{6,7},{7,6},{8,9},{9,8},{10,11... | collective-permute-start | bytes 786440 | tf_op jit(solution)/shard_map/ppermute | solution.py:50
